TPU v7x, 32 devices: a whole 2x2x4 slice. The times are simulated.
32 devices in a mesh: grp: 2 (over x), tile: 16 (over z, y, core).
Axes of the slice: x: 2, y: 2, z: 4, core: 2. Of those that a mesh axis runs over, the one named last changes fastest.
Arguments:
- features: bfloat16 [768, 48, 48, 128], P(('grp', 'tile')), parts along dimension 0, may hold values from -6 to 6
- edge_table: int32 [384, 4, 2], replicated, may hold values from 0 to 383, as said below
- w_enc0: bfloat16 [3, 3, 128, 128], replicated, may hold values from -0.25 to 0.25
- w_enc1: bfloat16 [3, 3, 128, 128], replicated, may hold values from -0.25 to 0.25
- w_enc2: bfloat16 [3, 3, 128, 128], replicated, may hold values from -0.25 to 0.25
- w_mid: bfloat16 [3, 3, 128, 128], replicated, may hold values from -0.25 to 0.25
- w_dec2: bfloat16 [3, 3, 256, 128], replicated, may hold values from -0.1875 to 0.1875
- w_dec1: bfloat16 [3, 3, 256, 128], replicated, may hold values from -0.1875 to 0.1875
- w_dec0: bfloat16 [3, 3, 256, 128], replicated, may hold values from -0.1875 to 0.1875
Outputs:
- decoded: bfloat16 [768, 48, 48, 128], P(('grp', 'tile')), parts along dimension 0
There are 2 independent parts, one for each index of `grp`. A program takes and returns all parts, laid end to end along the dimension named above; an argument that names none is the same for every part. Nothing has to cross between parts.
Inputs may be any that keep to these rules, and one draw needn't show every extreme that they name: `edge_table`: edges are numbered 0 for row 0, 1 for the last column, 2 for the last row, 3 for column 0 of a tile; pairs are symmetric, with the same reversal flag on both sides. The tiles are those of a cube with 8 x 8 tiles a face, numbered face by face (faces +x, -x, +y, -y, +z, -z; on the face of axis k, rows run along axis k+1 and columns along axis k+2, modulo 3) and row by row within a face; blocks of 24 consecutive tiles of that numbering are placed on the devices in an order drawn at random, and the arrays hold the tiles in device order.
All inputs are finite; a program needn't handle non-finite values.
Results may differ from a plain program's by a relative error of at most 0.0053.
Values may be sent and summed in bfloat16 or wider, within the bound.
No kernel may reach another device: no remote copies, remote signals or barrier semaphores. Data moves between devices by JAX's collectives and lax.ppermute only.
A program may use at most 128 MiB of HBM per device.

v0:
```python
import jax
import jax.numpy as jnp
import numpy as np
from jax import lax
from jax.experimental import pallas as pl
from jax.experimental.pallas import tpu as pltpu
from jax.sharding import PartitionSpec as P

FACE_TILES = 8
VMEM_LIMIT = 50 * 2**20
BF = jnp.bfloat16
F32 = jnp.float32


def cube_links(tiles_side):
    basis = np.eye(3, dtype=np.int64)
    frames = []
    for axis_id in range(3):
        for orient in (1, -1):
            frames.append(
                (orient * basis[axis_id], basis[(axis_id + 1) % 3], basis[(axis_id + 2) % 3])
            )
    per_face = tiles_side * tiles_side
    tile_total = 6 * per_face
    centres = np.zeros((tile_total, 3), np.int64)
    lookup = {}
    for face_id in range(6):
        normal, row_axis, col_axis = frames[face_id]
        for row_id in range(tiles_side):
            for col_id in range(tiles_side):
                slot_id = face_id * per_face + row_id * tiles_side + col_id
                centre = (
                    tiles_side * normal
                    + (2 * row_id + 1 - tiles_side) * row_axis
                    + (2 * col_id + 1 - tiles_side) * col_axis
                )
                centres[slot_id] = centre
                lookup[tuple((int(entry) for entry in centre))] = slot_id
    partner = np.zeros((tile_total, 4), np.int64)
    for slot_id in range(tile_total):
        normal, row_axis, col_axis = frames[slot_id // per_face]
        outward = (-row_axis, col_axis, row_axis, -col_axis)
        for edge_id in range(4):
            beyond = tuple((int(entry) for entry in centres[slot_id] + 2 * outward[edge_id]))
            if beyond in lookup:
                partner[slot_id, edge_id] = lookup[beyond]
            else:
                partner[slot_id, edge_id] = lookup[
                    tuple((int(entry) for entry in centres[slot_id] + outward[edge_id] - normal))
                ]
    return partner


def pair_capacity(tiles_side, tiles_here):
    partner = cube_links(tiles_side)
    tile_total = partner.shape[0]
    blocks = tile_total // tiles_here
    source = np.repeat(np.arange(tile_total) // tiles_here, 4)
    target = partner.reshape(-1) // tiles_here
    identity = np.eye(blocks, dtype=np.int64)
    shared = identity[source].T @ identity[target]
    shared = shared * (1 - identity)
    return max(int(shared.max()), 1)


def own_strips(edge_table, position, tiles_here):
    rows = lax.dynamic_slice_in_dim(edge_table, position * tiles_here, tiles_here, 0)
    rows = rows.reshape(tiles_here * 4, 2)
    return rows[:, 0], rows[:, 1] // 2, rows[:, 1] % 2


def send_slots(edge_table, position, tiles_here, slot_count):
    partner, _, _ = own_strips(edge_table, position, tiles_here)
    target = partner // tiles_here
    order = jnp.arange(tiles_here * 4, dtype=jnp.int32)
    earlier = (order[None, :] < order[:, None]) & (target[None, :] == target[:, None])
    slot_rank = jnp.sum(earlier.astype(jnp.int32), axis=1)
    return jnp.where(target != position, target * slot_count + slot_rank, -1)


def listed(mask):
    order = jnp.arange(mask.shape[0], dtype=jnp.int32)
    rank = jnp.sum((mask[None, :] & (order[None, :] < order[:, None])).astype(jnp.int32), axis=1)
    hit = mask[None, :] & (rank[None, :] == order[:, None])
    found = jnp.sum(jnp.where(hit, order[None, :], 0), axis=1)
    return jnp.concatenate([found, jnp.sum(mask.astype(jnp.int32), keepdims=True)])


def receive_plan(edge_table, slot_row, position, tiles_here, slot_count, devices):
    strip_count = tiles_here * 4
    partner, matching, reversed_rows = own_strips(edge_table, position, tiles_here)
    target = partner // tiles_here
    order = jnp.arange(strip_count, dtype=jnp.int32)
    remote = target != position
    source_tiles = target[:, None] * tiles_here + jnp.arange(tiles_here, dtype=jnp.int32)[None, :]
    their_partners = jnp.take(edge_table[:, :, 0], source_tiles, axis=0).reshape(
        strip_count, strip_count
    )
    toward_me = their_partners // tiles_here == position
    wanted = partner % tiles_here * 4 + matching
    before_wanted = order[None, :] < wanted[:, None]
    recv_rank = jnp.sum((toward_me & before_wanted).astype(jnp.int32), axis=1)
    pick_row = jnp.where(remote, target * slot_count + recv_rank, devices * slot_count + wanted)
    odd = (matching != (order + 2) % 4) | (reversed_rows == 1)
    return (pick_row, reversed_rows, slot_row, matching, listed(remote), listed(odd))


def up16(n):
    return (n + 15) // 16 * 16


def strip_rows(n):
    return {6: 8, 12: 16}.get(n, n)


def params():
    return pltpu.CompilerParams(vmem_limit_bytes=VMEM_LIMIT)


def rims_kernel(slot_ref, lo_ref, hi_ref, top_ref, bottom_ref, out_ref, send_ref, colbuf):
    group, n = lo_ref.shape[0], lo_ref.shape[1]
    first = pl.program_id(0) * group * 4
    for g in range(group):
        colbuf[...] = lo_ref[g, :, 0:8, :].astype(F32).reshape(n * 8, 128)
        left = colbuf[pl.ds(0, n, 8), :]
        colbuf[...] = hi_ref[g, :, 8:16, :].astype(F32).reshape(n * 8, 128)
        right = colbuf[pl.ds(7, n, 8), :]
        out_ref[g, 0] = top_ref[g, 0]
        out_ref[g, 1] = right.astype(BF)
        out_ref[g, 2] = bottom_ref[g, 0]
        out_ref[g, 3] = left.astype(BF)
    for g in range(group):
        for e in range(4):
            slot = slot_ref[first + g * 4 + e]

            @pl.when(slot >= 0)
            def _():
                send_ref[slot] = out_ref[g, e]


def tile_rims(x, slot_row, rows):
    tiles, n, _, c = x.shape
    g = group_of(tiles, 4)
    last = n // 16 - 1
    return pl.pallas_call(
        rims_kernel,
        grid=(tiles // g,),
        in_specs=[
            pl.BlockSpec(memory_space=pltpu.SMEM),
            pl.BlockSpec((g, n, 16, c), lambda i: (i, 0, 0, 0)),
            pl.BlockSpec((g, n, 16, c), lambda i: (i, 0, last, 0)),
            pl.BlockSpec((g, 1, n, c), lambda i: (i, 0, 0, 0)),
            pl.BlockSpec((g, 1, n, c), lambda i: (i, n - 1, 0, 0)),
        ],
        out_specs=[tile_spec(g, 4, n, c), whole_spec((rows, n, c))],
        out_shape=[
            jax.ShapeDtypeStruct((tiles, 4, n, c), BF),
            jax.ShapeDtypeStruct((rows, n, c), BF),
        ],
        scratch_shapes=[pltpu.VMEM((n * 8, 128), F32)],
        compiler_params=params(),
        name="tile_rims",
    )(slot_row, x, x, x, x)


def silu(s):
    return s / (1.0 + jnp.exp(-s))


def strip_shifts(h, n):
    rows = h.shape[0]
    row = lax.broadcasted_iota(jnp.int32, h.shape, 0)
    half = h * 0.5
    down = jnp.where(row == 0, half, pltpu.roll(h, 1, 0))
    up = jnp.where(row == n - 1, half, pltpu.roll(h, rows - 1, 0))
    return down, up


def flip_matrix(rows, n):
    ri = lax.broadcasted_iota(jnp.int32, (rows, rows), 0)
    ci = lax.broadcasted_iota(jnp.int32, (rows, rows), 1)
    return (ri + ci == n - 1).astype(F32).astype(BF)


def put_shifts(ref, index, lane, h, n):
    down, up = strip_shifts(h, n)
    for s, part in enumerate((down, h, up)):
        ref[index + (slice(None), slice(lane + s * 128, lane + s * 128 + 128))] = part.astype(ref.dtype)


def each_tile(tiles, body):
    side = group_of(tiles, 3)

    def step(i, carry):
        for k in range(side):
            body(i * side + k, k)
        return carry

    lax.fori_loop(0, tiles // side, step, 0)


def each_listed(list_ref, body):
    def step(j, carry):
        body(list_ref[j])
        return carry

    lax.fori_loop(0, list_ref[list_ref.shape[0] - 1], step, 0)


def incoming(pick_ref, recv_ref, own_ref, i):
    rows = recv_ref.shape[0]
    pick = pick_ref[i]
    a = recv_ref[jnp.minimum(pick, rows - 1)].astype(F32)
    b = own_ref[jnp.maximum(pick - rows, 0)].astype(F32)
    return jnp.where(pick < rows, a, b)


def edge_taps(w_ref, e, lo):
    taps = ((0, 1, 2), (2, 5, 8), (6, 7, 8), (0, 3, 6))[e]
    return jnp.concatenate([w_ref[tap, lo : lo + 128, :] for tap in taps], axis=0)


def contributions(n, tiles, strip_of, w_ref, lo, rev_ref, edge_ref, odd_ref, lhs_ref, con_ref, taps_ref, buf):
    lp = lhs_ref.shape[2]
    for e in range(4):
        taps_ref[e] = edge_taps(w_ref, e, lo)

    def fill(t, k):
        for f in range(4):
            put_shifts(lhs_ref, (f, t), 0, strip_of(f, t, k), n)

    each_tile(tiles, fill)
    for f in range(4):
        lhs = lhs_ref[f].reshape(tiles * lp, 384).astype(BF)
        out = jnp.dot(lhs, taps_ref[(f + 2) % 4], preferred_element_type=F32)
        con_ref[f] = out.reshape(tiles, lp, 128)
    flip = flip_matrix(lp, n)

    def odd_one(i):
        f, t = i % 4, i // 4
        buf[...] = lhs_ref[f, t, :, 128:256].astype(F32)

        @pl.when(rev_ref[i] == 1)
        def _():
            buf[...] = jnp.dot(flip, buf[...].astype(BF), preferred_element_type=F32)

        put_shifts(lhs_ref, (f, t), 0, buf[...], n)
        con_ref[f, t] = jnp.dot(lhs_ref[f, t].astype(BF), taps_ref[edge_ref[i]], preferred_element_type=F32)

    each_listed(odd_ref, odd_one)


def skip_kernel(n, rev_ref, edge_ref, odd_ref, rim_ref, w_ref, out_ref, lhs_ref, con_ref, taps_ref, buf):
    tiles = rim_ref.shape[0] // 4
    contributions(
        n, tiles, lambda f, t, k: rim_ref[t * 4 + f].astype(F32), w_ref, 128,
        rev_ref, edge_ref, odd_ref, lhs_ref, con_ref, taps_ref, buf,
    )

    def put(t, k):
        for f in range(4):
            out_ref[t * 4 + f] = con_ref[f, t]

    each_tile(tiles, put)


def wide(rows):
    return BF if rows % 16 == 0 else F32


def skip_step(n, plan, rim, w):
    strips, lp, c = rim.shape
    smem = pl.BlockSpec(memory_space=pltpu.SMEM)
    vmem = pl.BlockSpec(memory_space=pltpu.VMEM)
    return pl.pallas_call(
        lambda *refs: skip_kernel(n, *refs),
        in_specs=[smem, smem, smem, vmem, vmem],
        out_specs=vmem,
        out_shape=jax.ShapeDtypeStruct((strips, lp, c), F32),
        scratch_shapes=[
            pltpu.VMEM((4, strips // 4, lp, 384), wide(lp)),
            pltpu.VMEM((4, strips // 4, lp, 128), F32),
            pltpu.VMEM((4, 384, 128), BF),
            pltpu.VMEM((lp, 128), F32),
        ],
        compiler_params=params(),
        cost_estimate=pl.CostEstimate(flops=strips * lp * 2 * 384 * 256, bytes_accessed=strips * lp * 768, transcendentals=0),
        name="skip_step",
    )(plan[1], plan[3], plan[5], rim, w.reshape(9, -1, c))


def corners(end):
    return (
        (0, 0, 3, 0), (0, end, 1, 0), (2, 0, 3, end), (2, end, 1, end),
        (3, 0, 0, 0), (3, end, 2, 0), (1, 0, 0, end), (1, end, 2, end),
    )


def rim_kernel(n, strips_in, nxt, refs):
    it = iter(refs)
    pick_ref, rev_ref, slot_ref, edge_ref, remote_ref, odd_ref = [next(it) for _ in range(6)]
    recv_ref, own_ref, sum_ref = next(it), next(it), next(it)
    w_ref = next(it) if strips_in else None
    ring_ref = next(it) if nxt == "shrink" else None
    skip_ref, wn_ref = (next(it), next(it)) if nxt == "halo" else (None, None)
    rim_ref, next_ref, send_ref = next(it), next(it), next(it)
    halo_ref, lhs_ref, con_ref = next(it), next(it), next(it)
    edge_buf, ring_buf, sum_buf, out_buf = next(it), next(it), next(it), next(it)
    lhsn_ref, conn_ref, taps_ref, big_buf = [next(it) for _ in range(4)] if nxt == "halo" else [None] * 4

    lp = recv_ref.shape[1]
    strips = own_ref.shape[0]
    tiles = strips // 4
    flip = flip_matrix(lp, n)

    if strips_in:

        def fetch(t, k):
            for e in range(4):
                i = t * 4 + e
                halo_ref[i] = incoming(pick_ref, recv_ref, own_ref, i).astype(BF)

        each_tile(tiles, fetch)

        def turn(i):
            @pl.when(rev_ref[i] == 1)
            def _():
                halo_ref[i] = jnp.dot(flip, halo_ref[i], preferred_element_type=F32).astype(BF)

        each_listed(odd_ref, turn)

        def fill(t, k):
            for e in range(4):
                put_shifts(lhs_ref, (e, t), 0, halo_ref[t * 4 + e].astype(F32), n)

        each_tile(tiles, fill)
        for e in range(4):
            lhs = lhs_ref[e].reshape(tiles * lp, 384).astype(BF)
            out = jnp.dot(lhs, edge_taps(w_ref, e, 0), preferred_element_type=F32)
            con_ref[e] = out.reshape(tiles, lp, 128)
    else:

        def fill(t, k):
            for e in range(4):
                con_ref[e, t] = incoming(pick_ref, recv_ref, own_ref, t * 4 + e)

        each_tile(tiles, fill)

    end = n - 1
    joints = (
        (0, 0, 3, 1), (0, end, 1, 1), (2, 0, 3, end - 1), (2, end, 1, end - 1),
        (3, 0, 0, 1), (3, end, 2, 1), (1, 0, 0, end - 1), (1, end, 2, end - 1),
    )
    if nxt == "shrink":
        out_buf[...] = jnp.zeros_like(out_buf)

    def finish(t, k):
        for e in range(4):
            edge_buf[k, e] = sum_ref[t * 4 + e] + con_ref[e, t]
        for e, cell, other, at in corners(end):
            cells = slice(cell, cell + 1)
            edge_buf[k, e, cells] = edge_buf[k, e, cells] + con_ref[other, t, at : at + 1]
        for e in range(4):
            y = silu(edge_buf[k, e]).astype(BF)
            rim_ref[t * 4 + e] = y
            edge_buf[k, e] = y.astype(F32)
        if nxt == "shrink":
            for e in range(4):
                ring_buf[k, e] = ring_ref[t * 4 + e].astype(F32)
            for e, cell, other, at in joints:
                ring_buf[k, e, cell : cell + 1] = edge_buf[k, other, at : at + 1]
            for e in range(4):
                sum_buf[k, e] = edge_buf[k, e] + ring_buf[k, e]
                small = sum_buf[k, e, pl.ds(0, lp // 2, 2), :] + sum_buf[k, e, pl.ds(1, lp // 2, 2), :]
                out_buf[k, e, 0 : lp // 2] = small * 0.25
                next_ref[t * 4 + e] = out_buf[k, e].astype(BF)

    each_tile(tiles, finish)

    if nxt == "halo":
        half = big_buf.shape[2] // 2

        def enlarged(f, t, k):
            rim = rim_ref[t * 4 + f].astype(F32)[0:half]
            big_buf[k, f, pl.ds(0, half, 2), :] = rim
            big_buf[k, f, pl.ds(1, half, 2), :] = rim
            return big_buf[k, f]

        contributions(
            2 * n, tiles, enlarged, wn_ref, 0,
            rev_ref, edge_ref, odd_ref, lhsn_ref, conn_ref, taps_ref, big_buf.at[0, 0],
        )

        def put(t, k):
            for f in range(4):
                next_ref[t * 4 + f] = (conn_ref[f, t] + skip_ref[t * 4 + f]).astype(BF)

        each_tile(tiles, put)

    def send(i):
        send_ref[slot_ref[i]] = next_ref[i]

    each_listed(remote_ref, send)


def rim_step(n, plan, recv, own, sums, w=None, ring=None, skip=None, wn=None):
    rows, lp, c = recv.shape
    strips = own.shape[0]
    tiles = strips // 4
    side = group_of(tiles, 3)
    nxt = "shrink" if ring is not None else "halo"
    smem = pl.BlockSpec(memory_space=pltpu.SMEM)
    vmem = pl.BlockSpec(memory_space=pltpu.VMEM)
    w = w if w is None else w.reshape(9, -1, c)
    wn = wn if wn is None else wn.reshape(9, -1, c)
    args = [recv, own, sums] + [a for a in (w, ring, skip, wn) if a is not None]
    lo = strip_rows(n // 2) if nxt == "shrink" else strip_rows(2 * n)
    outs = [
        jax.ShapeDtypeStruct((strips, lp, c), BF),
        jax.ShapeDtypeStruct((strips, lo, c), BF),
        jax.ShapeDtypeStruct((rows, lo, c), BF),
    ]
    scratch = [
        pltpu.VMEM((strips, lp, 128), BF),
        pltpu.VMEM((4, tiles, lp, 384), wide(lp)),
        pltpu.VMEM((4, tiles, lp, 128), F32),
        pltpu.VMEM((side, 4, lp, 128), F32),
        pltpu.VMEM((side, 4, lp, 128), F32),
        pltpu.VMEM((side, 4, lp, 128), F32),
        pltpu.VMEM((side, 4, lo, 128), F32),
    ]
    if nxt == "halo":
        scratch += [
            pltpu.VMEM((4, tiles, lo, 384), wide(lo)),
            pltpu.VMEM((4, tiles, lo, 128), F32),
            pltpu.VMEM((4, 384, 128), BF),
            pltpu.VMEM((side, 4, lo, 128), F32),
        ]

    def kernel(*refs):
        rim_kernel(n, w is not None, nxt, refs)

    return pl.pallas_call(
        kernel,
        in_specs=[smem] * 6 + [vmem] * len(args),
        out_specs=[vmem] * len(outs),
        out_shape=outs,
        scratch_shapes=scratch,
        compiler_params=params(),
        cost_estimate=pl.CostEstimate(flops=strips * lp * 2 * 384 * 512, bytes_accessed=strips * lp * 1500, transcendentals=0),
        name="rim_step",
    )(*plan, *args)


def spread_columns(strip, n, sublane, buf):
    buf[pl.ds(sublane, n, 8), :] = strip
    return buf[...].reshape(n, 8, 128)


def with_rims(x, rim, n, buf):
    sub = lax.broadcasted_iota(jnp.int32, (n, 8, 128), 1)
    head = jnp.where(sub == 0, spread_columns(rim[3], n, 0, buf), x[:, 0:8])
    tail = jnp.where(sub == 7, spread_columns(rim[1], n, 7, buf), x[:, n - 8 : n])
    x = jnp.concatenate([head, x[:, 8 : n - 8], tail], axis=1)
    return jnp.concatenate([rim[0][None], x[1 : n - 1], rim[2][None]], axis=0)


def column_shifts(x, n):
    col = lax.broadcasted_iota(jnp.int32, x.shape, 1)
    down = jnp.where(col == 0, 0.0, pltpu.roll(x, 1, 1))
    up = jnp.where(col == n - 1, 0.0, pltpu.roll(x, n - 1, 1))
    return down, x, up


def fill_pairs(y_ref, x, n):
    half, n_p = n // 2, y_ref.shape[1]
    zero = jnp.zeros((n_p, 384), BF)
    y_ref[0, :, 0:384] = zero
    y_ref[half, :, 384:768] = zero
    for s, body in enumerate(column_shifts(x, n)):
        b = body.astype(BF).reshape(half, 2, n, 128)
        y_ref[0:half, 0:n, 384 + s * 128 : 384 + s * 128 + 128] = b[:, 0]
        y_ref[1 : half + 1, 0:n, s * 128 : s * 128 + 128] = b[:, 1]


def fill_rows(u_ref, x, n):
    zero = jnp.zeros((u_ref.shape[1], 384), BF)
    u_ref[0] = zero
    u_ref[n + 1] = zero
    for s, body in enumerate(column_shifts(x, n)):
        u_ref[1 : n + 1, 0:n, s * 128 : s * 128 + 128] = body.astype(BF)


def pair_sums(y_ref, w_ref, q0, m, extra):
    n_p = y_ref.shape[1]
    a = y_ref[q0 : q0 + m].reshape(m * n_p, 768)
    b = y_ref[q0 + 1 : q0 + 1 + m].reshape(m * n_p, 768)
    acc = jnp.dot(a, w_ref[0:768, :], preferred_element_type=F32)
    acc = acc + jnp.dot(b, w_ref[768:1536, :], preferred_element_type=F32)
    acc = acc.reshape(m, n_p, 256)
    return acc if extra is None else acc + extra


def pair_chunks(n):
    half = n // 2
    m = 6 if half % 6 == 0 else half
    return [(q, m) for q in range(0, half, m)]


def column_of(acc, m, lo, sublane, colbuf):
    rows = jnp.stack([acc[:, lo : lo + 8, 0:128], acc[:, lo : lo + 8, 128:256]], axis=1)
    colbuf[0 : 16 * m] = rows.reshape(16 * m, 128)
    return colbuf[pl.ds(sublane, 2 * m, 8), :]


def put_sums(acc, sums_ref, g, q0, m, n, colbuf):
    cells = slice(2 * q0, 2 * q0 + 2 * m)
    if q0 == 0:
        sums_ref[g, 0] = acc[0, 0:n, 0:128]
    if q0 + m == n // 2:
        sums_ref[g, 2] = acc[m - 1, 0:n, 128:256]
    sums_ref[g, 3, cells] = column_of(acc, m, 0, 0, colbuf)
    sums_ref[g, 1, cells] = column_of(acc, m, n - 8, 7, colbuf)


def fill_pair_weights(raw_ref, lo, w_ref):
    for p in range(4):
        for col in range(3):
            at = slice((p * 3 + col) * 128, (p * 3 + col) * 128 + 128)
            for out in range(2):
                row = p - out
                tap = raw_ref[row * 3 + col, lo : lo + 128, :] if 0 <= row <= 2 else jnp.zeros((128, 128), BF)
                w_ref[at, out * 128 : out * 128 + 128] = tap


def fill_coarse_weights(raw_ref, w_ref):
    along = (((0,), (1, 2), ()), ((), (0, 1), (2,)))
    for b in range(2):
        for k in range(3):
            for slot in range(2):
                cols = along[b][slot + b]
                for out in range(2):
                    taps = [raw_ref[r * 3 + col, 0:128, :].astype(F32) for r in along[out][k] for col in cols]
                    total = sum(taps[1:], taps[0]) if taps else jnp.zeros((128, 128), F32)
                    w_ref[b, k, slot * 128 : slot * 128 + 128, out * 128 : out * 128 + 128] = total.astype(BF)


def enc_kernel(*refs):
    it = iter(refs[:-5])
    x_ref, raw_ref = next(it), next(it)
    rest = list(it)
    rim_ref = rest.pop(0) if len(rest) == 5 else None
    y_ref, sums_ref, ring_ref, s_ref = rest
    pairs, colbuf, sumbuf, ringbuf, w_ref = refs[-5:]

    @pl.when(pl.program_id(0) == 0)
    def _():
        fill_pair_weights(raw_ref, 0, w_ref)

    group, n = x_ref.shape[0], x_ref.shape[1]
    half = n // 2

    for g in range(group):
        x = x_ref[g].astype(F32)
        if rim_ref is not None:
            x = with_rims(x, [rim_ref[g, e].astype(F32) for e in range(4)], n, colbuf)
        fill_pairs(pairs, x, n)
        for q0, m in pair_chunks(n):
            acc = pair_sums(pairs, w_ref, q0, m, None)
            put_sums(acc, sums_ref, g, q0, m, n, colbuf)
            out = silu(acc).astype(BF)[:, 0:n]
            y_ref[g, q0 : q0 + m, 0] = out[:, :, 0:128]
            y_ref[g, q0 : q0 + m, 1] = out[:, :, 128:256]
            wide = out.astype(F32)
            if q0 == 0:
                ring_ref[g, 0] = out[0, :, 128:256]
            if q0 + m == half:
                ring_ref[g, 2] = out[m - 1, :, 0:128]
            ringbuf[1, 2 * q0 : 2 * q0 + 2 * m] = column_of(wide, m, n - 8, 6, colbuf)
            ringbuf[0, 2 * q0 : 2 * q0 + 2 * m] = column_of(wide, m, 0, 1, colbuf)
            both = wide[:, :, 0:128] + wide[:, :, 128:256]
            sumbuf[...] = both.reshape(m * n, 128)
            small = sumbuf[pl.ds(0, m * half, 2), :] + sumbuf[pl.ds(1, m * half, 2), :]
            s_ref[g, q0 : q0 + m] = (small * 0.25).reshape(m, half, 128).astype(BF)
        ring_ref[g, 1] = ringbuf[1].astype(BF)
        ring_ref[g, 3] = ringbuf[0].astype(BF)


def dec_kernel(x_ref, rim_ref, u_ref, *refs):
    refs = list(refs)
    urim_ref = refs.pop(0) if len(refs) == 10 else None
    raw_ref, y_ref, sums_ref, pairs, rows, colbuf, acc_ref, w_ref, wu_ref = refs

    @pl.when(pl.program_id(0) == 0)
    def _():
        fill_pair_weights(raw_ref, 128, w_ref)
        fill_coarse_weights(raw_ref, wu_ref)

    group, n = x_ref.shape[0], x_ref.shape[1]
    half = n // 2
    hp = rows.shape[1]

    for g in range(group):
        u = u_ref[g].astype(F32)
        if urim_ref is not None:
            u = with_rims(u, [urim_ref[g, e].astype(F32) for e in range(4)], half, colbuf.at[0 : half * 8])
        fill_rows(rows, u, half)
        x = with_rims(x_ref[g].astype(F32), [rim_ref[g, e].astype(F32) for e in range(4)], n, colbuf)
        fill_pairs(pairs, x, n)
        for q0, m in pair_chunks(n):
            for b in range(2):
                acc = None
                for k in range(3):
                    lhs = rows[q0 + k : q0 + k + m, :, b * 128 : b * 128 + 256].reshape(m * hp, 256)
                    part = jnp.dot(lhs, wu_ref[b, k], preferred_element_type=F32)
                    acc = part if acc is None else acc + part
                acc = acc.reshape(m, hp, 256)
                for i in range(m):
                    for p in range(2):
                        acc_ref[p, i, pl.ds(b, half, 2), :] = acc[i, 0:half, p * 128 : p * 128 + 128]
            extra = jnp.concatenate([acc_ref[0], acc_ref[1]], axis=2)
            acc = pair_sums(pairs, w_ref, q0, m, extra)
            put_sums(acc, sums_ref, g, q0, m, n, colbuf)
            out = silu(acc).astype(BF)[:, 0:n]
            y_ref[g, q0 : q0 + m, 0] = out[:, :, 0:128]
            y_ref[g, q0 : q0 + m, 1] = out[:, :, 128:256]


def last_kernel(pick_ref, recv_ref, own_ref, sum_ref, x_ref, y_ref, *scratch):
    rim_ref, edge_buf, slab_ref, colbuf, in_sem, out_sem, row_sem = scratch
    del x_ref
    strips, n = own_ref.shape[0], own_ref.shape[1]
    tiles = strips // 4
    parts = in_sem.shape[1]
    span = tiles // parts

    def slab(side, part):
        return y_ref.at[pl.ds(part * span, span), :, pl.ds(side * (n - 16), 16), :]

    def held(side, part):
        return slab_ref.at[side, pl.ds(part * span, span)]

    reads = [
        [pltpu.make_async_copy(slab(side, p), held(side, p), in_sem.at[side, p]) for p in range(parts)]
        for side in range(2)
    ]
    for p in range(parts):
        for side in range(2):
            reads[side][p].start()

    end = n - 1

    def finish(t, k):
        con = [incoming(pick_ref, recv_ref, own_ref, t * 4 + e) for e in range(4)]
        for e in range(4):
            edge_buf[k, e] = sum_ref[t * 4 + e] + con[e]
        for e, cell, other, at in corners(end):
            cells = slice(cell, cell + 1)
            edge_buf[k, e, cells] = edge_buf[k, e, cells] + con[other][at : at + 1]
        for e in range(4):
            rim_ref[t, e] = silu(edge_buf[k, e]).astype(BF)

    each_tile(tiles, finish)

    rows = [
        pltpu.make_async_copy(
            rim_ref.at[:, e, pl.ds(16, n - 32), :], y_ref.at[:, row, pl.ds(16, n - 32), :], row_sem.at[j]
        )
        for j, (e, row) in enumerate(((0, 0), (2, n - 1)))
    ]
    for copy in rows:
        copy.start()

    sub = lax.broadcasted_iota(jnp.int32, (n, 8, 128), 1)

    def patch(side, t):
        lo = 0 if side == 0 else n - 16
        near = slice(0, 8) if side == 0 else slice(8, 16)
        far = slice(8, 16) if side == 0 else slice(0, 8)
        x = slab_ref[side, t].astype(F32)
        cells = spread_columns(rim_ref[t, 3 if side == 0 else 1].astype(F32), n, 0 if side == 0 else 7, colbuf)
        new = jnp.where(sub == (0 if side == 0 else 7), cells, x[:, near])
        both = [new, x[:, far]] if side == 0 else [x[:, far], new]
        slab_ref[side, t] = jnp.concatenate(both, axis=1).astype(BF)
        slab_ref[side, t, 0] = rim_ref[t, 0, lo : lo + 16]
        slab_ref[side, t, n - 1] = rim_ref[t, 2, lo : lo + 16]

    writes = []
    for p in range(parts):
        for side in range(2):
            reads[side][p].wait()

            def step(t, carry, side=side):
                patch(side, t)
                return carry

            lax.fori_loop(p * span, p * span + span, step, 0)
            copy = pltpu.make_async_copy(held(side, p), slab(side, p), out_sem.at[side, p])
            copy.start()
            writes.append(copy)
    for copy in writes + rows:
        copy.wait()


def last_step(x, plan, recv, own, sums):
    tiles, n, _, c = x.shape
    strips = own.shape[0]
    parts = 4 if tiles % 4 == 0 else 1
    smem = pl.BlockSpec(memory_space=pltpu.SMEM)
    vmem = pl.BlockSpec(memory_space=pltpu.VMEM)
    anywhere = pl.BlockSpec(memory_space=pl.ANY)
    return pl.pallas_call(
        last_kernel,
        in_specs=[smem, vmem, vmem, vmem, anywhere],
        out_specs=anywhere,
        out_shape=jax.ShapeDtypeStruct(x.shape, BF),
        scratch_shapes=[
            pltpu.VMEM((tiles, 4, n, c), BF),
            pltpu.VMEM((group_of(tiles, 3), 4, n, c), F32),
            pltpu.VMEM((2, tiles, n, 16, c), BF),
            pltpu.VMEM((n * 8, c), F32),
            pltpu.SemaphoreType.DMA((2, parts)),
            pltpu.SemaphoreType.DMA((2, parts)),
            pltpu.SemaphoreType.DMA((2,)),
        ],
        input_output_aliases={4: 0},
        compiler_params=params(),
        name="last_step",
    )(plan[0], recv, own, sums, x)


def group_of(tiles, want):
    return max(g for g in range(1, want + 1) if tiles % g == 0)


def tile_spec(group, *dims):
    return pl.BlockSpec((group,) + dims, lambda i: (i,) + (0,) * len(dims))


def whole_spec(shape):
    return pl.BlockSpec(shape, lambda i: (0,) * len(shape))


def enc_conv(x, rim, w, want):
    tiles, n, _, c = x.shape
    half, n_p = n // 2, up16(n)
    g = group_of(tiles, want)
    m = pair_chunks(n)[0][1]
    args, specs = [x, w.reshape(9, c, c)], [tile_spec(g, n, n, c), whole_spec((9, c, c))]
    if rim is not None:
        args.append(rim.reshape(tiles, 4, n, c))
        specs.append(tile_spec(g, 4, n, c))
    y, sums, ring, s = pl.pallas_call(
        enc_kernel,
        grid=(tiles // g,),
        in_specs=specs,
        out_specs=[
            tile_spec(g, half, 2, n, c), tile_spec(g, 4, n, c), tile_spec(g, 4, n, c), tile_spec(g, half, half, c)
        ],
        out_shape=[
            jax.ShapeDtypeStruct((tiles, half, 2, n, c), BF),
            jax.ShapeDtypeStruct((tiles, 4, n, c), F32),
            jax.ShapeDtypeStruct((tiles, 4, n, c), BF),
            jax.ShapeDtypeStruct((tiles, half, half, c), BF),
        ],
        scratch_shapes=[
            pltpu.VMEM((half + 1, n_p, 768), BF),
            pltpu.VMEM((n * 8, 128), F32),
            pltpu.VMEM((m * n, 128), F32),
            pltpu.VMEM((2, n, 128), F32),
            pltpu.VMEM((1536, 256), BF),
        ],
        compiler_params=params(),
        cost_estimate=pl.CostEstimate(
            flops=tiles * n * n * 2 * 1536 * 128, bytes_accessed=tiles * n * n * 600, transcendentals=tiles * n * n * 128
        ),
        name="enc_conv",
    )(*args)
    strips = lambda a: a.reshape(tiles * 4, n, c)
    return y.reshape(tiles, n, n, c), strips(sums), strips(ring), s


def dec_conv(x, rim, u, urim, w, want):
    tiles, n, _, c = x.shape
    half, n_p, h_p = n // 2, up16(n), up16(n // 2)
    g = group_of(tiles, want)
    m = pair_chunks(n)[0][1]
    args = [x, rim.reshape(tiles, 4, n, c), u]
    specs = [tile_spec(g, n, n, c), tile_spec(g, 4, n, c), tile_spec(g, half, half, c)]
    if urim is not None:
        args.append(urim.reshape(tiles, 4, half, c))
        specs.append(tile_spec(g, 4, half, c))
    y, sums = pl.pallas_call(
        dec_kernel,
        grid=(tiles // g,),
        in_specs=specs + [whole_spec((9, 2 * c, c))],
        out_specs=[tile_spec(g, half, 2, n, c), tile_spec(g, 4, n, c)],
        out_shape=[
            jax.ShapeDtypeStruct((tiles, half, 2, n, c), BF),
            jax.ShapeDtypeStruct((tiles, 4, n, c), F32),
        ],
        scratch_shapes=[
            pltpu.VMEM((half + 1, n_p, 768), BF),
            pltpu.VMEM((half + 2, h_p, 384), BF),
            pltpu.VMEM((n * 8, 128), F32),
            pltpu.VMEM((2, m, n_p, 128), F32),
            pltpu.VMEM((1536, 256), BF),
            pltpu.VMEM((2, 3, 256, 256), BF),
        ],
        compiler_params=params(),
        cost_estimate=pl.CostEstimate(
            flops=tiles * n * n * 2 * 2300 * 128, bytes_accessed=tiles * n * n * 600, transcendentals=tiles * n * n * 128
        ),
        name="dec_conv",
    )(*args, w.reshape(9, 2 * c, c))
    return y.reshape(tiles, n, n, c), sums.reshape(tiles * 4, n, c)


def strips_of(field, ring=0):
    n = field.shape[1]
    far = n - 1 - ring
    out = jnp.stack([field[:, ring], field[:, :, far], field[:, far], field[:, :, ring]], axis=1)
    out = jnp.pad(out, ((0, 0), (0, 0), (0, strip_rows(n) - n), (0, 0)))
    return out.reshape(field.shape[0] * 4, strip_rows(n), field.shape[3])


def patched(field, rim):
    tiles, n, _, c = field.shape
    rim = rim.reshape(tiles, 4, -1, c)[:, :, :n]
    middle = jnp.concatenate(
        [rim[:, 3, 1 : n - 1, None], field[:, 1 : n - 1, 1 : n - 1], rim[:, 1, 1 : n - 1, None]], axis=2
    )
    return jnp.concatenate([rim[:, 0][:, None], middle, rim[:, 2][:, None]], axis=1)


def inner_sums(field, weight):
    return lax.conv_general_dilated(
        field,
        weight,
        (1, 1),
        ((1, 1), (1, 1)),
        dimension_numbers=("NHWC", "HWIO", "NHWC"),
        preferred_element_type=F32,
    )


def shrink(field):
    count, length, _, channels = field.shape
    blocks = field.astype(F32).reshape(count, length // 2, 2, length // 2, 2, channels)
    return (jnp.sum(blocks, axis=(2, 4)) * 0.25).astype(BF)


def enlarge(field):
    return jnp.repeat(jnp.repeat(field, 2, axis=1), 2, axis=2)


def per_device(features, edge_table, w_enc0, w_enc1, w_enc2, w_mid, w_dec2, w_dec1, w_dec0):
    tiles, n0 = features.shape[0], features.shape[1]
    devices = lax.axis_size("tile")
    position = lax.axis_index("tile")
    cap = pair_capacity(FACE_TILES, tiles)
    rows = devices * cap
    slot_row = send_slots(edge_table, position, tiles, cap)

    def trade(strips):
        length = strips.shape[1]
        out = lax.all_to_all(
            strips.reshape(devices, cap * length, 128), "tile", split_axis=0, concat_axis=0, tiled=True
        )
        return out.reshape(rows, length, 128)

    def after(value, token):
        return lax.optimization_barrier((value, token))[0]

    rim0, send = tile_rims(features, slot_row, rows)
    rim0 = rim0.reshape(tiles * 4, n0, 128)
    plan = receive_plan(after(edge_table, send), slot_row, position, tiles, cap, devices)
    recv = trade(send)
    enc0, sums, ring, x1 = enc_conv(features, None, w_enc0, 1)
    enc0_rim, x1_rim, send = rim_step(n0, plan, recv, rim0, sums, w=w_enc0, ring=ring)

    recv = trade(send)
    enc1, sums, ring, x2 = enc_conv(x1, x1_rim, w_enc1, 4)
    enc1_rim, x2_rim, send = rim_step(n0 // 2, plan, recv, x1_rim, sums, w=w_enc1, ring=ring)

    recv = trade(send)
    sums = inner_sums(patched(x2, x2_rim), w_enc2)
    enc2 = jax.nn.silu(sums).astype(BF)
    enc2_rim, x3_rim, send = rim_step(
        n0 // 4, plan, recv, x2_rim, strips_of(sums), w=w_enc2, ring=strips_of(enc2, 1)
    )

    recv = trade(send)
    sums = inner_sums(patched(shrink(enc2), x3_rim), w_mid)
    middle = jax.nn.silu(sums).astype(BF)
    skip2 = skip_step(n0 // 4, plan, enc2_rim, w_dec2)
    skip0 = skip_step(n0, plan, after(enc0_rim, x3_rim), w_dec0)
    mid_rim, own, send = rim_step(
        n0 // 8, plan, recv, x3_rim, strips_of(sums), w=w_mid,
        skip=skip2, wn=w_dec2,
    )

    recv = trade(send)
    joined = jnp.concatenate([enlarge(patched(middle, mid_rim)), patched(enc2, enc2_rim)], axis=3)
    sums = inner_sums(joined, w_dec2)
    dec2 = jax.nn.silu(sums).astype(BF)
    skip1 = skip_step(n0 // 2, plan, after(enc1_rim, mid_rim), w_dec1)
    dec2_rim, own, send = rim_step(
        n0 // 4, plan, recv, own, strips_of(sums), skip=skip1, wn=w_dec1
    )

    recv = trade(send)
    dec1, sums = dec_conv(enc1, enc1_rim, patched(dec2, dec2_rim), None, w_dec1, 4)
    dec1_rim, own, send = rim_step(
        n0 // 2, plan, recv, own, sums, skip=skip0, wn=w_dec0
    )

    recv = trade(send)
    dec0, sums = dec_conv(enc0, enc0_rim, dec1, dec1_rim, w_dec0, 1)
    return last_step(dec0, plan, recv, own, sums)


def solution(mesh):
    return jax.shard_map(
        per_device,
        mesh=mesh,
        in_specs=(P(("grp", "tile"), None, None, None), P(), P(), P(), P(), P(), P(), P(), P()),
        out_specs=P(("grp", "tile"), None, None, None),
        check_vma=False,
    )
```

profile of v0, /device:TPU:15, one launch (start us, length us, event | category | flops | bytes accessed | tf_op | source)
XLA Modules:
  0.0 311.8 jit_solution(10236222690323489154)
XLA Ops:
  0.0 0.8 constant_dynamic-slice_fusion.1
  1.2 7.3 %tile_rims.1 = (bf16[24,4,48,128]{3,2,1,0:T(8,128)(2,1)S(1)}, bf16[176,48,128]{2,1,0:T(8,128)(2,1)}) custom-call(s32[96]{0:T(128)S(1)} %compare_select_fusion.4.slot_ref.refs_2_, bf16[24,48,48,128]{3,2,1,0:T(8,128)(2,1)} %refs_0_.1, bf16[24,48,48,128]{3,2,1,0:T(8,128)(2,1)} %refs_0_.1, bf16[24,48,48,128]{3,2,1,0:T(8,128)(2,1)} %refs_0_.1, ...), custom_call_target="tpu_custom_call" | custom-call | tf_op jit(solution)/shard_map/tile_rims/pallas_call | solution.py:145
  8.5 1.0 copy-done.10
  9.5 6.7 %all-to-all-start = ((bf16[16,528,128]{2,1,0:T(8,128)(2,1)}), bf16[16,528,128]{2,1,0:T(8,128)(2,1)S(1)}, u32[]{:S(2)}, u32[]{:S(2)}) async-start(bf16[16,528,128]{2,1,0:T(8,128)(2,1)} %bitcast.13), calls=%async_computation | async-start | bytes 4325376 | tf_op jit(solution)/shard_map/all_to_all | solution.py:867
  16.7 0.7 convert_reduce_fusion.5
  17.6 5.1 %gather_fusion = s32[2304,4]{1,0:T(8,128)} fusion(s32[384,4]{1,0:T(8,128)S(1)} %slice_bitcast_fusion, s32[3072]{0:T(1024)S(1)} %pad_clamp_fusion), kind=kCustom, calls=%fused_computation | custom fusion | bytes 82944 | tf_op jit(solution)/shard_map/jit(_take)/gather | solution.py:96
  22.7 1.7 copy.146
  24.8 0.7 pad_add_fusion.refs_4_
  25.5 0.7 pad_add_fusion.1.refs_5_.refs_2_
  26.4 39.8 %enc_conv.2 = (bf16[24,24,2,48,128]{4,3,2,1,0:T(8,128)(2,1)}, f32[24,4,48,128]{3,2,1,0:T(8,128)S(1)}, bf16[24,4,48,128]{3,2,1,0:T(8,128)(2,1)S(1)}, bf16[24,24,24,128]{3,2,1,0:T(8,128)(2,1)}) custom-call(bf16[24,48,48,128]{3,2,1,0:T(8,128)(2,1)} %refs_0_.1, bf16[9,128,128]{2,1,0:T(8,128)(2,1)S(1)} %bitcast.195), custom_call_target="tpu_custom_call" | custom-call | flops 21743271936 | bytes 33177600 | tf_op jit(solution)/shard_map/enc_conv/pallas_call | solution.py:753
  66.1 1.4 copy-done.3
  67.5 1.0 copy-done.12
  68.6 1.4 copy-done.27
  69.9 8.2 %rim_step.6 = (bf16[96,48,128]{2,1,0:T(8,128)(2,1)S(1)}, bf16[96,24,128]{2,1,0:T(8,128)(2,1)S(1)}, bf16[176,24,128]{2,1,0:T(8,128)(2,1)}) custom-call(s32[96]{0:T(128)S(1)} %add_select_fusion.2.refs_0_.pick_ref, s32[96]{0:T(128)S(1)} %get-tuple-element.77.refs_1_.refs_0_, s32[96]{0:T(128)S(1)} %compare_select_fusion.4.slot_ref.refs_2_, ...), custom_call_target="tpu_custom_call" | custom-call | flops 1811939328 | bytes 6912000 | tf_op jit(solution)/shard_map/rim_step/pallas_call | solution.py:443
  78.1 1.1 copy-done.7
  79.2 6.2 %all-to-all-start.1 = ((bf16[16,264,128]{2,1,0:T(8,128)(2,1)}), bf16[16,264,128]{2,1,0:T(8,128)(2,1)}, u32[]{:S(2)}, u32[]{:S(2)}) async-start(bf16[16,264,128]{2,1,0:T(8,128)(2,1)} %bitcast.19), calls=%async_computation.1 | async-start | bytes 2162688 | tf_op jit(solution)/shard_map/all_to_all | solution.py:867
  85.4 15.6 %enc_conv.3 = (bf16[24,12,2,24,128]{4,3,2,1,0:T(8,128)(2,1)}, f32[24,4,24,128]{3,2,1,0:T(8,128)S(1)}, bf16[24,4,24,128]{3,2,1,0:T(8,128)(2,1)S(1)}, bf16[24,12,12,128]{3,2,1,0:T(8,128)(2,1)S(1)}) custom-call(bf16[24,24,24,128]{3,2,1,0:T(8,128)(2,1)} %get-tuple-element.47.refs_0_, bf16[9,128,128]{2,1,0:T(8,128)(2,1)S(1)} %bitcast.199, ...), custom_call_target="tpu_custom_call" | custom-call | flops 5435817984 | bytes 8294400 | tf_op jit(solution)/shard_map/enc_conv/pallas_call | solution.py:753
  101.0 1.0 copy-done.13
  102.0 1.4 slice.167
  103.4 7.7 %all-to-all-done.1 = bf16[16,264,128]{2,1,0:T(8,128)(2,1)} async-done(((bf16[16,264,128]{2,1,0:T(8,128)(2,1)}), bf16[16,264,128]{2,1,0:T(8,128)(2,1)}, u32[]{:S(2)}, u32[]{:S(2)}) %all-to-all-start.1) | async-done | bytes 1081376 | tf_op jit(solution)/shard_map/all_to_all | solution.py:867
  111.1 5.3 %rim_step.7 = (bf16[96,24,128]{2,1,0:T(8,128)(2,1)S(1)}, bf16[96,16,128]{2,1,0:T(8,128)(2,1)S(1)}, bf16[176,16,128]{2,1,0:T(8,128)(2,1)}) custom-call(s32[96]{0:T(128)S(1)} %add_select_fusion.2.refs_0_.pick_ref, s32[96]{0:T(128)S(1)} %get-tuple-element.77.refs_1_.refs_0_, s32[96]{0:T(128)S(1)} %compare_select_fusion.4.slot_ref.refs_2_, ...), custom_call_target="tpu_custom_call" | custom-call | flops 905969664 | bytes 3456000 | tf_op jit(solution)/shard_map/rim_step/pallas_call | solution.py:443
  116.4 0.8 copy-done.16
  117.3 5.0 %all-to-all-start.2 = ((bf16[16,176,128]{2,1,0:T(8,128)(2,1)}), bf16[16,176,128]{2,1,0:T(8,128)(2,1)S(1)}, u32[]{:S(2)}, u32[]{:S(2)}) async-start(bf16[16,176,128]{2,1,0:T(8,128)(2,1)} %bitcast.25), calls=%async_computation.2 | async-start | bytes 1441792 | tf_op jit(solution)/shard_map/all_to_all | solution.py:867
  122.6 0.7 pad_maximum_fusion
  123.3 2.6 multiply_convert_fusion
  126.1 0.9 slice.237
  127.5 12.6 %all-to-all-done.2 = bf16[16,176,128]{2,1,0:T(8,128)(2,1)S(1)} async-done(((bf16[16,176,128]{2,1,0:T(8,128)(2,1)}), bf16[16,176,128]{2,1,0:T(8,128)(2,1)S(1)}, u32[]{:S(2)}, u32[]{:S(2)}) %all-to-all-start.2) | async-done | bytes 720928 | tf_op jit(solution)/shard_map/all_to_all | solution.py:867
  140.2 3.7 %rim_step.8 = (bf16[96,16,128]{2,1,0:T(8,128)(2,1)S(1)}, bf16[96,8,128]{2,1,0:T(8,128)(2,1)S(1)}, bf16[176,8,128]{2,1,0:T(8,128)(2,1)}) custom-call(s32[96]{0:T(128)S(1)} %add_select_fusion.2.refs_0_.pick_ref, s32[96]{0:T(128)S(1)} %get-tuple-element.77.refs_1_.refs_0_, s32[96]{0:T(128)S(1)} %compare_select_fusion.4.slot_ref.refs_2_, ...), custom_call_target="tpu_custom_call" | custom-call | flops 603979776 | bytes 2304000 | tf_op jit(solution)/shard_map/rim_step/pallas_call | solution.py:443
  144.0 1.7 fusion.18
  145.8 0.7 copy-done.32
  146.5 4.9 %all-to-all-start.3 = ((bf16[16,88,128]{2,1,0:T(8,128)(2,1)}), bf16[16,88,128]{2,1,0:T(8,128)(2,1)S(1)}, u32[]{:S(2)}, u32[]{:S(2)}) async-start(bf16[16,88,128]{2,1,0:T(8,128)(2,1)} %bitcast.37), calls=%async_computation.3 | async-start | bytes 720896 | tf_op jit(solution)/shard_map/all_to_all | solution.py:867
  151.8 0.6 copy.222
  152.5 3.5 %skip_step.3.refs_10_ = f32[96,16,128]{2,1,0:T(8,128)S(1)} custom-call(s32[96]{0:T(128)S(1)} %get-tuple-element.77.refs_1_.refs_0_, s32[96]{0:T(128)S(1)} %get-tuple-element.78.refs_3_.refs_1_, s32[97]{0:T(128)S(1)} %pad_add_fusion.1.refs_5_.refs_2_, bf16[96,16,128]{2,1,0:T(8,128)(2,1)S(1)} %get-tuple-element.55.refs_3_, bf16[9,256,128]{2,1,0:T(8,128)(2,1)S(1)} %bitcast.170), custom_call_target="tpu_custom_call" | custom-call | flops 301989888 | bytes 1179648 | tf_op jit(solution)/shard_map/skip_step/pallas_call | solution.py:275
  156.0 1.0 multiply_convert_fusion.1
  157.0 4.5 %all-to-all-done.3 = bf16[16,88,128]{2,1,0:T(8,128)(2,1)S(1)} async-done(((bf16[16,88,128]{2,1,0:T(8,128)(2,1)}), bf16[16,88,128]{2,1,0:T(8,128)(2,1)S(1)}, u32[]{:S(2)}, u32[]{:S(2)}) %all-to-all-start.3) | async-done | bytes 360480 | tf_op jit(solution)/shard_map/all_to_all | solution.py:867
  161.5 6.1 %rim_step.9 = (bf16[96,8,128]{2,1,0:T(8,128)(2,1)S(1)}, bf16[96,16,128]{2,1,0:T(8,128)(2,1)S(1)}, bf16[176,16,128]{2,1,0:T(8,128)(2,1)}) custom-call(s32[96]{0:T(128)S(1)} %add_select_fusion.2.refs_0_.pick_ref, s32[96]{0:T(128)S(1)} %get-tuple-element.77.refs_1_.refs_0_, s32[96]{0:T(128)S(1)} %compare_select_fusion.4.slot_ref.refs_2_, ...), custom_call_target="tpu_custom_call" | custom-call | flops 301989888 | bytes 1152000 | tf_op jit(solution)/shard_map/rim_step/pallas_call | solution.py:443
  167.6 0.8 copy-done.19
  168.4 5.0 %all-to-all-start.4 = ((bf16[16,176,128]{2,1,0:T(8,128)(2,1)}), bf16[16,176,128]{2,1,0:T(8,128)(2,1)S(1)}, u32[]{:S(2)}, u32[]{:S(2)}) async-start(bf16[16,176,128]{2,1,0:T(8,128)(2,1)} %bitcast.48), calls=%async_computation.4 | async-start | bytes 1441792 | tf_op jit(solution)/shard_map/all_to_all | solution.py:867
  173.7 0.7 copy-done.31
  174.4 4.5 %fusion.4 = f32[24,12,12,128]{3,0,2,1:T(8,128)S(1)} fusion(bf16[3,3,256,128]{3,2,1,0:T(8,128)(2,1)S(1)} %copy-done.2, bf16[24,1,12,128]{3,0,2,1:T(8,128)(2,1)S(1)} %copy.192, bf16[24,10,1,128]{3,0,2,1:T(8,128)(2,1)S(1)} %bitcast.215, bf16[24,10,10,128]{3,0,2,1:T(8,128)(2,1)S(1)} %copy-done.31, bf16[24,10,1,128]{3,0,2,1:T(8,128)(2,1)S(1)} %bitcast.216, ...), kind=kOutput, calls=%fused_computation.7 | convolution fusion | flops 1828847616 | bytes 4128768 | tf_op jit(solution)/shard_map/conv_general_dilated | solution.py:837
  179.3 0.9 copy-done.29
  180.3 0.3 copy-done.4
  180.6 0.3 copy-done.17
  180.9 3.6 %skip_step.4.refs_9_ = f32[96,24,128]{2,1,0:T(8,128)S(1)} custom-call(s32[96]{0:T(128)S(1)} %get-tuple-element.77.refs_1_.refs_0_, s32[96]{0:T(128)S(1)} %get-tuple-element.78.refs_3_.refs_1_, s32[97]{0:T(128)S(1)} %pad_add_fusion.1.refs_5_.refs_2_, bf16[96,24,128]{2,1,0:T(8,128)(2,1)S(1)} %copy-done.17, bf16[9,256,128]{2,1,0:T(8,128)(2,1)S(1)} %bitcast.173), custom_call_target="tpu_custom_call" | custom-call | flops 452984832 | bytes 1769472 | tf_op jit(solution)/shard_map/skip_step/pallas_call | solution.py:275
  184.5 1.0 copy-done
  185.6 5.7 %all-to-all-done.4 = bf16[16,176,128]{2,1,0:T(8,128)(2,1)S(1)} async-done(((bf16[16,176,128]{2,1,0:T(8,128)(2,1)}), bf16[16,176,128]{2,1,0:T(8,128)(2,1)S(1)}, u32[]{:S(2)}, u32[]{:S(2)}) %all-to-all-start.4) | async-done | bytes 720928 | tf_op jit(solution)/shard_map/all_to_all | solution.py:867
  191.2 6.7 %rim_step.10 = (bf16[96,16,128]{2,1,0:T(8,128)(2,1)S(1)}, bf16[96,24,128]{2,1,0:T(8,128)(2,1)S(1)}, bf16[176,24,128]{2,1,0:T(8,128)(2,1)}) custom-call(s32[96]{0:T(128)S(1)} %add_select_fusion.2.refs_0_.pick_ref, s32[96]{0:T(128)S(1)} %get-tuple-element.77.refs_1_.refs_0_, s32[96]{0:T(128)S(1)} %compare_select_fusion.4.slot_ref.refs_2_, ...), custom_call_target="tpu_custom_call" | custom-call | flops 603979776 | bytes 2304000 | tf_op jit(solution)/shard_map/rim_step/pallas_call | solution.py:443
  197.9 0.8 copy-done.14
  198.7 5.2 %all-to-all-start.5 = ((bf16[16,264,128]{2,1,0:T(8,128)(2,1)}), bf16[16,264,128]{2,1,0:T(8,128)(2,1)S(1)}, u32[]{:S(2)}, u32[]{:S(2)}) async-start(bf16[16,264,128]{2,1,0:T(8,128)(2,1)} %bitcast.211), calls=%async_computation.5 | async-start | bytes 2162688 | tf_op jit(solution)/shard_map/all_to_all | solution.py:867
  203.9 1.3 copy-done.8
  205.2 6.4 %skip_step.5.refs_9_ = f32[96,48,128]{2,1,0:T(8,128)} custom-call(s32[96]{0:T(128)S(1)} %get-tuple-element.77.refs_1_.refs_0_, s32[96]{0:T(128)S(1)} %get-tuple-element.78.refs_3_.refs_1_, s32[97]{0:T(128)S(1)} %pad_add_fusion.1.refs_5_.refs_2_, bf16[96,48,128]{2,1,0:T(8,128)(2,1)S(1)} %copy-done.8, bf16[9,256,128]{2,1,0:T(8,128)(2,1)S(1)} %bitcast.167), custom_call_target="tpu_custom_call" | custom-call | flops 905969664 | bytes 3538944 | tf_op jit(solution)/shard_map/skip_step/pallas_call | solution.py:275
  211.6 0.5 fusion.3
  212.5 0.7 pad_maximum_fusion.1.u_ref
  213.3 18.2 %dec_conv.2 = (bf16[24,12,2,24,128]{4,3,2,1,0:T(8,128)(2,1)}, f32[24,4,24,128]{3,2,1,0:T(8,128)S(1)}) custom-call(bf16[24,24,24,128]{3,2,1,0:T(8,128)(2,1)} %bitcast.220, bf16[24,4,24,128]{3,2,1,0:T(8,128)(2,1)S(1)} %bitcast.190, bf16[24,12,12,128]{3,2,1,0:T(8,128)(2,1)S(1)} %pad_maximum_fusion.1.u_ref, bf16[9,256,128]{2,1,0:T(8,128)(2,1)S(1)} %bitcast.175), custom_call_target="tpu_custom_call" | custom-call | flops 8139571200 | bytes 8294400 | tf_op jit(solution)/shard_map/dec_conv/pallas_call | solution.py:793
  231.5 1.0 copy-done.11
  232.5 1.1 copy-done.15
  233.6 9.0 %rim_step.11 = (bf16[96,24,128]{2,1,0:T(8,128)(2,1)S(1)}, bf16[96,48,128]{2,1,0:T(8,128)(2,1)S(1)}, bf16[176,48,128]{2,1,0:T(8,128)(2,1)}) custom-call(s32[96]{0:T(128)S(1)} %add_select_fusion.2.refs_0_.pick_ref, s32[96]{0:T(128)S(1)} %get-tuple-element.77.refs_1_.refs_0_, s32[96]{0:T(128)S(1)} %compare_select_fusion.4.slot_ref.refs_2_, ...), custom_call_target="tpu_custom_call" | custom-call | flops 905969664 | bytes 3456000 | tf_op jit(solution)/shard_map/rim_step/pallas_call | solution.py:443
  242.6 1.0 copy-done.5
  243.7 0.8 copy-done.25
  244.5 6.7 %all-to-all-start.6 = ((bf16[16,528,128]{2,1,0:T(8,128)(2,1)}), bf16[16,528,128]{2,1,0:T(8,128)(2,1)S(1)}, u32[]{:S(2)}, u32[]{:S(2)}) async-start(bf16[16,528,128]{2,1,0:T(8,128)(2,1)} %bitcast.209), calls=%async_computation.6 | async-start | bytes 4325376 | tf_op jit(solution)/shard_map/all_to_all | solution.py:867
  251.2 1.3 copy-done.9
  252.5 48.7 %dec_conv.3 = (bf16[24,24,2,48,128]{4,3,2,1,0:T(8,128)(2,1)}, f32[24,4,48,128]{3,2,1,0:T(8,128)}) custom-call(bf16[24,48,48,128]{3,2,1,0:T(8,128)(2,1)} %bitcast.219, bf16[24,4,48,128]{3,2,1,0:T(8,128)(2,1)S(1)} %bitcast.183, bf16[24,24,24,128]{3,2,1,0:T(8,128)(2,1)} %bitcast.221, bf16[24,4,24,128]{3,2,1,0:T(8,128)(2,1)S(1)} %bitcast.203, ...), custom_call_target="tpu_custom_call" | custom-call | flops 32558284800 | bytes 33177600 | tf_op jit(solution)/shard_map/dec_conv/pallas_call | solution.py:793
  301.2 1.3 copy-done.6
  302.4 9.2 %last_step.1 = bf16[24,48,48,128]{3,2,1,0:T(8,128)(2,1)} custom-call(s32[96]{0:T(128)S(1)} %add_select_fusion.2.refs_0_.pick_ref, bf16[176,48,128]{2,1,0:T(8,128)(2,1)S(1)} %bitcast.161, bf16[96,48,128]{2,1,0:T(8,128)(2,1)S(1)} %copy-done.6, f32[96,48,128]{2,1,0:T(8,128)} %bitcast.208, ...), custom_call_target="tpu_custom_call", output_to_operand_aliasing={{}: (4, {})} | custom-call | tf_op jit(solution)/shard_map/last_step/pallas_call | solution.py:712
  (124 shorter events, 4.1 us)
Async XLA Ops:
  8.5 1.0 copy-start.10
  9.5 6.7 %copy-start.34 = (s32[384,4,2]{0,2,1:T(2,128)S(1)}, s32[384,4,2]{0,2,1:T(2,128)}, u32[]{:S(2)}) copy-start(s32[384,4,2]{0,2,1:T(2,128)} %param.10) | copy-start | bytes 36868
  9.5 59.0 %all-to-all-start = ((bf16[16,528,128]{2,1,0:T(8,128)(2,1)}), bf16[16,528,128]{2,1,0:T(8,128)(2,1)S(1)}, u32[]{:S(2)}, u32[]{:S(2)}) async-start(bf16[16,528,128]{2,1,0:T(8,128)(2,1)} %bitcast.13), calls=%async_computation | async-start | bytes 4325376 | tf_op jit(solution)/shard_map/all_to_all | solution.py:867
  17.6 8.7 %copy-start.21 = (bf16[3,3,128,128]{3,2,1,0:T(8,128)(2,1)S(1)}, bf16[3,3,128,128]{3,2,1,0:T(8,128)(2,1)}, u32[]{:S(2)}) copy-start(bf16[3,3,128,128]{3,2,1,0:T(8,128)(2,1)} %param.11) | copy-start | bytes 884740
  66.1 1.4 copy-start.3
  67.5 1.0 copy-start.12
  68.6 1.4 copy-start.27
  78.1 1.1 copy-start.7
  79.2 6.2 %copy-start.24 = (bf16[3,3,128,128]{3,2,1,0:T(8,128)(2,1)S(1)}, bf16[3,3,128,128]{3,2,1,0:T(8,128)(2,1)}, u32[]{:S(2)}) copy-start(bf16[3,3,128,128]{3,2,1,0:T(8,128)(2,1)} %param.12) | copy-start | bytes 884740
  79.2 31.9 %all-to-all-start.1 = ((bf16[16,264,128]{2,1,0:T(8,128)(2,1)}), bf16[16,264,128]{2,1,0:T(8,128)(2,1)}, u32[]{:S(2)}, u32[]{:S(2)}) async-start(bf16[16,264,128]{2,1,0:T(8,128)(2,1)} %bitcast.19), calls=%async_computation.1 | async-start | bytes 2162688 | tf_op jit(solution)/shard_map/all_to_all | solution.py:867
  101.0 1.0 copy-start.13
  116.4 0.8 copy-start.16
  117.2 5.3 %copy-start.28 = (bf16[24,10,10,128]{3,2,1,0:T(8,128)(2,1)S(1)}, bf16[24,10,10,128]{3,2,1,0:T(8,128)(2,1)}, u32[]{:S(2)}) copy-start(bf16[24,10,10,128]{3,2,1,0:T(8,128)(2,1)} %slice.167) | copy-start | bytes 1843204
  117.3 22.8 %all-to-all-start.2 = ((bf16[16,176,128]{2,1,0:T(8,128)(2,1)}), bf16[16,176,128]{2,1,0:T(8,128)(2,1)S(1)}, u32[]{:S(2)}, u32[]{:S(2)}) async-start(bf16[16,176,128]{2,1,0:T(8,128)(2,1)} %bitcast.25), calls=%async_computation.2 | async-start | bytes 1441792 | tf_op jit(solution)/shard_map/all_to_all | solution.py:867
  122.3 1.0 copy-start.22
  145.7 0.8 copy-start.32
  146.5 15.0 %all-to-all-start.3 = ((bf16[16,88,128]{2,1,0:T(8,128)(2,1)}), bf16[16,88,128]{2,1,0:T(8,128)(2,1)S(1)}, u32[]{:S(2)}, u32[]{:S(2)}) async-start(bf16[16,88,128]{2,1,0:T(8,128)(2,1)} %bitcast.37), calls=%async_computation.3 | async-start | bytes 720896 | tf_op jit(solution)/shard_map/all_to_all | solution.py:867
  151.4 1.1 copy-start.2
  151.6 9.9 %copy-start.23 = (bf16[3,3,128,128]{3,2,1,0:T(8,128)(2,1)S(1)}, bf16[3,3,128,128]{3,2,1,0:T(8,128)(2,1)}, u32[]{:S(2)}) copy-start(bf16[3,3,128,128]{3,2,1,0:T(8,128)(2,1)} %param.14) | copy-start | bytes 884740
  167.6 0.8 copy-start.19
  168.4 22.9 %all-to-all-start.4 = ((bf16[16,176,128]{2,1,0:T(8,128)(2,1)}), bf16[16,176,128]{2,1,0:T(8,128)(2,1)S(1)}, u32[]{:S(2)}, u32[]{:S(2)}) async-start(bf16[16,176,128]{2,1,0:T(8,128)(2,1)} %bitcast.48), calls=%async_computation.4 | async-start | bytes 1441792 | tf_op jit(solution)/shard_map/all_to_all | solution.py:867
  173.4 1.1 copy-start.31
  173.4 1.1 copy-start.33
  179.0 1.2 copy-start.29
  179.1 1.5 copy-start.4
  179.1 1.8 copy-start.17
  180.2 11.0 %copy-start.20 = (bf16[96,16,128]{2,1,0:T(8,128)(2,1)S(1)}, bf16[96,16,128]{2,1,0:T(8,128)(2,1)}, u32[]{:S(2)}) copy-start(bf16[96,16,128]{2,1,0:T(8,128)(2,1)} %copy-done.19) | copy-start | bytes 1179652
  184.5 1.0 copy-start
  197.9 0.8 copy-start.14
  198.7 5.2 %copy-start.1 = (bf16[3,3,256,128]{3,2,1,0:T(8,128)(2,1)S(1)}, bf16[3,3,256,128]{3,2,1,0:T(8,128)(2,1)}, u32[]{:S(2)}) copy-start(bf16[3,3,256,128]{3,2,1,0:T(8,128)(2,1)} %param.17) | copy-start | bytes 1769476
  198.7 33.8 %all-to-all-start.5 = ((bf16[16,264,128]{2,1,0:T(8,128)(2,1)}), bf16[16,264,128]{2,1,0:T(8,128)(2,1)S(1)}, u32[]{:S(2)}, u32[]{:S(2)}) async-start(bf16[16,264,128]{2,1,0:T(8,128)(2,1)} %bitcast.211), calls=%async_computation.5 | async-start | bytes 2162688 | tf_op jit(solution)/shard_map/all_to_all | solution.py:867
  203.9 1.3 copy-start.8
  205.2 6.4 %copy-start.30 = (f32[24,12,12,128]{3,0,2,1:T(8,128)S(1)}, f32[24,12,12,128]{3,0,2,1:T(8,128)}, u32[]{:S(2)}) copy-start(f32[24,12,12,128]{3,0,2,1:T(8,128)} %copy-done.29) | copy-start | bytes 5308420
  212.2 1.1 copy-start.18
  231.5 1.0 copy-start.11
  232.5 1.1 copy-start.15
  242.6 1.0 copy-start.5
  243.7 0.8 copy-start.25
  244.5 6.7 %copy-start.26 = (bf16[96,24,128]{2,1,0:T(8,128)(2,1)S(1)}, bf16[96,24,128]{2,1,0:T(8,128)(2,1)}, u32[]{:S(2)}) copy-start(bf16[96,24,128]{2,1,0:T(8,128)(2,1)} %copy-done.25) | copy-start | bytes 1769476
  244.5 56.6 %all-to-all-start.6 = ((bf16[16,528,128]{2,1,0:T(8,128)(2,1)}), bf16[16,528,128]{2,1,0:T(8,128)(2,1)S(1)}, u32[]{:S(2)}, u32[]{:S(2)}) async-start(bf16[16,528,128]{2,1,0:T(8,128)(2,1)} %bitcast.209), calls=%async_computation.6 | async-start | bytes 4325376 | tf_op jit(solution)/shard_map/all_to_all | solution.py:867
  251.2 1.3 copy-start.9
  301.2 1.3 copy-start.6
where the time goes:
time: 317 us; the launch traced here: 312 us
  Pallas kernels  191 us (60%)
  starting transfers between devices  39.7 us (13%)
  local copies, waits for them, and re-layouts  34.3 us (11%)
  waiting for transfers between devices  30.5 us (10%)
  matrix products  8.83 us (3%)
  other arithmetic  6.22 us (2%)
    pallas_call x2, Pallas kernels, dec_conv(): pl.pallas_call(dec_kernel, grid=(tiles // g,), in_specs=specs + [whole_sp...  66.9 us
    pallas_call x2, Pallas kernels, enc_conv(): pl.pallas_call(enc_kernel, grid=(tiles // g,), in_specs=specs, out_specs=...  55.4 us
    all_to_all x7, starting transfers between devices, trade(): lax.all_to_all(strips.reshape(devices, cap * length, 128), 'tile', split_...  39.7 us
    pallas_call x6, Pallas kernels, rim_step(): pl.pallas_call(kernel, in_specs=[smem] * 6 + [vmem] * len(args), out_spec...  39.1 us
    all_to_all x7, waiting for transfers between devices, trade(): lax.all_to_all(strips.reshape(devices, cap * length, 128), 'tile', split_...  30.5 us
    unnamed x86, local copies, waits for them, and re-layouts  22.5 us
    pallas_call x3, Pallas kernels, skip_step(): pl.pallas_call(lambda *refs: skip_kernel(n, *refs), in_specs=[smem, smem,...  13.5 us
    pallas_call x1, Pallas kernels, last_step(): pl.pallas_call(last_kernel, in_specs=[smem, vmem, vmem, vmem, anywhere],...  9.16 us
  transfers between devices with their start and end apart: 7, of which 4 were waited for; matrix products, arithmetic and copies ran while one was open for 8% of the time, Pallas kernels for 44%

commit v1 on v0

--- a/solution.py
+++ b/solution.py
@@ -7,6 +7,7 @@
 from jax.sharding import PartitionSpec as P
 
 FACE_TILES = 8
+EARLY_TILES = (0, 0, 0)
 VMEM_LIMIT = 50 * 2**20
 BF = jnp.bfloat16
 F32 = jnp.float32
@@ -92,14 +93,14 @@
     target = partner // tiles_here
     order = jnp.arange(strip_count, dtype=jnp.int32)
     remote = target != position
-    source_tiles = target[:, None] * tiles_here + jnp.arange(tiles_here, dtype=jnp.int32)[None, :]
-    their_partners = jnp.take(edge_table[:, :, 0], source_tiles, axis=0).reshape(
-        strip_count, strip_count
-    )
-    toward_me = their_partners // tiles_here == position
     wanted = partner % tiles_here * 4 + matching
-    before_wanted = order[None, :] < wanted[:, None]
-    recv_rank = jnp.sum((toward_me & before_wanted).astype(jnp.int32), axis=1)
+    toward_me = edge_table[:, :, 0].reshape(devices, strip_count) // tiles_here == position
+    before = (order[:, None] < order[None, :]).astype(BF)
+    ranks = jnp.dot(toward_me.astype(BF), before, preferred_element_type=F32).astype(BF)
+    blocks = jnp.arange(devices, dtype=jnp.int32)
+    from_target = (target[:, None] == blocks[None, :]).astype(BF)
+    their_ranks = jnp.dot(from_target, ranks, preferred_element_type=F32)
+    recv_rank = jnp.sum(jnp.where(wanted[:, None] == order[None, :], their_ranks, 0.0), axis=1).astype(jnp.int32)
     pick_row = jnp.where(remote, target * slot_count + recv_rank, devices * slot_count + wanted)
     odd = (matching != (order + 2) % 4) | (reversed_rows == 1)
     return (pick_row, reversed_rows, slot_row, matching, listed(remote), listed(odd))
@@ -164,7 +165,8 @@
 
 
 def silu(s):
-    return s / (1.0 + jnp.exp(-s))
+    half = s * 0.5
+    return half + half * jnp.tanh(half)
 
 
 def strip_shifts(h, n):
@@ -466,9 +468,11 @@
 
 
 def column_shifts(x, n):
-    col = lax.broadcasted_iota(jnp.int32, x.shape, 1)
-    down = jnp.where(col == 0, 0.0, pltpu.roll(x, 1, 1))
-    up = jnp.where(col == n - 1, 0.0, pltpu.roll(x, n - 1, 1))
+    sub = lax.broadcasted_iota(jnp.int32, (x.shape[0], 8, 128), 1)
+    down = pltpu.roll(x, 1, 1)
+    up = pltpu.roll(x, n - 1, 1)
+    down = jnp.concatenate([jnp.where(sub == 0, 0.0, down[:, 0:8]), down[:, 8:n]], axis=1)
+    up = jnp.concatenate([up[:, 0 : n - 8], jnp.where(sub == 7, 0.0, up[:, n - 8 : n])], axis=1)
     return down, x, up
 
 
@@ -501,10 +505,14 @@
     return acc if extra is None else acc + extra
 
 
-def pair_chunks(n):
+def pair_chunks(n, most):
     half = n // 2
-    m = 6 if half % 6 == 0 else half
+    m = max(m for m in range(1, most + 1) if half % m == 0)
     return [(q, m) for q in range(0, half, m)]
+
+
+ENC_PAIRS = {48: 24}
+DEC_PAIRS = {48: 12}
 
 
 def column_of(acc, m, lo, sublane, colbuf):
@@ -565,7 +573,7 @@
         if rim_ref is not None:
             x = with_rims(x, [rim_ref[g, e].astype(F32) for e in range(4)], n, colbuf)
         fill_pairs(pairs, x, n)
-        for q0, m in pair_chunks(n):
+        for q0, m in pair_chunks(n, ENC_PAIRS.get(n, 6)):
             acc = pair_sums(pairs, w_ref, q0, m, None)
             put_sums(acc, sums_ref, g, q0, m, n, colbuf)
             out = silu(acc).astype(BF)[:, 0:n]
@@ -586,28 +594,76 @@
         ring_ref[g, 3] = ringbuf[0].astype(BF)
 
 
-def dec_kernel(x_ref, rim_ref, u_ref, *refs):
-    refs = list(refs)
-    urim_ref = refs.pop(0) if len(refs) == 10 else None
-    raw_ref, y_ref, sums_ref, pairs, rows, colbuf, acc_ref, w_ref, wu_ref = refs
+def skip_sums_kernel(x_ref, rim_ref, raw_ref, out_ref, pairs, colbuf, w_ref):
+    n = x_ref.shape[1]
 
     @pl.when(pl.program_id(0) == 0)
     def _():
         fill_pair_weights(raw_ref, 128, w_ref)
-        fill_coarse_weights(raw_ref, wu_ref)
-
-    group, n = x_ref.shape[0], x_ref.shape[1]
+
+    x = with_rims(x_ref[0].astype(F32), [rim_ref[0, e].astype(F32) for e in range(4)], n, colbuf)
+    fill_pairs(pairs, x, n)
+    for q0, m in pair_chunks(n, DEC_PAIRS.get(n, 6)):
+        out_ref[0, q0 : q0 + m] = pair_sums(pairs, w_ref, q0, m, None)
+
+
+def skip_sums(x, rim, w, first, count):
+    tiles, n, _, c = x.shape
+    half, n_p = n // 2, up16(n)
+    return pl.pallas_call(
+        skip_sums_kernel,
+        grid=(count,),
+        in_specs=[
+            pl.BlockSpec((1, n, n, c), lambda i: (first + i, 0, 0, 0)),
+            pl.BlockSpec((1, 4, n, c), lambda i: (first + i, 0, 0, 0)),
+            whole_spec((9, 2 * c, c)),
+        ],
+        out_specs=tile_spec(1, half, n_p, 2 * c),
+        out_shape=jax.ShapeDtypeStruct((count, half, n_p, 2 * c), F32),
+        scratch_shapes=[
+            pltpu.VMEM((half + 1, n_p, 768), BF),
+            pltpu.VMEM((n * 8, 128), F32),
+            pltpu.VMEM((1536, 256), BF),
+        ],
+        compiler_params=params(),
+        cost_estimate=pl.CostEstimate(
+            flops=count * n * n * 2 * 1536 * 128, bytes_accessed=count * n * n * 1300, transcendentals=0
+        ),
+        name="skip_sums",
+    )(x, rim.reshape(tiles, 4, n, c), w.reshape(9, 2 * c, c))
+
+
+def dec_kernel(ready, coarse_rims, aliased, *refs):
+    refs = list(refs)
+    if ready:
+        pre_ref = refs.pop(0)
+    else:
+        x_ref, rim_ref = refs.pop(0), refs.pop(0)
+    u_ref = refs.pop(0)
+    urim_ref = refs.pop(0) if coarse_rims else None
+    raw_ref = refs.pop(0)
+    if aliased:
+        refs = refs[2:]
+    y_ref, sums_ref, pairs, rows, colbuf, acc_ref, w_ref, wu_ref = refs
+    group, n = y_ref.shape[0], y_ref.shape[3]
     half = n // 2
     hp = rows.shape[1]
+
+    @pl.when(pl.program_id(0) == 0)
+    def _():
+        if not ready:
+            fill_pair_weights(raw_ref, 128, w_ref)
+        fill_coarse_weights(raw_ref, wu_ref)
 
     for g in range(group):
         u = u_ref[g].astype(F32)
         if urim_ref is not None:
             u = with_rims(u, [urim_ref[g, e].astype(F32) for e in range(4)], half, colbuf.at[0 : half * 8])
         fill_rows(rows, u, half)
-        x = with_rims(x_ref[g].astype(F32), [rim_ref[g, e].astype(F32) for e in range(4)], n, colbuf)
-        fill_pairs(pairs, x, n)
-        for q0, m in pair_chunks(n):
+        if not ready:
+            x = with_rims(x_ref[g].astype(F32), [rim_ref[g, e].astype(F32) for e in range(4)], n, colbuf)
+            fill_pairs(pairs, x, n)
+        for q0, m in pair_chunks(n, DEC_PAIRS.get(n, 6)):
             for b in range(2):
                 acc = None
                 for k in range(3):
@@ -619,7 +675,10 @@
                     for p in range(2):
                         acc_ref[p, i, pl.ds(b, half, 2), :] = acc[i, 0:half, p * 128 : p * 128 + 128]
             extra = jnp.concatenate([acc_ref[0], acc_ref[1]], axis=2)
-            acc = pair_sums(pairs, w_ref, q0, m, extra)
+            if ready:
+                acc = pre_ref[g, q0 : q0 + m] + extra
+            else:
+                acc = pair_sums(pairs, w_ref, q0, m, extra)
             put_sums(acc, sums_ref, g, q0, m, n, colbuf)
             out = silu(acc).astype(BF)[:, 0:n]
             y_ref[g, q0 : q0 + m, 0] = out[:, :, 0:128]
@@ -745,7 +804,7 @@
     tiles, n, _, c = x.shape
     half, n_p = n // 2, up16(n)
     g = group_of(tiles, want)
-    m = pair_chunks(n)[0][1]
+    m = pair_chunks(n, ENC_PAIRS.get(n, 6))[0][1]
     args, specs = [x, w.reshape(9, c, c)], [tile_spec(g, n, n, c), whole_spec((9, c, c))]
     if rim is not None:
         args.append(rim.reshape(tiles, 4, n, c))
@@ -780,21 +839,39 @@
     return y.reshape(tiles, n, n, c), strips(sums), strips(ring), s
 
 
-def dec_conv(x, rim, u, urim, w, want):
+def dec_conv(x, rim, u, urim, w, want, pre=None, first=0, last=None, base=None):
     tiles, n, _, c = x.shape
+    last = tiles if last is None else last
     half, n_p, h_p = n // 2, up16(n), up16(n // 2)
-    g = group_of(tiles, want)
-    m = pair_chunks(n)[0][1]
-    args = [x, rim.reshape(tiles, 4, n, c), u]
-    specs = [tile_spec(g, n, n, c), tile_spec(g, 4, n, c), tile_spec(g, half, half, c)]
+    g = group_of(last - first, want)
+    m = pair_chunks(n, DEC_PAIRS.get(n, 6))[0][1]
+    at = first // g
+    spec = lambda *dims: pl.BlockSpec((g,) + dims, lambda i: (at + i,) + (0,) * len(dims))
+    if pre is None:
+        args, specs = [x, rim.reshape(tiles, 4, n, c)], [spec(n, n, c), spec(4, n, c)]
+    else:
+        args, specs = [pre], [tile_spec(g, half, n_p, 2 * c)]
+    args, specs = args + [u], specs + [spec(half, half, c)]
     if urim is not None:
         args.append(urim.reshape(tiles, 4, half, c))
-        specs.append(tile_spec(g, 4, half, c))
+        specs.append(spec(4, half, c))
+    args.append(w.reshape(9, 2 * c, c))
+    specs.append(whole_spec((9, 2 * c, c)))
+    aliases = {}
+    if base is not None:
+        aliases = {len(args): 0, len(args) + 1: 1}
+        args += list(base)
+        specs += [pl.BlockSpec(memory_space=pl.ANY)] * 2
+
+    def kernel(*refs):
+        dec_kernel(pre is not None, urim is not None, base is not None, *refs)
+
+    count = last - first
     y, sums = pl.pallas_call(
-        dec_kernel,
-        grid=(tiles // g,),
-        in_specs=specs + [whole_spec((9, 2 * c, c))],
-        out_specs=[tile_spec(g, half, 2, n, c), tile_spec(g, 4, n, c)],
+        kernel,
+        grid=(count // g,),
+        in_specs=specs,
+        out_specs=[spec(half, 2, n, c), spec(4, n, c)],
         out_shape=[
             jax.ShapeDtypeStruct((tiles, half, 2, n, c), BF),
             jax.ShapeDtypeStruct((tiles, 4, n, c), F32),
@@ -807,13 +884,14 @@
             pltpu.VMEM((1536, 256), BF),
             pltpu.VMEM((2, 3, 256, 256), BF),
         ],
+        input_output_aliases=aliases,
         compiler_params=params(),
         cost_estimate=pl.CostEstimate(
-            flops=tiles * n * n * 2 * 2300 * 128, bytes_accessed=tiles * n * n * 600, transcendentals=tiles * n * n * 128
+            flops=count * n * n * 2 * 2300 * 128, bytes_accessed=count * n * n * 600, transcendentals=count * n * n * 128
         ),
         name="dec_conv",
-    )(*args, w.reshape(9, 2 * c, c))
-    return y.reshape(tiles, n, n, c), sums.reshape(tiles * 4, n, c)
+    )(*args)
+    return y, sums
 
 
 def strips_of(field, ring=0):
@@ -872,6 +950,15 @@
     def after(value, token):
         return lax.optimization_barrier((value, token))[0]
 
+    cuts = [0] + [tiles * share // 24 for share in EARLY_TILES] + [tiles]
+    early_tiles = list(zip(cuts[:-1], cuts[1:]))
+
+    def ahead(value, token, part):
+        first, last = early_tiles[part]
+        if last == first:
+            return value, None
+        return lax.optimization_barrier((value, skip_sums(enc0, after(enc0_rim, token), w_dec0, first, last - first)))
+
     rim0, send = tile_rims(features, slot_row, rows)
     rim0 = rim0.reshape(tiles * 4, n0, 128)
     plan = receive_plan(after(edge_table, send), slot_row, position, tiles, cap, devices)
@@ -885,6 +972,7 @@
 
     recv = trade(send)
     sums = inner_sums(patched(x2, x2_rim), w_enc2)
+    sums, early3 = ahead(sums, x2_rim, 0)
     enc2 = jax.nn.silu(sums).astype(BF)
     enc2_rim, x3_rim, send = rim_step(
         n0 // 4, plan, recv, x2_rim, strips_of(sums), w=w_enc2, ring=strips_of(enc2, 1)
@@ -893,6 +981,7 @@
     recv = trade(send)
     sums = inner_sums(patched(shrink(enc2), x3_rim), w_mid)
     middle = jax.nn.silu(sums).astype(BF)
+    sums, early4 = ahead(sums, x3_rim, 1)
     skip2 = skip_step(n0 // 4, plan, enc2_rim, w_dec2)
     skip0 = skip_step(n0, plan, after(enc0_rim, x3_rim), w_dec0)
     mid_rim, own, send = rim_step(
@@ -904,6 +993,7 @@
     joined = jnp.concatenate([enlarge(patched(middle, mid_rim)), patched(enc2, enc2_rim)], axis=3)
     sums = inner_sums(joined, w_dec2)
     dec2 = jax.nn.silu(sums).astype(BF)
+    sums, early5 = ahead(sums, mid_rim, 2)
     skip1 = skip_step(n0 // 2, plan, after(enc1_rim, mid_rim), w_dec1)
     dec2_rim, own, send = rim_step(
         n0 // 4, plan, recv, own, strips_of(sums), skip=skip1, wn=w_dec1
@@ -911,13 +1001,18 @@
 
     recv = trade(send)
     dec1, sums = dec_conv(enc1, enc1_rim, patched(dec2, dec2_rim), None, w_dec1, 4)
+    dec1, sums = dec1.reshape(enc1.shape), sums.reshape(x1_rim.shape)
     dec1_rim, own, send = rim_step(
         n0 // 2, plan, recv, own, sums, skip=skip0, wn=w_dec0
     )
 
     recv = trade(send)
-    dec0, sums = dec_conv(enc0, enc0_rim, dec1, dec1_rim, w_dec0, 1)
-    return last_step(dec0, plan, recv, own, sums)
+    base = None
+    for (first, last), pre in zip(early_tiles, (early3, early4, early5, None)):
+        if last > first:
+            base = dec_conv(enc0, enc0_rim, dec1, dec1_rim, w_dec0, 1, pre, first, last, base)
+    dec0, sums = base
+    return last_step(dec0.reshape(enc0.shape), plan, recv, own, sums.reshape(rim0.shape))
 
 
 def solution(mesh):

time: 317 us -> 313 us (0.987)
  Pallas kernels: 191 us -> 174 us
  waiting for transfers between devices: 30.5 us -> 43.3 us
  starting transfers between devices: 39.7 us -> 48.6 us
  local copies, waits for them, and re-layouts: 34.3 us -> 28.9 us
    all_to_all x7, waiting for transfers between devices: 30.5 us -> 43.3 us  [trade(): lax.all_to_all(strips.reshape(devices, cap * length, 128), 'tile', split_...]
    all_to_all x7, starting transfers between devices: 39.7 us -> 48.6 us  [trade(): lax.all_to_all(strips.reshape(devices, cap * length, 128), 'tile', split_...]
    gather x2 -> x0, local copies, waits for them, and re-layouts: 6.75 us -> none  [receive_plan(): jnp.take(edge_table[:, :, 0], source_tiles, axis=0)]
    pallas_call x2, Pallas kernels: 55.4 us -> 49.6 us  [enc_conv(): pl.pallas_call(enc_kernel, grid=(tiles // g,), in_specs=specs, out_specs=...]
    pallas_call x6, Pallas kernels: 39.1 us -> 34.1 us  [rim_step(): pl.pallas_call(kernel, in_specs=[smem] * 6 + [vmem] * len(args), out_spec...]
    pallas_call x3, Pallas kernels: 13.5 us -> 9.89 us  [skip_step(): pl.pallas_call(lambda *refs: skip_kernel(n, *refs), in_specs=[smem, smem,...]
    pallas_call x2, Pallas kernels: 66.9 us -> 63.7 us  [dec_conv(): pl.pallas_call(kernel, grid=(count // g,), in_specs=specs, out_specs=[spe...]
    unnamed x86 -> x88, local copies, waits for them, and re-layouts: 22.5 us -> 23.5 us
  transfers between devices with their start and end apart: 7 -> 7, of which waited for: 4 -> 6; matrix products, arithmetic and copies ran while one was open for 8% -> 6% of each run, Pallas kernels for 44% -> 40%
where the time goes in v1:
time: 313 us; the launch traced here: 311 us
  Pallas kernels  174 us (56%)
  starting transfers between devices  48.6 us (16%)
  waiting for transfers between devices  43.3 us (14%)
  local copies, waits for them, and re-layouts  28.9 us (9%)
  matrix products  9.18 us (3%)
  other arithmetic  6 us (2%)
    pallas_call x2, Pallas kernels, dec_conv(): pl.pallas_call(kernel, grid=(count // g,), in_specs=specs, out_specs=[spe...  63.7 us
    pallas_call x2, Pallas kernels, enc_conv(): pl.pallas_call(enc_kernel, grid=(tiles // g,), in_specs=specs, out_specs=...  49.6 us
    all_to_all x7, starting transfers between devices, trade(): lax.all_to_all(strips.reshape(devices, cap * length, 128), 'tile', split_...  48.6 us
    all_to_all x7, waiting for transfers between devices, trade(): lax.all_to_all(strips.reshape(devices, cap * length, 128), 'tile', split_...  43.3 us
    pallas_call x6, Pallas kernels, rim_step(): pl.pallas_call(kernel, in_specs=[smem] * 6 + [vmem] * len(args), out_spec...  34.1 us
    unnamed x88, local copies, waits for them, and re-layouts  23.5 us
    pallas_call x3, Pallas kernels, skip_step(): pl.pallas_call(lambda *refs: skip_kernel(n, *refs), in_specs=[smem, smem,...  9.89 us
    pallas_call x1, Pallas kernels, last_step(): pl.pallas_call(last_kernel, in_specs=[smem, vmem, vmem, vmem, anywhere],...  9.16 us
  transfers between devices with their start and end apart: 7, of which 6 were waited for; matrix products, arithmetic and copies ran while one was open for 6% of the time, Pallas kernels for 40%

profile of v1, /device:TPU:15, one launch (start us, length us, event | category | flops | bytes accessed | tf_op | source)
XLA Modules:
  0.0 310.7 jit_solution(1037032705371076695)
XLA Ops:
  0.0 0.8 constant_dynamic-slice_fusion.1
  1.2 7.3 %tile_rims.1 = (bf16[24,4,48,128]{3,2,1,0:T(8,128)(2,1)S(1)}, bf16[176,48,128]{2,1,0:T(8,128)(2,1)}) custom-call(s32[96]{0:T(128)S(1)} %compare_select_fusion.2.slot_ref.refs_2_, bf16[24,48,48,128]{3,2,1,0:T(8,128)(2,1)} %refs_0_.1, bf16[24,48,48,128]{3,2,1,0:T(8,128)(2,1)} %refs_0_.1, bf16[24,48,48,128]{3,2,1,0:T(8,128)(2,1)} %refs_0_.1, ...), custom_call_target="tpu_custom_call" | custom-call | tf_op jit(solution)/shard_map/tile_rims/pallas_call | solution.py:146
  8.5 1.0 copy-done.10
  9.5 6.7 %all-to-all-start = ((bf16[16,528,128]{2,1,0:T(8,128)(2,1)}), bf16[16,528,128]{2,1,0:T(8,128)(2,1)S(1)}, u32[]{:S(2)}, u32[]{:S(2)}) async-start(bf16[16,528,128]{2,1,0:T(8,128)(2,1)} %bitcast.11), calls=%async_computation | async-start | bytes 4325376 | tf_op jit(solution)/shard_map/all_to_all | solution.py:945
  17.1 0.7 convert_reduce_fusion.4
  18.2 0.7 pad_add_fusion.refs_4_
  18.9 0.7 pad_add_fusion.1.refs_5_.refs_2_
  20.0 34.6 %enc_conv.2 = (bf16[24,24,2,48,128]{4,3,2,1,0:T(8,128)(2,1)}, f32[24,4,48,128]{3,2,1,0:T(8,128)S(1)}, bf16[24,4,48,128]{3,2,1,0:T(8,128)(2,1)S(1)}, bf16[24,24,24,128]{3,2,1,0:T(8,128)(2,1)}) custom-call(bf16[24,48,48,128]{3,2,1,0:T(8,128)(2,1)} %refs_0_.1, bf16[9,128,128]{2,1,0:T(8,128)(2,1)S(1)} %bitcast.194), custom_call_target="tpu_custom_call" | custom-call | flops 21743271936 | bytes 33177600 | tf_op jit(solution)/shard_map/enc_conv/pallas_call | solution.py:812
  54.6 1.4 copy-done.3
  56.0 1.0 copy-done.12
  57.0 8.0 %all-to-all-done = bf16[16,528,128]{2,1,0:T(8,128)(2,1)S(1)} async-done(((bf16[16,528,128]{2,1,0:T(8,128)(2,1)}), bf16[16,528,128]{2,1,0:T(8,128)(2,1)S(1)}, u32[]{:S(2)}, u32[]{:S(2)}) %all-to-all-start) | async-done | bytes 2162720 | tf_op jit(solution)/shard_map/all_to_all | solution.py:945
  65.0 1.4 copy-done.27
  66.4 7.8 %rim_step.6 = (bf16[96,48,128]{2,1,0:T(8,128)(2,1)S(1)}, bf16[96,24,128]{2,1,0:T(8,128)(2,1)S(1)}, bf16[176,24,128]{2,1,0:T(8,128)(2,1)}) custom-call(s32[96]{0:T(128)S(1)} %add_select_fusion.2.refs_0_.pick_ref, s32[96]{0:T(128)S(1)} %get-tuple-element.77.refs_1_.refs_0_, s32[96]{0:T(128)S(1)} %compare_select_fusion.2.slot_ref.refs_2_, ...), custom_call_target="tpu_custom_call" | custom-call | flops 1811939328 | bytes 6912000 | tf_op jit(solution)/shard_map/rim_step/pallas_call | solution.py:445
  74.2 1.1 copy-done.7
  75.3 5.3 %all-to-all-start.1 = ((bf16[16,264,128]{2,1,0:T(8,128)(2,1)}), bf16[16,264,128]{2,1,0:T(8,128)(2,1)S(1)}, u32[]{:S(2)}, u32[]{:S(2)}) async-start(bf16[16,264,128]{2,1,0:T(8,128)(2,1)} %bitcast.17), calls=%async_computation.1 | async-start | bytes 2162688 | tf_op jit(solution)/shard_map/all_to_all | solution.py:945
  80.7 15.1 %enc_conv.3 = (bf16[24,12,2,24,128]{4,3,2,1,0:T(8,128)(2,1)}, f32[24,4,24,128]{3,2,1,0:T(8,128)S(1)}, bf16[24,4,24,128]{3,2,1,0:T(8,128)(2,1)S(1)}, bf16[24,12,12,128]{3,2,1,0:T(8,128)(2,1)S(1)}) custom-call(bf16[24,24,24,128]{3,2,1,0:T(8,128)(2,1)} %get-tuple-element.47.refs_0_, bf16[9,128,128]{2,1,0:T(8,128)(2,1)S(1)} %bitcast.198, ...), custom_call_target="tpu_custom_call" | custom-call | flops 5435817984 | bytes 8294400 | tf_op jit(solution)/shard_map/enc_conv/pallas_call | solution.py:812
  95.7 1.0 copy-done.13
  96.7 1.4 slice.167
  98.1 8.2 %all-to-all-done.1 = bf16[16,264,128]{2,1,0:T(8,128)(2,1)S(1)} async-done(((bf16[16,264,128]{2,1,0:T(8,128)(2,1)}), bf16[16,264,128]{2,1,0:T(8,128)(2,1)S(1)}, u32[]{:S(2)}, u32[]{:S(2)}) %all-to-all-start.1) | async-done | bytes 1081376 | tf_op jit(solution)/shard_map/all_to_all | solution.py:945
  106.3 1.0 copy-done.28
  107.3 5.0 %rim_step.7 = (bf16[96,24,128]{2,1,0:T(8,128)(2,1)S(1)}, bf16[96,16,128]{2,1,0:T(8,128)(2,1)S(1)}, bf16[176,16,128]{2,1,0:T(8,128)(2,1)}) custom-call(s32[96]{0:T(128)S(1)} %add_select_fusion.2.refs_0_.pick_ref, s32[96]{0:T(128)S(1)} %get-tuple-element.77.refs_1_.refs_0_, s32[96]{0:T(128)S(1)} %compare_select_fusion.2.slot_ref.refs_2_, ...), custom_call_target="tpu_custom_call" | custom-call | flops 905969664 | bytes 3456000 | tf_op jit(solution)/shard_map/rim_step/pallas_call | solution.py:445
  112.3 0.8 copy-done.16
  113.2 5.3 %all-to-all-start.2 = ((bf16[16,176,128]{2,1,0:T(8,128)(2,1)}), bf16[16,176,128]{2,1,0:T(8,128)(2,1)S(1)}, u32[]{:S(2)}, u32[]{:S(2)}) async-start(bf16[16,176,128]{2,1,0:T(8,128)(2,1)} %bitcast.23), calls=%async_computation.2 | async-start | bytes 1441792 | tf_op jit(solution)/shard_map/all_to_all | solution.py:945
  118.8 0.7 pad_maximum_fusion
  119.5 2.6 multiply_convert_fusion
  122.3 0.9 slice.235
  123.7 12.6 %all-to-all-done.2 = bf16[16,176,128]{2,1,0:T(8,128)(2,1)S(1)} async-done(((bf16[16,176,128]{2,1,0:T(8,128)(2,1)}), bf16[16,176,128]{2,1,0:T(8,128)(2,1)S(1)}, u32[]{:S(2)}, u32[]{:S(2)}) %all-to-all-start.2) | async-done | bytes 720928 | tf_op jit(solution)/shard_map/all_to_all | solution.py:945
  136.4 3.5 %rim_step.8 = (bf16[96,16,128]{2,1,0:T(8,128)(2,1)S(1)}, bf16[96,8,128]{2,1,0:T(8,128)(2,1)S(1)}, bf16[176,8,128]{2,1,0:T(8,128)(2,1)}) custom-call(s32[96]{0:T(128)S(1)} %add_select_fusion.2.refs_0_.pick_ref, s32[96]{0:T(128)S(1)} %get-tuple-element.77.refs_1_.refs_0_, s32[96]{0:T(128)S(1)} %compare_select_fusion.2.slot_ref.refs_2_, ...), custom_call_target="tpu_custom_call" | custom-call | flops 603979776 | bytes 2304000 | tf_op jit(solution)/shard_map/rim_step/pallas_call | solution.py:445
  140.0 1.7 fusion.19
  141.7 0.7 copy-done.33
  142.5 5.2 %all-to-all-start.3 = ((bf16[16,88,128]{2,1,0:T(8,128)(2,1)}), bf16[16,88,128]{2,1,0:T(8,128)(2,1)S(1)}, u32[]{:S(2)}, u32[]{:S(2)}) async-start(bf16[16,88,128]{2,1,0:T(8,128)(2,1)} %bitcast.35), calls=%async_computation.3 | async-start | bytes 720896 | tf_op jit(solution)/shard_map/all_to_all | solution.py:945
  148.0 0.6 copy.189
  148.8 2.3 skip_step.3.refs_10_
  151.1 1.0 multiply_convert_fusion.1
  152.1 5.7 %all-to-all-done.3 = bf16[16,88,128]{2,1,0:T(8,128)(2,1)S(1)} async-done(((bf16[16,88,128]{2,1,0:T(8,128)(2,1)}), bf16[16,88,128]{2,1,0:T(8,128)(2,1)S(1)}, u32[]{:S(2)}, u32[]{:S(2)}) %all-to-all-start.3) | async-done | bytes 360480 | tf_op jit(solution)/shard_map/all_to_all | solution.py:945
  157.8 4.7 %rim_step.9 = (bf16[96,8,128]{2,1,0:T(8,128)(2,1)S(1)}, bf16[96,16,128]{2,1,0:T(8,128)(2,1)S(1)}, bf16[176,16,128]{2,1,0:T(8,128)(2,1)}) custom-call(s32[96]{0:T(128)S(1)} %add_select_fusion.2.refs_0_.pick_ref, s32[96]{0:T(128)S(1)} %get-tuple-element.77.refs_1_.refs_0_, s32[96]{0:T(128)S(1)} %compare_select_fusion.2.slot_ref.refs_2_, ...), custom_call_target="tpu_custom_call" | custom-call | flops 301989888 | bytes 1152000 | tf_op jit(solution)/shard_map/rim_step/pallas_call | solution.py:445
  162.5 0.8 copy-done.19
  163.2 7.6 %all-to-all-start.4 = ((bf16[16,176,128]{2,1,0:T(8,128)(2,1)}), bf16[16,176,128]{2,1,0:T(8,128)(2,1)S(1)}, u32[]{:S(2)}, u32[]{:S(2)}) async-start(bf16[16,176,128]{2,1,0:T(8,128)(2,1)} %bitcast.46), calls=%async_computation.4 | async-start | bytes 1441792 | tf_op jit(solution)/shard_map/all_to_all | solution.py:945
  171.2 0.7 copy-done.32
  171.9 4.5 %fusion.4 = f32[24,12,12,128]{3,0,2,1:T(8,128)S(1)} fusion(bf16[3,3,256,128]{3,2,1,0:T(8,128)(2,1)S(1)} %copy-done.2, bf16[24,1,12,128]{3,0,2,1:T(8,128)(2,1)S(1)} %copy.159, bf16[24,10,1,128]{3,0,2,1:T(8,128)(2,1)S(1)} %bitcast.214, bf16[24,10,10,128]{3,0,2,1:T(8,128)(2,1)S(1)} %copy-done.32, bf16[24,10,1,128]{3,0,2,1:T(8,128)(2,1)S(1)} %bitcast.215, ...), kind=kOutput, calls=%fused_computation.6 | convolution fusion | flops 1828847616 | bytes 4128768 | tf_op jit(solution)/shard_map/conv_general_dilated | solution.py:915
  176.7 0.9 copy-done.30
  177.7 0.4 copy-done.4
  178.3 2.5 skip_step.4.refs_9_
  180.8 1.0 copy-done
  181.8 6.8 %all-to-all-done.4 = bf16[16,176,128]{2,1,0:T(8,128)(2,1)S(1)} async-done(((bf16[16,176,128]{2,1,0:T(8,128)(2,1)}), bf16[16,176,128]{2,1,0:T(8,128)(2,1)S(1)}, u32[]{:S(2)}, u32[]{:S(2)}) %all-to-all-start.4) | async-done | bytes 720928 | tf_op jit(solution)/shard_map/all_to_all | solution.py:945
  188.7 5.4 %rim_step.10 = (bf16[96,16,128]{2,1,0:T(8,128)(2,1)S(1)}, bf16[96,24,128]{2,1,0:T(8,128)(2,1)S(1)}, bf16[176,24,128]{2,1,0:T(8,128)(2,1)}) custom-call(s32[96]{0:T(128)S(1)} %add_select_fusion.2.refs_0_.pick_ref, s32[96]{0:T(128)S(1)} %get-tuple-element.77.refs_1_.refs_0_, s32[96]{0:T(128)S(1)} %compare_select_fusion.2.slot_ref.refs_2_, ...), custom_call_target="tpu_custom_call" | custom-call | flops 603979776 | bytes 2304000 | tf_op jit(solution)/shard_map/rim_step/pallas_call | solution.py:445
  194.1 0.8 copy-done.14
  194.9 7.5 %all-to-all-start.5 = ((bf16[16,264,128]{2,1,0:T(8,128)(2,1)}), bf16[16,264,128]{2,1,0:T(8,128)(2,1)S(1)}, u32[]{:S(2)}, u32[]{:S(2)}) async-start(bf16[16,264,128]{2,1,0:T(8,128)(2,1)} %bitcast.210), calls=%async_computation.5 | async-start | bytes 2162688 | tf_op jit(solution)/shard_map/all_to_all | solution.py:945
  202.4 1.3 copy-done.8
  203.6 5.1 %skip_step.5.refs_9_ = f32[96,48,128]{2,1,0:T(8,128)} custom-call(s32[96]{0:T(128)S(1)} %get-tuple-element.77.refs_1_.refs_0_, s32[96]{0:T(128)S(1)} %get-tuple-element.78.refs_3_.refs_1_, s32[97]{0:T(128)S(1)} %pad_add_fusion.1.refs_5_.refs_2_, bf16[96,48,128]{2,1,0:T(8,128)(2,1)S(1)} %copy-done.8, bf16[9,256,128]{2,1,0:T(8,128)(2,1)S(1)} %bitcast.166), custom_call_target="tpu_custom_call" | custom-call | flops 905969664 | bytes 3538944 | tf_op jit(solution)/shard_map/skip_step/pallas_call | solution.py:277
  208.8 0.5 fusion.3
  209.7 0.7 pad_maximum_fusion.1.refs_2_
  210.5 18.1 %dec_conv.2 = (bf16[24,12,2,24,128]{4,3,2,1,0:T(8,128)(2,1)}, f32[24,4,24,128]{3,2,1,0:T(8,128)S(1)}) custom-call(bf16[24,24,24,128]{3,2,1,0:T(8,128)(2,1)} %bitcast.219, bf16[24,4,24,128]{3,2,1,0:T(8,128)(2,1)S(1)} %bitcast.189, bf16[24,12,12,128]{3,2,1,0:T(8,128)(2,1)S(1)} %pad_maximum_fusion.1.refs_2_, bf16[9,256,128]{2,1,0:T(8,128)(2,1)S(1)} %bitcast.174), custom_call_target="tpu_custom_call" | custom-call | flops 8139571200 | bytes 8294400 | tf_op jit(solution)/shard_map/dec_conv/pallas_call | solution.py:870
  228.6 1.0 copy-done.11
  229.6 1.1 copy-done.15
  230.7 7.7 %rim_step.11 = (bf16[96,24,128]{2,1,0:T(8,128)(2,1)S(1)}, bf16[96,48,128]{2,1,0:T(8,128)(2,1)S(1)}, bf16[176,48,128]{2,1,0:T(8,128)(2,1)}) custom-call(s32[96]{0:T(128)S(1)} %add_select_fusion.2.refs_0_.pick_ref, s32[96]{0:T(128)S(1)} %get-tuple-element.77.refs_1_.refs_0_, s32[96]{0:T(128)S(1)} %compare_select_fusion.2.slot_ref.refs_2_, ...), custom_call_target="tpu_custom_call" | custom-call | flops 905969664 | bytes 3456000 | tf_op jit(solution)/shard_map/rim_step/pallas_call | solution.py:445
  238.4 1.0 copy-done.5
  239.4 0.8 copy-done.25
  240.2 11.0 %all-to-all-start.6 = ((bf16[16,528,128]{2,1,0:T(8,128)(2,1)}), bf16[16,528,128]{2,1,0:T(8,128)(2,1)S(1)}, u32[]{:S(2)}, u32[]{:S(2)}) async-start(bf16[16,528,128]{2,1,0:T(8,128)(2,1)} %bitcast.208), calls=%async_computation.6 | async-start | bytes 4325376 | tf_op jit(solution)/shard_map/all_to_all | solution.py:945
  251.2 1.3 copy-done.9
  252.5 45.6 %dec_conv.3 = (bf16[24,24,2,48,128]{4,3,2,1,0:T(8,128)(2,1)}, f32[24,4,48,128]{3,2,1,0:T(8,128)}) custom-call(bf16[24,48,48,128]{3,2,1,0:T(8,128)(2,1)} %bitcast.218, bf16[24,4,48,128]{3,2,1,0:T(8,128)(2,1)S(1)} %bitcast.182, bf16[24,24,24,128]{3,2,1,0:T(8,128)(2,1)} %bitcast.220, bf16[24,4,24,128]{3,2,1,0:T(8,128)(2,1)S(1)} %bitcast.202, ...), custom_call_target="tpu_custom_call" | custom-call | flops 32558284800 | bytes 33177600 | tf_op jit(solution)/shard_map/dec_conv/pallas_call | solution.py:870
  298.1 1.9 all-to-all-done.6
  300.1 1.3 copy-done.6
  301.3 9.2 %last_step.1 = bf16[24,48,48,128]{3,2,1,0:T(8,128)(2,1)} custom-call(s32[96]{0:T(128)S(1)} %add_select_fusion.2.refs_0_.pick_ref, bf16[176,48,128]{2,1,0:T(8,128)(2,1)S(1)} %bitcast.160, bf16[96,48,128]{2,1,0:T(8,128)(2,1)S(1)} %copy-done.6, f32[96,48,128]{2,1,0:T(8,128)} %bitcast.207, ...), custom_call_target="tpu_custom_call", output_to_operand_aliasing={{}: (4, {})} | custom-call | tf_op jit(solution)/shard_map/last_step/pallas_call | solution.py:771
  (124 shorter events, 4.8 us)
Async XLA Ops:
  8.5 1.0 copy-start.10
  9.5 6.7 %copy-start.35 = (s32[384,4,2]{0,2,1:T(2,128)S(1)}, s32[384,4,2]{0,2,1:T(2,128)}, u32[]{:S(2)}) copy-start(s32[384,4,2]{0,2,1:T(2,128)} %param.10) | copy-start | bytes 36868
  9.5 10.5 %copy-start.21 = (bf16[3,3,128,128]{3,2,1,0:T(8,128)(2,1)S(1)}, bf16[3,3,128,128]{3,2,1,0:T(8,128)(2,1)}, u32[]{:S(2)}) copy-start(bf16[3,3,128,128]{3,2,1,0:T(8,128)(2,1)} %param.11) | copy-start | bytes 884740
  9.5 55.5 %all-to-all-start = ((bf16[16,528,128]{2,1,0:T(8,128)(2,1)}), bf16[16,528,128]{2,1,0:T(8,128)(2,1)S(1)}, u32[]{:S(2)}, u32[]{:S(2)}) async-start(bf16[16,528,128]{2,1,0:T(8,128)(2,1)} %bitcast.11), calls=%async_computation | async-start | bytes 4325376 | tf_op jit(solution)/shard_map/all_to_all | solution.py:945
  54.6 1.4 copy-start.3
  56.0 1.0 copy-start.12
  65.0 1.4 copy-start.27
  74.2 1.1 copy-start.7
  75.3 5.3 %copy-start.24 = (bf16[3,3,128,128]{3,2,1,0:T(8,128)(2,1)S(1)}, bf16[3,3,128,128]{3,2,1,0:T(8,128)(2,1)}, u32[]{:S(2)}) copy-start(bf16[3,3,128,128]{3,2,1,0:T(8,128)(2,1)} %param.12) | copy-start | bytes 884740
  75.3 31.0 %all-to-all-start.1 = ((bf16[16,264,128]{2,1,0:T(8,128)(2,1)}), bf16[16,264,128]{2,1,0:T(8,128)(2,1)S(1)}, u32[]{:S(2)}, u32[]{:S(2)}) async-start(bf16[16,264,128]{2,1,0:T(8,128)(2,1)} %bitcast.17), calls=%async_computation.1 | async-start | bytes 2162688 | tf_op jit(solution)/shard_map/all_to_all | solution.py:945
  95.7 1.0 copy-start.13
  106.3 1.0 copy-start.28
  112.3 0.8 copy-start.16
  113.2 5.6 %copy-start.29 = (bf16[24,10,10,128]{3,2,1,0:T(8,128)(2,1)S(1)}, bf16[24,10,10,128]{3,2,1,0:T(8,128)(2,1)}, u32[]{:S(2)}) copy-start(bf16[24,10,10,128]{3,2,1,0:T(8,128)(2,1)} %slice.167) | copy-start | bytes 1843204
  113.2 23.1 %all-to-all-start.2 = ((bf16[16,176,128]{2,1,0:T(8,128)(2,1)}), bf16[16,176,128]{2,1,0:T(8,128)(2,1)S(1)}, u32[]{:S(2)}, u32[]{:S(2)}) async-start(bf16[16,176,128]{2,1,0:T(8,128)(2,1)} %bitcast.23), calls=%async_computation.2 | async-start | bytes 1441792 | tf_op jit(solution)/shard_map/all_to_all | solution.py:945
  118.5 1.0 copy-start.22
  141.7 0.8 copy-start.33
  142.5 15.3 %all-to-all-start.3 = ((bf16[16,88,128]{2,1,0:T(8,128)(2,1)}), bf16[16,88,128]{2,1,0:T(8,128)(2,1)S(1)}, u32[]{:S(2)}, u32[]{:S(2)}) async-start(bf16[16,88,128]{2,1,0:T(8,128)(2,1)} %bitcast.35), calls=%async_computation.3 | async-start | bytes 720896 | tf_op jit(solution)/shard_map/all_to_all | solution.py:945
  147.7 1.1 copy-start.2
  147.9 9.9 %copy-start.23 = (bf16[3,3,128,128]{3,2,1,0:T(8,128)(2,1)S(1)}, bf16[3,3,128,128]{3,2,1,0:T(8,128)(2,1)}, u32[]{:S(2)}) copy-start(bf16[3,3,128,128]{3,2,1,0:T(8,128)(2,1)} %param.14) | copy-start | bytes 884740
  162.5 0.8 copy-start.19
  163.2 25.4 %all-to-all-start.4 = ((bf16[16,176,128]{2,1,0:T(8,128)(2,1)}), bf16[16,176,128]{2,1,0:T(8,128)(2,1)S(1)}, u32[]{:S(2)}, u32[]{:S(2)}) async-start(bf16[16,176,128]{2,1,0:T(8,128)(2,1)} %bitcast.46), calls=%async_computation.4 | async-start | bytes 1441792 | tf_op jit(solution)/shard_map/all_to_all | solution.py:945
  170.8 1.1 copy-start.32
  170.8 1.1 copy-start.34
  176.4 1.2 copy-start.30
  176.5 1.5 copy-start.4
  176.6 1.8 copy-start.17
  177.6 11.0 %copy-start.20 = (bf16[96,16,128]{2,1,0:T(8,128)(2,1)S(1)}, bf16[96,16,128]{2,1,0:T(8,128)(2,1)}, u32[]{:S(2)}) copy-start(bf16[96,16,128]{2,1,0:T(8,128)(2,1)} %copy-done.19) | copy-start | bytes 1179652
  180.8 1.0 copy-start
  194.1 0.8 copy-start.14
  194.9 7.5 %copy-start.1 = (bf16[3,3,256,128]{3,2,1,0:T(8,128)(2,1)S(1)}, bf16[3,3,256,128]{3,2,1,0:T(8,128)(2,1)}, u32[]{:S(2)}) copy-start(bf16[3,3,256,128]{3,2,1,0:T(8,128)(2,1)} %param.17) | copy-start | bytes 1769476
  194.9 34.7 %all-to-all-start.5 = ((bf16[16,264,128]{2,1,0:T(8,128)(2,1)}), bf16[16,264,128]{2,1,0:T(8,128)(2,1)S(1)}, u32[]{:S(2)}, u32[]{:S(2)}) async-start(bf16[16,264,128]{2,1,0:T(8,128)(2,1)} %bitcast.210), calls=%async_computation.5 | async-start | bytes 2162688 | tf_op jit(solution)/shard_map/all_to_all | solution.py:945
  202.4 1.3 copy-start.8
  203.6 5.1 %copy-start.31 = (f32[24,12,12,128]{3,0,2,1:T(8,128)S(1)}, f32[24,12,12,128]{3,0,2,1:T(8,128)}, u32[]{:S(2)}) copy-start(f32[24,12,12,128]{3,0,2,1:T(8,128)} %copy-done.30) | copy-start | bytes 5308420
  209.4 1.1 copy-start.18
  228.6 1.0 copy-start.11
  229.6 1.1 copy-start.15
  238.4 1.0 copy-start.5
  239.4 0.8 copy-start.25
  240.2 11.0 %copy-start.26 = (bf16[96,24,128]{2,1,0:T(8,128)(2,1)S(1)}, bf16[96,24,128]{2,1,0:T(8,128)(2,1)}, u32[]{:S(2)}) copy-start(bf16[96,24,128]{2,1,0:T(8,128)(2,1)} %copy-done.25) | copy-start | bytes 1769476
  240.2 59.8 %all-to-all-start.6 = ((bf16[16,528,128]{2,1,0:T(8,128)(2,1)}), bf16[16,528,128]{2,1,0:T(8,128)(2,1)S(1)}, u32[]{:S(2)}, u32[]{:S(2)}) async-start(bf16[16,528,128]{2,1,0:T(8,128)(2,1)} %bitcast.208), calls=%async_computation.6 | async-start | bytes 4325376 | tf_op jit(solution)/shard_map/all_to_all | solution.py:945
  251.2 1.3 copy-start.9
  300.1 1.3 copy-start.6

commit v2 on v0

--- a/solution.py
+++ b/solution.py
@@ -83,7 +83,9 @@
     rank = jnp.sum((mask[None, :] & (order[None, :] < order[:, None])).astype(jnp.int32), axis=1)
     hit = mask[None, :] & (rank[None, :] == order[:, None])
     found = jnp.sum(jnp.where(hit, order[None, :], 0), axis=1)
-    return jnp.concatenate([found, jnp.sum(mask.astype(jnp.int32), keepdims=True)])
+    total = jnp.sum(mask.astype(jnp.int32), keepdims=True)
+    found = jnp.where(order < total, found, mask.shape[0])
+    return jnp.concatenate([found, jnp.full((3,), mask.shape[0], jnp.int32), total])
 
 
 def receive_plan(edge_table, slot_row, position, tiles_here, slot_count, devices):
@@ -92,17 +94,18 @@
     target = partner // tiles_here
     order = jnp.arange(strip_count, dtype=jnp.int32)
     remote = target != position
-    source_tiles = target[:, None] * tiles_here + jnp.arange(tiles_here, dtype=jnp.int32)[None, :]
-    their_partners = jnp.take(edge_table[:, :, 0], source_tiles, axis=0).reshape(
-        strip_count, strip_count
-    )
-    toward_me = their_partners // tiles_here == position
     wanted = partner % tiles_here * 4 + matching
-    before_wanted = order[None, :] < wanted[:, None]
-    recv_rank = jnp.sum((toward_me & before_wanted).astype(jnp.int32), axis=1)
+    toward_me = edge_table[:, :, 0].reshape(devices, strip_count) // tiles_here == position
+    before = (order[:, None] < order[None, :]).astype(BF)
+    ranks = jnp.dot(toward_me.astype(BF), before, preferred_element_type=F32).astype(BF)
+    blocks = jnp.arange(devices, dtype=jnp.int32)
+    from_target = (target[:, None] == blocks[None, :]).astype(BF)
+    their_ranks = jnp.dot(from_target, ranks, preferred_element_type=F32)
+    recv_rank = jnp.sum(jnp.where(wanted[:, None] == order[None, :], their_ranks, 0.0), axis=1).astype(jnp.int32)
     pick_row = jnp.where(remote, target * slot_count + recv_rank, devices * slot_count + wanted)
     odd = (matching != (order + 2) % 4) | (reversed_rows == 1)
-    return (pick_row, reversed_rows, slot_row, matching, listed(remote), listed(odd))
+    one_more = lambda a: jnp.concatenate([a, jnp.zeros((1,), jnp.int32)])
+    return (pick_row, one_more(reversed_rows), slot_row, one_more(matching), listed(remote), listed(odd))
 
 
 def up16(n):
@@ -164,7 +167,8 @@
 
 
 def silu(s):
-    return s / (1.0 + jnp.exp(-s))
+    half = s * 0.5
+    return half + half * jnp.tanh(half)
 
 
 def strip_shifts(h, n):
@@ -176,10 +180,10 @@
     return down, up
 
 
-def flip_matrix(rows, n):
+def flip_matrices(rows, n):
     ri = lax.broadcasted_iota(jnp.int32, (rows, rows), 0)
     ci = lax.broadcasted_iota(jnp.int32, (rows, rows), 1)
-    return (ri + ci == n - 1).astype(F32).astype(BF)
+    return (ri + ci == n - 1).astype(F32), (ri == ci).astype(F32)
 
 
 def put_shifts(ref, index, lane, h, n):
@@ -205,6 +209,19 @@
         return carry
 
     lax.fori_loop(0, list_ref[list_ref.shape[0] - 1], step, 0)
+
+
+def each_four(list_ref, body):
+    def step(j, carry):
+        body([list_ref[j * 4 + k] for k in range(4)])
+        return carry
+
+    lax.fori_loop(0, (list_ref[list_ref.shape[0] - 1] + 3) // 4, step, 0)
+
+
+def turned(rev_ref, i, h, flip, keep):
+    order = jnp.where(rev_ref[i] == 1, flip, keep).astype(BF)
+    return jnp.dot(order, h.astype(BF), preferred_element_type=F32)
 
 
 def incoming(pick_ref, recv_ref, own_ref, i):
@@ -220,7 +237,7 @@
     return jnp.concatenate([w_ref[tap, lo : lo + 128, :] for tap in taps], axis=0)
 
 
-def contributions(n, tiles, strip_of, w_ref, lo, rev_ref, edge_ref, odd_ref, lhs_ref, con_ref, taps_ref, buf):
+def contributions(n, tiles, strip_of, w_ref, lo, rev_ref, edge_ref, odd_ref, lhs_ref, con_ref, taps_ref):
     lp = lhs_ref.shape[2]
     for e in range(4):
         taps_ref[e] = edge_taps(w_ref, e, lo)
@@ -231,30 +248,31 @@
 
     each_tile(tiles, fill)
     for f in range(4):
-        lhs = lhs_ref[f].reshape(tiles * lp, 384).astype(BF)
+        lhs = lhs_ref[f, 0:tiles].reshape(tiles * lp, 384).astype(BF)
         out = jnp.dot(lhs, taps_ref[(f + 2) % 4], preferred_element_type=F32)
-        con_ref[f] = out.reshape(tiles, lp, 128)
-    flip = flip_matrix(lp, n)
-
-    def odd_one(i):
-        f, t = i % 4, i // 4
-        buf[...] = lhs_ref[f, t, :, 128:256].astype(F32)
-
-        @pl.when(rev_ref[i] == 1)
-        def _():
-            buf[...] = jnp.dot(flip, buf[...].astype(BF), preferred_element_type=F32)
-
-        put_shifts(lhs_ref, (f, t), 0, buf[...], n)
-        con_ref[f, t] = jnp.dot(lhs_ref[f, t].astype(BF), taps_ref[edge_ref[i]], preferred_element_type=F32)
-
-    each_listed(odd_ref, odd_one)
-
-
-def skip_kernel(n, rev_ref, edge_ref, odd_ref, rim_ref, w_ref, out_ref, lhs_ref, con_ref, taps_ref, buf):
+        con_ref[f, 0:tiles] = out.reshape(tiles, lp, 128)
+    flip, keep = flip_matrices(lp, n)
+
+    def odd_ones(four):
+        halos = [lhs_ref[i % 4, i // 4, :, 128:256] for i in four]
+        halos = [turned(rev_ref, i, h, flip, keep) for i, h in zip(four, halos)]
+        taps = [taps_ref[edge_ref[i]] for i in four]
+        sums = []
+        for h, tap in zip(halos, taps):
+            down, up = strip_shifts(h, n)
+            lhs = jnp.concatenate([down.astype(BF), h.astype(BF), up.astype(BF)], axis=1)
+            sums.append(jnp.dot(lhs, tap, preferred_element_type=F32))
+        for i, total in zip(four, sums):
+            con_ref[i % 4, i // 4] = total
+
+    each_four(odd_ref, odd_ones)
+
+
+def skip_kernel(n, rev_ref, edge_ref, odd_ref, rim_ref, w_ref, out_ref, lhs_ref, con_ref, taps_ref):
     tiles = rim_ref.shape[0] // 4
     contributions(
         n, tiles, lambda f, t, k: rim_ref[t * 4 + f].astype(F32), w_ref, 128,
-        rev_ref, edge_ref, odd_ref, lhs_ref, con_ref, taps_ref, buf,
+        rev_ref, edge_ref, odd_ref, lhs_ref, con_ref, taps_ref,
     )
 
     def put(t, k):
@@ -278,10 +296,9 @@
         out_specs=vmem,
         out_shape=jax.ShapeDtypeStruct((strips, lp, c), F32),
         scratch_shapes=[
-            pltpu.VMEM((4, strips // 4, lp, 384), wide(lp)),
-            pltpu.VMEM((4, strips // 4, lp, 128), F32),
+            pltpu.VMEM((4, strips // 4 + 1, lp, 384), wide(lp)),
+            pltpu.VMEM((4, strips // 4 + 1, lp, 128), F32),
             pltpu.VMEM((4, 384, 128), BF),
-            pltpu.VMEM((lp, 128), F32),
         ],
         compiler_params=params(),
         cost_estimate=pl.CostEstimate(flops=strips * lp * 2 * 384 * 256, bytes_accessed=strips * lp * 768, transcendentals=0),
@@ -311,7 +328,7 @@
     lp = recv_ref.shape[1]
     strips = own_ref.shape[0]
     tiles = strips // 4
-    flip = flip_matrix(lp, n)
+    flip, keep = flip_matrices(lp, n)
 
     if strips_in:
 
@@ -322,12 +339,12 @@
 
         each_tile(tiles, fetch)
 
-        def turn(i):
-            @pl.when(rev_ref[i] == 1)
-            def _():
-                halo_ref[i] = jnp.dot(flip, halo_ref[i], preferred_element_type=F32).astype(BF)
-
-        each_listed(odd_ref, turn)
+        def turn(four):
+            halos = [turned(rev_ref, i, halo_ref[i], flip, keep).astype(BF) for i in four]
+            for i, h in zip(four, halos):
+                halo_ref[i] = h
+
+        each_four(odd_ref, turn)
 
         def fill(t, k):
             for e in range(4):
@@ -388,7 +405,7 @@
 
         contributions(
             2 * n, tiles, enlarged, wn_ref, 0,
-            rev_ref, edge_ref, odd_ref, lhsn_ref, conn_ref, taps_ref, big_buf.at[0, 0],
+            rev_ref, edge_ref, odd_ref, lhsn_ref, conn_ref, taps_ref,
         )
 
         def put(t, k):
@@ -421,7 +438,7 @@
         jax.ShapeDtypeStruct((rows, lo, c), BF),
     ]
     scratch = [
-        pltpu.VMEM((strips, lp, 128), BF),
+        pltpu.VMEM((strips + 1, lp, 128), BF),
         pltpu.VMEM((4, tiles, lp, 384), wide(lp)),
         pltpu.VMEM((4, tiles, lp, 128), F32),
         pltpu.VMEM((side, 4, lp, 128), F32),
@@ -431,8 +448,8 @@
     ]
     if nxt == "halo":
         scratch += [
-            pltpu.VMEM((4, tiles, lo, 384), wide(lo)),
-            pltpu.VMEM((4, tiles, lo, 128), F32),
+            pltpu.VMEM((4, tiles + 1, lo, 384), wide(lo)),
+            pltpu.VMEM((4, tiles + 1, lo, 128), F32),
             pltpu.VMEM((4, 384, 128), BF),
             pltpu.VMEM((side, 4, lo, 128), F32),
         ]
@@ -466,9 +483,11 @@
 
 
 def column_shifts(x, n):
-    col = lax.broadcasted_iota(jnp.int32, x.shape, 1)
-    down = jnp.where(col == 0, 0.0, pltpu.roll(x, 1, 1))
-    up = jnp.where(col == n - 1, 0.0, pltpu.roll(x, n - 1, 1))
+    sub = lax.broadcasted_iota(jnp.int32, (x.shape[0], 8, 128), 1)
+    down = pltpu.roll(x, 1, 1)
+    up = pltpu.roll(x, n - 1, 1)
+    down = jnp.concatenate([jnp.where(sub == 0, 0.0, down[:, 0:8]), down[:, 8:n]], axis=1)
+    up = jnp.concatenate([up[:, 0 : n - 8], jnp.where(sub == 7, 0.0, up[:, n - 8 : n])], axis=1)
     return down, x, up
 
 
@@ -483,6 +502,31 @@
         y_ref[1 : half + 1, 0:n, s * 128 : s * 128 + 128] = b[:, 1]
 
 
+def in_pairs(n):
+    return n % 16 == 8 and n % 2 == 0
+
+
+def fill_row_pairs(u_ref, x, n):
+    half = n // 2
+    zero = jnp.zeros((n, 384), BF)
+    u_ref[0, 0:n] = zero
+    u_ref[half, n : 2 * n] = zero
+    for s, body in enumerate(column_shifts(x, n)):
+        b = body.astype(BF).reshape(half, 2, n, 128)
+        lanes = slice(s * 128, s * 128 + 128)
+        u_ref[0:half, n : 2 * n, lanes] = b[:, 0]
+        u_ref[1 : half + 1, 0:n, lanes] = b[:, 1]
+        u_ref[half + 1 : n + 1, 0:n, lanes] = b[:, 0]
+        u_ref[half + 1 : n + 1, n : 2 * n, lanes] = b[:, 1]
+
+
+def coarse_lhs(u_ref, n, start, m, lanes):
+    if in_pairs(n):
+        at = start // 2 if start % 2 == 0 else n // 2 + 1 + start // 2
+        return u_ref[at : at + m // 2, :, lanes].reshape(m * n, 256), n
+    return u_ref[start : start + m, :, lanes].reshape(m * u_ref.shape[1], 256), u_ref.shape[1]
+
+
 def fill_rows(u_ref, x, n):
     zero = jnp.zeros((u_ref.shape[1], 384), BF)
     u_ref[0] = zero
@@ -501,10 +545,14 @@
     return acc if extra is None else acc + extra
 
 
-def pair_chunks(n):
+def pair_chunks(n, most):
     half = n // 2
-    m = 6 if half % 6 == 0 else half
+    m = max(m for m in range(1, most + 1) if half % m == 0)
     return [(q, m) for q in range(0, half, m)]
+
+
+ENC_PAIRS = {48: 24}
+DEC_PAIRS = {48: 12}
 
 
 def column_of(acc, m, lo, sublane, colbuf):
@@ -565,7 +613,7 @@
         if rim_ref is not None:
             x = with_rims(x, [rim_ref[g, e].astype(F32) for e in range(4)], n, colbuf)
         fill_pairs(pairs, x, n)
-        for q0, m in pair_chunks(n):
+        for q0, m in pair_chunks(n, ENC_PAIRS.get(n, 6)):
             acc = pair_sums(pairs, w_ref, q0, m, None)
             put_sums(acc, sums_ref, g, q0, m, n, colbuf)
             out = silu(acc).astype(BF)[:, 0:n]
@@ -586,32 +634,32 @@
         ring_ref[g, 3] = ringbuf[0].astype(BF)
 
 
-def dec_kernel(x_ref, rim_ref, u_ref, *refs):
+def dec_kernel(coarse_rims, *refs):
     refs = list(refs)
-    urim_ref = refs.pop(0) if len(refs) == 10 else None
-    raw_ref, y_ref, sums_ref, pairs, rows, colbuf, acc_ref, w_ref, wu_ref = refs
+    x_ref, rim_ref, u_ref = refs.pop(0), refs.pop(0), refs.pop(0)
+    urim_ref = refs.pop(0) if coarse_rims else None
+    raw_ref = refs.pop(0)
+    y_ref, sums_ref, pairs, rows, colbuf, acc_ref, w_ref, wu_ref = refs
+    group, n = y_ref.shape[0], y_ref.shape[3]
+    half = n // 2
 
     @pl.when(pl.program_id(0) == 0)
     def _():
         fill_pair_weights(raw_ref, 128, w_ref)
         fill_coarse_weights(raw_ref, wu_ref)
 
-    group, n = x_ref.shape[0], x_ref.shape[1]
-    half = n // 2
-    hp = rows.shape[1]
-
     for g in range(group):
         u = u_ref[g].astype(F32)
         if urim_ref is not None:
             u = with_rims(u, [urim_ref[g, e].astype(F32) for e in range(4)], half, colbuf.at[0 : half * 8])
-        fill_rows(rows, u, half)
+        (fill_row_pairs if in_pairs(half) else fill_rows)(rows, u, half)
         x = with_rims(x_ref[g].astype(F32), [rim_ref[g, e].astype(F32) for e in range(4)], n, colbuf)
         fill_pairs(pairs, x, n)
-        for q0, m in pair_chunks(n):
+        for q0, m in pair_chunks(n, DEC_PAIRS.get(n, 6)):
             for b in range(2):
                 acc = None
                 for k in range(3):
-                    lhs = rows[q0 + k : q0 + k + m, :, b * 128 : b * 128 + 256].reshape(m * hp, 256)
+                    lhs, hp = coarse_lhs(rows, half, q0 + k, m, slice(b * 128, b * 128 + 256))
                     part = jnp.dot(lhs, wu_ref[b, k], preferred_element_type=F32)
                     acc = part if acc is None else acc + part
                 acc = acc.reshape(m, hp, 256)
@@ -745,7 +793,7 @@
     tiles, n, _, c = x.shape
     half, n_p = n // 2, up16(n)
     g = group_of(tiles, want)
-    m = pair_chunks(n)[0][1]
+    m = pair_chunks(n, ENC_PAIRS.get(n, 6))[0][1]
     args, specs = [x, w.reshape(9, c, c)], [tile_spec(g, n, n, c), whole_spec((9, c, c))]
     if rim is not None:
         args.append(rim.reshape(tiles, 4, n, c))
@@ -782,18 +830,25 @@
 
 def dec_conv(x, rim, u, urim, w, want):
     tiles, n, _, c = x.shape
-    half, n_p, h_p = n // 2, up16(n), up16(n // 2)
+    half, n_p = n // 2, up16(n)
     g = group_of(tiles, want)
-    m = pair_chunks(n)[0][1]
+    m = pair_chunks(n, DEC_PAIRS.get(n, 6))[0][1]
     args = [x, rim.reshape(tiles, 4, n, c), u]
     specs = [tile_spec(g, n, n, c), tile_spec(g, 4, n, c), tile_spec(g, half, half, c)]
     if urim is not None:
         args.append(urim.reshape(tiles, 4, half, c))
         specs.append(tile_spec(g, 4, half, c))
+    args.append(w.reshape(9, 2 * c, c))
+    specs.append(whole_spec((9, 2 * c, c)))
+    rows = (half + 1, 2 * half, 384) if in_pairs(half) else (half + 2, up16(half), 384)
+
+    def kernel(*refs):
+        dec_kernel(urim is not None, *refs)
+
     y, sums = pl.pallas_call(
-        dec_kernel,
+        kernel,
         grid=(tiles // g,),
-        in_specs=specs + [whole_spec((9, 2 * c, c))],
+        in_specs=specs,
         out_specs=[tile_spec(g, half, 2, n, c), tile_spec(g, 4, n, c)],
         out_shape=[
             jax.ShapeDtypeStruct((tiles, half, 2, n, c), BF),
@@ -801,7 +856,7 @@
         ],
         scratch_shapes=[
             pltpu.VMEM((half + 1, n_p, 768), BF),
-            pltpu.VMEM((half + 2, h_p, 384), BF),
+            pltpu.VMEM(rows, BF),
             pltpu.VMEM((n * 8, 128), F32),
             pltpu.VMEM((2, m, n_p, 128), F32),
             pltpu.VMEM((1536, 256), BF),
@@ -812,8 +867,8 @@
             flops=tiles * n * n * 2 * 2300 * 128, bytes_accessed=tiles * n * n * 600, transcendentals=tiles * n * n * 128
         ),
         name="dec_conv",
-    )(*args, w.reshape(9, 2 * c, c))
-    return y.reshape(tiles, n, n, c), sums.reshape(tiles * 4, n, c)
+    )(*args)
+    return y.reshape(x.shape), sums.reshape(tiles * 4, n, c)
 
 
 def strips_of(field, ring=0):
@@ -895,6 +950,7 @@
     middle = jax.nn.silu(sums).astype(BF)
     skip2 = skip_step(n0 // 4, plan, enc2_rim, w_dec2)
     skip0 = skip_step(n0, plan, after(enc0_rim, x3_rim), w_dec0)
+    sums, skip0 = lax.optimization_barrier((sums, skip0))
     mid_rim, own, send = rim_step(
         n0 // 8, plan, recv, x3_rim, strips_of(sums), w=w_mid,
         skip=skip2, wn=w_dec2,

time: 317 us -> 309 us (0.975)
  Pallas kernels: 191 us -> 178 us
  waiting for transfers between devices: 30.5 us -> 41.7 us
    all_to_all x7, waiting for transfers between devices: 30.5 us -> 41.7 us  [trade(): lax.all_to_all(strips.reshape(devices, cap * length, 128), 'tile', split_...]
    gather x2 -> x0, local copies, waits for them, and re-layouts: 6.75 us -> none  [receive_plan(): jnp.take(edge_table[:, :, 0], source_tiles, axis=0)]
    pallas_call x2, Pallas kernels: 66.9 us -> 60.4 us  [dec_conv(): pl.pallas_call(kernel, grid=(tiles // g,), in_specs=specs, out_specs=[til...]
    pallas_call x2, Pallas kernels: 55.4 us -> 49.6 us  [enc_conv(): pl.pallas_call(enc_kernel, grid=(tiles // g,), in_specs=specs, out_specs=...]
    unnamed x86 -> x106, local copies, waits for them, and re-layouts: 22.5 us -> 26.6 us
  transfers between devices with their start and end apart: 7 -> 7, of which waited for: 4 -> 6; matrix products, arithmetic and copies ran while one was open for 8% -> 8% of each run, Pallas kernels for 44% -> 40%
where the time goes in v2:
time: 309 us; the launch traced here: 307 us
  Pallas kernels  178 us (58%)
  waiting for transfers between devices  41.7 us (13%)
  starting transfers between devices  37.3 us (12%)
  local copies, waits for them, and re-layouts  33.3 us (11%)
  matrix products  8.2 us (3%)
  other arithmetic  7.42 us (2%)
    pallas_call x2, Pallas kernels, dec_conv(): pl.pallas_call(kernel, grid=(tiles // g,), in_specs=specs, out_specs=[til...  60.4 us
    pallas_call x2, Pallas kernels, enc_conv(): pl.pallas_call(enc_kernel, grid=(tiles // g,), in_specs=specs, out_specs=...  49.6 us
    all_to_all x7, waiting for transfers between devices, trade(): lax.all_to_all(strips.reshape(devices, cap * length, 128), 'tile', split_...  41.7 us
    pallas_call x6, Pallas kernels, rim_step(): pl.pallas_call(kernel, in_specs=[smem] * 6 + [vmem] * len(args), out_spec...  38.8 us
    all_to_all x7, starting transfers between devices, trade(): lax.all_to_all(strips.reshape(devices, cap * length, 128), 'tile', split_...  37.3 us
    unnamed x106, local copies, waits for them, and re-layouts  26.6 us
    pallas_call x3, Pallas kernels, skip_step(): pl.pallas_call(lambda *refs: skip_kernel(n, *refs), in_specs=[smem, smem,...  12.5 us
    pallas_call x1, Pallas kernels, last_step(): pl.pallas_call(last_kernel, in_specs=[smem, vmem, vmem, vmem, anywhere],...  9.16 us
  transfers between devices with their start and end apart: 7, of which 6 were waited for; matrix products, arithmetic and copies ran while one was open for 8% of the time, Pallas kernels for 40%

profile of v2, /device:TPU:15, one launch (start us, length us, event | category | flops | bytes accessed | tf_op | source)
XLA Modules:
  0.0 306.8 jit_solution(4313436876786254843)
XLA Ops:
  0.0 0.8 constant_dynamic-slice_fusion.1
  1.2 7.3 %tile_rims.1 = (bf16[24,4,48,128]{3,2,1,0:T(8,128)(2,1)S(1)}, bf16[176,48,128]{2,1,0:T(8,128)(2,1)}) custom-call(s32[96]{0:T(128)S(1)} %compare_select_fusion.4.slot_ref.refs_2_, bf16[24,48,48,128]{3,2,1,0:T(8,128)(2,1)} %refs_0_.1, bf16[24,48,48,128]{3,2,1,0:T(8,128)(2,1)} %refs_0_.1, bf16[24,48,48,128]{3,2,1,0:T(8,128)(2,1)} %refs_0_.1, ...), custom_call_target="tpu_custom_call" | custom-call | tf_op jit(solution)/shard_map/tile_rims/pallas_call | solution.py:148
  8.5 1.0 copy-done.10
  9.5 6.7 %all-to-all-start = ((bf16[16,528,128]{2,1,0:T(8,128)(2,1)}), bf16[16,528,128]{2,1,0:T(8,128)(2,1)S(1)}, u32[]{:S(2)}, u32[]{:S(2)}) async-start(bf16[16,528,128]{2,1,0:T(8,128)(2,1)} %bitcast.11), calls=%async_computation | async-start | bytes 4325376 | tf_op jit(solution)/shard_map/all_to_all | solution.py:922
  17.1 0.6 convert_reduce_fusion.4
  18.2 0.7 compare_select_fusion.2
  19.4 1.3 fusion.46
  21.1 34.6 %enc_conv.2 = (bf16[24,24,2,48,128]{4,3,2,1,0:T(8,128)(2,1)}, f32[24,4,48,128]{3,2,1,0:T(8,128)S(1)}, bf16[24,4,48,128]{3,2,1,0:T(8,128)(2,1)S(1)}, bf16[24,24,24,128]{3,2,1,0:T(8,128)(2,1)}) custom-call(bf16[24,48,48,128]{3,2,1,0:T(8,128)(2,1)} %refs_0_.1, bf16[9,128,128]{2,1,0:T(8,128)(2,1)S(1)} %bitcast.194), custom_call_target="tpu_custom_call" | custom-call | flops 21743271936 | bytes 33177600 | tf_op jit(solution)/shard_map/enc_conv/pallas_call | solution.py:801
  55.7 1.4 copy-done.3
  57.1 1.0 copy-done.12
  58.1 6.9 %all-to-all-done = bf16[16,528,128]{2,1,0:T(8,128)(2,1)S(1)} async-done(((bf16[16,528,128]{2,1,0:T(8,128)(2,1)}), bf16[16,528,128]{2,1,0:T(8,128)(2,1)S(1)}, u32[]{:S(2)}, u32[]{:S(2)}) %all-to-all-start) | async-done | bytes 2162720 | tf_op jit(solution)/shard_map/all_to_all | solution.py:922
  65.0 1.4 copy-done.33
  66.4 8.8 %rim_step.6 = (bf16[96,48,128]{2,1,0:T(8,128)(2,1)S(1)}, bf16[96,24,128]{2,1,0:T(8,128)(2,1)S(1)}, bf16[176,24,128]{2,1,0:T(8,128)(2,1)}) custom-call(s32[96]{0:T(128)S(1)} %add_select_fusion.2.refs_0_.pick_ref, s32[97]{0:T(128)S(1)} %get-tuple-element.134.refs_1_.refs_0_, s32[96]{0:T(128)S(1)} %compare_select_fusion.4.slot_ref.refs_2_, ...), custom_call_target="tpu_custom_call" | custom-call | flops 1811939328 | bytes 6912000 | tf_op jit(solution)/shard_map/rim_step/pallas_call | solution.py:460
  75.2 1.1 copy-done.7
  76.3 5.0 %all-to-all-start.1 = ((bf16[16,264,128]{2,1,0:T(8,128)(2,1)}), bf16[16,264,128]{2,1,0:T(8,128)(2,1)S(1)}, u32[]{:S(2)}, u32[]{:S(2)}) async-start(bf16[16,264,128]{2,1,0:T(8,128)(2,1)} %bitcast.17), calls=%async_computation.1 | async-start | bytes 2162688 | tf_op jit(solution)/shard_map/all_to_all | solution.py:922
  81.3 15.1 %enc_conv.3 = (bf16[24,12,2,24,128]{4,3,2,1,0:T(8,128)(2,1)}, f32[24,4,24,128]{3,2,1,0:T(8,128)S(1)}, bf16[24,4,24,128]{3,2,1,0:T(8,128)(2,1)S(1)}, bf16[24,12,12,128]{3,2,1,0:T(8,128)(2,1)S(1)}) custom-call(bf16[24,24,24,128]{3,2,1,0:T(8,128)(2,1)} %get-tuple-element.49.refs_0_, bf16[9,128,128]{2,1,0:T(8,128)(2,1)S(1)} %bitcast.198, ...), custom_call_target="tpu_custom_call" | custom-call | flops 5435817984 | bytes 8294400 | tf_op jit(solution)/shard_map/enc_conv/pallas_call | solution.py:801
  96.3 1.0 copy-done.13
  97.3 1.4 slice.167
  98.7 8.2 %all-to-all-done.1 = bf16[16,264,128]{2,1,0:T(8,128)(2,1)S(1)} async-done(((bf16[16,264,128]{2,1,0:T(8,128)(2,1)}), bf16[16,264,128]{2,1,0:T(8,128)(2,1)S(1)}, u32[]{:S(2)}, u32[]{:S(2)}) %all-to-all-start.1) | async-done | bytes 1081376 | tf_op jit(solution)/shard_map/all_to_all | solution.py:922
  106.9 1.0 copy-done.34
  107.9 5.8 %rim_step.7 = (bf16[96,24,128]{2,1,0:T(8,128)(2,1)S(1)}, bf16[96,16,128]{2,1,0:T(8,128)(2,1)S(1)}, bf16[176,16,128]{2,1,0:T(8,128)(2,1)}) custom-call(s32[96]{0:T(128)S(1)} %add_select_fusion.2.refs_0_.pick_ref, s32[97]{0:T(128)S(1)} %get-tuple-element.134.refs_1_.refs_0_, s32[96]{0:T(128)S(1)} %compare_select_fusion.4.slot_ref.refs_2_, ...), custom_call_target="tpu_custom_call" | custom-call | flops 905969664 | bytes 3456000 | tf_op jit(solution)/shard_map/rim_step/pallas_call | solution.py:460
  113.7 0.9 copy-done.17
  114.7 4.9 %all-to-all-start.2 = ((bf16[16,176,128]{2,1,0:T(8,128)(2,1)}), bf16[16,176,128]{2,1,0:T(8,128)(2,1)S(1)}, u32[]{:S(2)}, u32[]{:S(2)}) async-start(bf16[16,176,128]{2,1,0:T(8,128)(2,1)} %bitcast.23), calls=%async_computation.2 | async-start | bytes 1441792 | tf_op jit(solution)/shard_map/all_to_all | solution.py:922
  119.9 0.7 pad_maximum_fusion
  120.6 2.6 multiply_convert_fusion
  123.2 0.9 slice.232
  124.8 0.6 fusion.29
  125.4 12.0 %all-to-all-done.2 = bf16[16,176,128]{2,1,0:T(8,128)(2,1)S(1)} async-done(((bf16[16,176,128]{2,1,0:T(8,128)(2,1)}), bf16[16,176,128]{2,1,0:T(8,128)(2,1)S(1)}, u32[]{:S(2)}, u32[]{:S(2)}) %all-to-all-start.2) | async-done | bytes 720928 | tf_op jit(solution)/shard_map/all_to_all | solution.py:922
  137.5 1.0 copy-done.27
  138.4 3.5 %rim_step.8 = (bf16[96,16,128]{2,1,0:T(8,128)(2,1)S(1)}, bf16[96,8,128]{2,1,0:T(8,128)(2,1)S(1)}, bf16[176,8,128]{2,1,0:T(8,128)(2,1)S(1)}) custom-call(s32[96]{0:T(128)S(1)} %add_select_fusion.2.refs_0_.pick_ref, s32[97]{0:T(128)S(1)} %get-tuple-element.134.refs_1_.refs_0_, s32[96]{0:T(128)S(1)} %compare_select_fusion.4.slot_ref.refs_2_, ...), custom_call_target="tpu_custom_call" | custom-call | flops 603979776 | bytes 2304000 | tf_op jit(solution)/shard_map/rim_step/pallas_call | solution.py:460
  142.7 4.9 %all-to-all-start.3 = ((bf16[16,88,128]{2,1,0:T(8,128)(2,1)}), bf16[16,88,128]{2,1,0:T(8,128)(2,1)S(1)}, u32[]{:S(2)}, u32[]{:S(2)}) async-start(bf16[16,88,128]{2,1,0:T(8,128)(2,1)} %bitcast.193), calls=%async_computation.3 | async-start | bytes 720896 | tf_op jit(solution)/shard_map/all_to_all | solution.py:922
  147.7 6.0 %skip_step.3.refs_9_ = f32[96,48,128]{2,1,0:T(8,128)} custom-call(s32[97]{0:T(128)S(1)} %get-tuple-element.134.refs_1_.refs_0_, s32[97]{0:T(128)S(1)} %get-tuple-element.133.refs_3_.refs_1_, s32[100]{0:T(128)S(1)} %get-tuple-element.127.refs_5_.refs_2_, bf16[96,48,128]{2,1,0:T(8,128)(2,1)S(1)} %copy-done.8, bf16[9,256,128]{2,1,0:T(8,128)(2,1)S(1)} %bitcast.164), custom_call_target="tpu_custom_call" | custom-call | flops 905969664 | bytes 3538944 | tf_op jit(solution)/shard_map/skip_step/pallas_call | solution.py:293
  153.7 0.7 fusion.19
  157.2 3.2 %skip_step.4.refs_10_ = f32[96,16,128]{2,1,0:T(8,128)S(1)} custom-call(s32[97]{0:T(128)S(1)} %get-tuple-element.134.refs_1_.refs_0_, s32[97]{0:T(128)S(1)} %get-tuple-element.133.refs_3_.refs_1_, s32[100]{0:T(128)S(1)} %get-tuple-element.127.refs_5_.refs_2_, bf16[96,16,128]{2,1,0:T(8,128)(2,1)S(1)} %get-tuple-element.60.refs_3_, ...), custom_call_target="tpu_custom_call" | custom-call | flops 301989888 | bytes 1179648 | tf_op jit(solution)/shard_map/skip_step/pallas_call | solution.py:293
  160.4 0.7 multiply_convert_fusion.1
  161.1 1.0 copy-done.29
  162.1 5.5 %rim_step.9 = (bf16[96,8,128]{2,1,0:T(8,128)(2,1)S(1)}, bf16[96,16,128]{2,1,0:T(8,128)(2,1)S(1)}, bf16[176,16,128]{2,1,0:T(8,128)(2,1)S(1)}) custom-call(s32[96]{0:T(128)S(1)} %add_select_fusion.2.refs_0_.pick_ref, s32[97]{0:T(128)S(1)} %get-tuple-element.134.refs_1_.refs_0_, s32[96]{0:T(128)S(1)} %compare_select_fusion.4.slot_ref.refs_2_, ...), custom_call_target="tpu_custom_call" | custom-call | flops 301989888 | bytes 1152000 | tf_op jit(solution)/shard_map/rim_step/pallas_call | solution.py:460
  167.6 0.9 copy-done.14
  168.5 0.8 copy-done.22
  169.2 5.9 %all-to-all-start.4 = ((bf16[16,176,128]{2,1,0:T(8,128)(2,1)}), bf16[16,176,128]{2,1,0:T(8,128)(2,1)S(1)}, u32[]{:S(2)}, u32[]{:S(2)}) async-start(bf16[16,176,128]{2,1,0:T(8,128)(2,1)} %bitcast.185), calls=%async_computation.4 | async-start | bytes 1441792 | tf_op jit(solution)/shard_map/all_to_all | solution.py:922
  175.6 0.7 copy-done.37
  176.2 4.5 %fusion.4 = f32[24,12,12,128]{3,0,2,1:T(8,128)S(1)} fusion(bf16[3,3,256,128]{3,2,1,0:T(8,128)(2,1)S(1)} %copy-done.2, bf16[24,1,12,128]{3,0,2,1:T(8,128)(2,1)S(1)} %copy-done.41, bf16[24,10,1,128]{3,0,2,1:T(8,128)(2,1)S(1)} %bitcast.215, bf16[24,10,10,128]{3,0,2,1:T(8,128)(2,1)S(1)} %copy-done.37, bf16[24,10,1,128]{3,0,2,1:T(8,128)(2,1)S(1)} %bitcast.214, ...), kind=kOutput, calls=%fused_computation.6 | convolution fusion | flops 1828847616 | bytes 4128768 | tf_op jit(solution)/shard_map/conv_general_dilated | solution.py:892
  181.1 0.9 copy-done.36
  182.7 3.4 %skip_step.5.refs_9_ = f32[96,24,128]{2,1,0:T(8,128)S(1)} custom-call(s32[97]{0:T(128)S(1)} %get-tuple-element.134.refs_1_.refs_0_, s32[97]{0:T(128)S(1)} %get-tuple-element.133.refs_3_.refs_1_, s32[100]{0:T(128)S(1)} %get-tuple-element.127.refs_5_.refs_2_, bf16[96,24,128]{2,1,0:T(8,128)(2,1)S(1)} %copy-done.18, bf16[9,256,128]{2,1,0:T(8,128)(2,1)S(1)} %bitcast.170), custom_call_target="tpu_custom_call" | custom-call | flops 452984832 | bytes 1769472 | tf_op jit(solution)/shard_map/skip_step/pallas_call | solution.py:293
  186.0 1.0 copy-done
  187.1 5.9 %all-to-all-done.4 = bf16[16,176,128]{2,1,0:T(8,128)(2,1)S(1)} async-done(((bf16[16,176,128]{2,1,0:T(8,128)(2,1)}), bf16[16,176,128]{2,1,0:T(8,128)(2,1)S(1)}, u32[]{:S(2)}, u32[]{:S(2)}) %all-to-all-start.4) | async-done | bytes 720928 | tf_op jit(solution)/shard_map/all_to_all | solution.py:922
  193.0 1.0 copy-done.23
  194.0 6.4 %rim_step.10 = (bf16[96,16,128]{2,1,0:T(8,128)(2,1)S(1)}, bf16[96,24,128]{2,1,0:T(8,128)(2,1)S(1)}, bf16[176,24,128]{2,1,0:T(8,128)(2,1)}) custom-call(s32[96]{0:T(128)S(1)} %add_select_fusion.2.refs_0_.pick_ref, s32[97]{0:T(128)S(1)} %get-tuple-element.134.refs_1_.refs_0_, s32[96]{0:T(128)S(1)} %compare_select_fusion.4.slot_ref.refs_2_, ...), custom_call_target="tpu_custom_call" | custom-call | flops 603979776 | bytes 2304000 | tf_op jit(solution)/shard_map/rim_step/pallas_call | solution.py:460
  200.4 0.7 copy-done.20
  201.1 4.9 %all-to-all-start.5 = ((bf16[16,264,128]{2,1,0:T(8,128)(2,1)}), bf16[16,264,128]{2,1,0:T(8,128)(2,1)S(1)}, u32[]{:S(2)}, u32[]{:S(2)}) async-start(bf16[16,264,128]{2,1,0:T(8,128)(2,1)} %bitcast.210), calls=%async_computation.5 | async-start | bytes 2162688 | tf_op jit(solution)/shard_map/all_to_all | solution.py:922
  206.0 1.4 slice.241
  208.3 0.7 pad_maximum_fusion.1.refs_2_
  209.1 17.8 %dec_conv.2 = (bf16[24,12,2,24,128]{4,3,2,1,0:T(8,128)(2,1)}, f32[24,4,24,128]{3,2,1,0:T(8,128)S(1)}) custom-call(bf16[24,24,24,128]{3,2,1,0:T(8,128)(2,1)} %bitcast.219, bf16[24,4,24,128]{3,2,1,0:T(8,128)(2,1)S(1)} %bitcast.188, bf16[24,12,12,128]{3,2,1,0:T(8,128)(2,1)S(1)} %pad_maximum_fusion.1.refs_2_, bf16[9,256,128]{2,1,0:T(8,128)(2,1)S(1)} %bitcast.172), custom_call_target="tpu_custom_call" | custom-call | flops 8139571200 | bytes 8294400 | tf_op jit(solution)/shard_map/dec_conv/pallas_call | solution.py:848
  226.9 1.0 copy-done.11
  228.0 3.7 %all-to-all-done.5 = bf16[16,264,128]{2,1,0:T(8,128)(2,1)S(1)} async-done(((bf16[16,264,128]{2,1,0:T(8,128)(2,1)}), bf16[16,264,128]{2,1,0:T(8,128)(2,1)S(1)}, u32[]{:S(2)}, u32[]{:S(2)}) %all-to-all-start.5) | async-done | bytes 1081376 | tf_op jit(solution)/shard_map/all_to_all | solution.py:922
  231.6 8.8 %rim_step.11 = (bf16[96,24,128]{2,1,0:T(8,128)(2,1)S(1)}, bf16[96,48,128]{2,1,0:T(8,128)(2,1)S(1)}, bf16[176,48,128]{2,1,0:T(8,128)(2,1)}) custom-call(s32[96]{0:T(128)S(1)} %add_select_fusion.2.refs_0_.pick_ref, s32[97]{0:T(128)S(1)} %get-tuple-element.134.refs_1_.refs_0_, s32[96]{0:T(128)S(1)} %compare_select_fusion.4.slot_ref.refs_2_, ...), custom_call_target="tpu_custom_call" | custom-call | flops 905969664 | bytes 3456000 | tf_op jit(solution)/shard_map/rim_step/pallas_call | solution.py:460
  240.5 1.1 copy-done.5
  241.6 0.8 copy-done.31
  242.4 4.9 %all-to-all-start.6 = ((bf16[16,528,128]{2,1,0:T(8,128)(2,1)}), bf16[16,528,128]{2,1,0:T(8,128)(2,1)S(1)}, u32[]{:S(2)}, u32[]{:S(2)}) async-start(bf16[16,528,128]{2,1,0:T(8,128)(2,1)} %bitcast.208), calls=%async_computation.6 | async-start | bytes 4325376 | tf_op jit(solution)/shard_map/all_to_all | solution.py:922
  247.3 1.3 copy-done.9
  248.6 42.6 %dec_conv.3 = (bf16[24,24,2,48,128]{4,3,2,1,0:T(8,128)(2,1)}, f32[24,4,48,128]{3,2,1,0:T(8,128)}) custom-call(bf16[24,48,48,128]{3,2,1,0:T(8,128)(2,1)} %bitcast.218, bf16[24,4,48,128]{3,2,1,0:T(8,128)(2,1)S(1)} %bitcast.180, bf16[24,24,24,128]{3,2,1,0:T(8,128)(2,1)} %bitcast.220, bf16[24,4,24,128]{3,2,1,0:T(8,128)(2,1)S(1)} %bitcast.202, ...), custom_call_target="tpu_custom_call" | custom-call | flops 32558284800 | bytes 33177600 | tf_op jit(solution)/shard_map/dec_conv/pallas_call | solution.py:848
  291.2 5.0 %all-to-all-done.6 = bf16[16,528,128]{2,1,0:T(8,128)(2,1)S(1)} async-done(((bf16[16,528,128]{2,1,0:T(8,128)(2,1)}), bf16[16,528,128]{2,1,0:T(8,128)(2,1)S(1)}, u32[]{:S(2)}, u32[]{:S(2)}) %all-to-all-start.6) | async-done | bytes 2162720 | tf_op jit(solution)/shard_map/all_to_all | solution.py:922
  296.1 1.3 copy-done.6
  297.4 9.2 %last_step.1 = bf16[24,48,48,128]{3,2,1,0:T(8,128)(2,1)} custom-call(s32[96]{0:T(128)S(1)} %add_select_fusion.2.refs_0_.pick_ref, bf16[176,48,128]{2,1,0:T(8,128)(2,1)S(1)} %bitcast.158, bf16[96,48,128]{2,1,0:T(8,128)(2,1)S(1)} %copy-done.6, f32[96,48,128]{2,1,0:T(8,128)} %bitcast.207, ...), custom_call_target="tpu_custom_call", output_to_operand_aliasing={{}: (4, {})} | custom-call | tf_op jit(solution)/shard_map/last_step/pallas_call | solution.py:760
  (146 shorter events, 9.3 us)
Async XLA Ops:
  8.5 1.0 copy-start.10
  9.5 6.7 %copy-start.44 = (s32[384,4,2]{0,2,1:T(2,128)S(1)}, s32[384,4,2]{0,2,1:T(2,128)}, u32[]{:S(2)}) copy-start(s32[384,4,2]{0,2,1:T(2,128)} %param.10) | copy-start | bytes 36868
  9.5 11.6 %copy-start.25 = (bf16[3,3,128,128]{3,2,1,0:T(8,128)(2,1)S(1)}, bf16[3,3,128,128]{3,2,1,0:T(8,128)(2,1)}, u32[]{:S(2)}) copy-start(bf16[3,3,128,128]{3,2,1,0:T(8,128)(2,1)} %param.11) | copy-start | bytes 884740
  9.5 55.5 %all-to-all-start = ((bf16[16,528,128]{2,1,0:T(8,128)(2,1)}), bf16[16,528,128]{2,1,0:T(8,128)(2,1)S(1)}, u32[]{:S(2)}, u32[]{:S(2)}) async-start(bf16[16,528,128]{2,1,0:T(8,128)(2,1)} %bitcast.11), calls=%async_computation | async-start | bytes 4325376 | tf_op jit(solution)/shard_map/all_to_all | solution.py:922
  55.7 1.4 copy-start.3
  57.1 1.0 copy-start.12
  65.0 1.4 copy-start.33
  75.2 1.1 copy-start.7
  76.3 5.0 %copy-start.30 = (bf16[3,3,128,128]{3,2,1,0:T(8,128)(2,1)S(1)}, bf16[3,3,128,128]{3,2,1,0:T(8,128)(2,1)}, u32[]{:S(2)}) copy-start(bf16[3,3,128,128]{3,2,1,0:T(8,128)(2,1)} %param.12) | copy-start | bytes 884740
  76.3 30.6 %all-to-all-start.1 = ((bf16[16,264,128]{2,1,0:T(8,128)(2,1)}), bf16[16,264,128]{2,1,0:T(8,128)(2,1)S(1)}, u32[]{:S(2)}, u32[]{:S(2)}) async-start(bf16[16,264,128]{2,1,0:T(8,128)(2,1)} %bitcast.17), calls=%async_computation.1 | async-start | bytes 2162688 | tf_op jit(solution)/shard_map/all_to_all | solution.py:922
  96.3 1.0 copy-start.13
  106.9 1.0 copy-start.34
  113.7 0.9 copy-start.17
  114.6 5.2 %copy-start.35 = (bf16[24,10,10,128]{3,2,1,0:T(8,128)(2,1)S(1)}, bf16[24,10,10,128]{3,2,1,0:T(8,128)(2,1)}, u32[]{:S(2)}) copy-start(bf16[24,10,10,128]{3,2,1,0:T(8,128)(2,1)} %slice.167) | copy-start | bytes 1843204
  114.7 22.8 %all-to-all-start.2 = ((bf16[16,176,128]{2,1,0:T(8,128)(2,1)}), bf16[16,176,128]{2,1,0:T(8,128)(2,1)S(1)}, u32[]{:S(2)}, u32[]{:S(2)}) async-start(bf16[16,176,128]{2,1,0:T(8,128)(2,1)} %bitcast.23), calls=%async_computation.2 | async-start | bytes 1441792 | tf_op jit(solution)/shard_map/all_to_all | solution.py:922
  119.6 1.0 copy-start.26
  137.5 1.0 copy-start.27
  138.4 9.2 %copy-start.1 = (bf16[3,3,256,128]{3,2,1,0:T(8,128)(2,1)S(1)}, bf16[3,3,256,128]{3,2,1,0:T(8,128)(2,1)}, u32[]{:S(2)}) copy-start(bf16[3,3,256,128]{3,2,1,0:T(8,128)(2,1)} %param.17) | copy-start | bytes 1769476
  142.0 0.7 copy-start.24
  142.0 11.7 %copy-start.15 = (bf16[96,8,128]{2,1,0:T(8,128)(2,1)}, bf16[96,8,128]{2,1,0:T(8,128)(2,1)S(1)}, u32[]{:S(2)}) copy-start(bf16[96,8,128]{2,1,0:T(8,128)(2,1)S(1)} %get-tuple-element.56.refs_7_) | copy-start | bytes 589828
  142.0 5.7 %copy-start.8 = (bf16[96,48,128]{2,1,0:T(8,128)(2,1)S(1)}, bf16[96,48,128]{2,1,0:T(8,128)(2,1)}, u32[]{:S(2)}) copy-start(bf16[96,48,128]{2,1,0:T(8,128)(2,1)} %copy-done.7) | copy-start | bytes 3538948
  142.7 18.4 %all-to-all-start.3 = ((bf16[16,88,128]{2,1,0:T(8,128)(2,1)}), bf16[16,88,128]{2,1,0:T(8,128)(2,1)S(1)}, u32[]{:S(2)}, u32[]{:S(2)}) async-start(bf16[16,88,128]{2,1,0:T(8,128)(2,1)} %bitcast.193), calls=%async_computation.3 | async-start | bytes 720896 | tf_op jit(solution)/shard_map/all_to_all | solution.py:922
  147.7 6.0 %copy-start.28 = (bf16[3,3,128,128]{3,2,1,0:T(8,128)(2,1)S(1)}, bf16[3,3,128,128]{3,2,1,0:T(8,128)(2,1)}, u32[]{:S(2)}) copy-start(bf16[3,3,128,128]{3,2,1,0:T(8,128)(2,1)} %param.14) | copy-start | bytes 884740
  147.7 6.0 %copy-start.39 = (bf16[24,4,4,128]{3,0,2,1:T(8,128)(2,1)S(1)}, bf16[24,4,4,128]{3,0,2,1:T(8,128)(2,1)}, u32[]{:S(2)}) copy-start(bf16[24,4,4,128]{3,0,2,1:T(8,128)(2,1)} %fusion.29) | copy-start | bytes 294916
  154.4 2.8 copy-start.2
  157.1 4.0 %copy-start.16 = (bf16[96,8,128]{2,1,0:T(8,128)(2,1)S(1)}, bf16[96,8,128]{2,1,0:T(8,128)(2,1)}, u32[]{:S(2)}) copy-start(bf16[96,8,128]{2,1,0:T(8,128)(2,1)} %copy-done.15) | copy-start | bytes 589828
  161.1 1.0 copy-start.29
  167.6 0.9 copy-start.14
  168.4 0.8 copy-start.22
  169.2 6.1 %copy-start.38 = (bf16[24,4,4,128]{3,0,2,1:T(8,128)(2,1)S(1)}, bf16[24,4,4,128]{3,0,2,1:T(8,128)(2,1)}, u32[]{:S(2)}) copy-start(bf16[24,4,4,128]{3,0,2,1:T(8,128)(2,1)} %multiply_convert_fusion.1) | copy-start | bytes 294916
  169.2 23.8 %all-to-all-start.4 = ((bf16[16,176,128]{2,1,0:T(8,128)(2,1)}), bf16[16,176,128]{2,1,0:T(8,128)(2,1)S(1)}, u32[]{:S(2)}, u32[]{:S(2)}) async-start(bf16[16,176,128]{2,1,0:T(8,128)(2,1)} %bitcast.185), calls=%async_computation.4 | async-start | bytes 1441792 | tf_op jit(solution)/shard_map/all_to_all | solution.py:922
  175.1 1.1 copy-start.37
  175.1 1.1 copy-start.40
  175.2 1.1 copy-start.41
  175.2 1.1 copy-start.42
  175.2 1.1 copy-start.43
  180.8 1.2 copy-start.36
  180.9 1.5 copy-start.4
  180.9 1.8 copy-start.18
  186.0 1.0 copy-start
  193.0 1.0 copy-start.23
  200.4 0.7 copy-start.20
  201.1 30.5 %all-to-all-start.5 = ((bf16[16,264,128]{2,1,0:T(8,128)(2,1)}), bf16[16,264,128]{2,1,0:T(8,128)(2,1)S(1)}, u32[]{:S(2)}, u32[]{:S(2)}) async-start(bf16[16,264,128]{2,1,0:T(8,128)(2,1)} %bitcast.210), calls=%async_computation.5 | async-start | bytes 2162688 | tf_op jit(solution)/shard_map/all_to_all | solution.py:922
  206.0 2.0 copy-start.21
  208.0 1.1 copy-start.19
  226.9 1.0 copy-start.11
  240.5 1.1 copy-start.5
  241.6 0.8 copy-start.31
  242.4 4.9 %copy-start.32 = (bf16[96,24,128]{2,1,0:T(8,128)(2,1)S(1)}, bf16[96,24,128]{2,1,0:T(8,128)(2,1)}, u32[]{:S(2)}) copy-start(bf16[96,24,128]{2,1,0:T(8,128)(2,1)} %copy-done.31) | copy-start | bytes 1769476
  242.4 53.8 %all-to-all-start.6 = ((bf16[16,528,128]{2,1,0:T(8,128)(2,1)}), bf16[16,528,128]{2,1,0:T(8,128)(2,1)S(1)}, u32[]{:S(2)}, u32[]{:S(2)}) async-start(bf16[16,528,128]{2,1,0:T(8,128)(2,1)} %bitcast.208), calls=%async_computation.6 | async-start | bytes 4325376 | tf_op jit(solution)/shard_map/all_to_all | solution.py:922
  247.3 1.3 copy-start.9
  296.1 1.3 copy-start.6

commit v3 on v2

--- a/solution.py
+++ b/solution.py
@@ -7,6 +7,7 @@
 from jax.sharding import PartitionSpec as P
 
 FACE_TILES = 8
+RIM_TILES = 12
 VMEM_LIMIT = 50 * 2**20
 BF = jnp.bfloat16
 F32 = jnp.float32
@@ -102,10 +103,13 @@
     from_target = (target[:, None] == blocks[None, :]).astype(BF)
     their_ranks = jnp.dot(from_target, ranks, preferred_element_type=F32)
     recv_rank = jnp.sum(jnp.where(wanted[:, None] == order[None, :], their_ranks, 0.0), axis=1).astype(jnp.int32)
-    pick_row = jnp.where(remote, target * slot_count + recv_rank, devices * slot_count + wanted)
+    pick_row = lambda count: jnp.where(remote, target * count + recv_rank, devices * count + wanted)
     odd = (matching != (order + 2) % 4) | (reversed_rows == 1)
     one_more = lambda a: jnp.concatenate([a, jnp.zeros((1,), jnp.int32)])
-    return (pick_row, one_more(reversed_rows), slot_row, one_more(matching), listed(remote), listed(odd))
+    even = (slot_count + 1) // 2 * 2
+    paired_slot = slot_row + target * (even - slot_count)
+    shared = (one_more(reversed_rows), one_more(matching), listed(remote), listed(odd))
+    return (pick_row(slot_count), pick_row(even)), (slot_row, paired_slot), shared
 
 
 def up16(n):
@@ -114,6 +118,14 @@
 
 def strip_rows(n):
     return {6: 8, 12: 16}.get(n, n)
+
+
+def two_up(rows):
+    return rows == 16
+
+
+def send_shape(devices, cap, rows):
+    return (devices * ((cap + 1) // 2), 24) if two_up(rows) else (devices * cap, rows)
 
 
 def params():
@@ -143,7 +155,7 @@
 
 def tile_rims(x, slot_row, rows):
     tiles, n, _, c = x.shape
-    g = group_of(tiles, 4)
+    g = group_of(tiles, RIM_TILES)
     last = n // 16 - 1
     return pl.pallas_call(
         rims_kernel,
@@ -225,11 +237,18 @@
 
 
 def incoming(pick_ref, recv_ref, own_ref, i):
-    rows = recv_ref.shape[0]
+    paired = own_ref.shape[1] != recv_ref.shape[1]
+    slots = recv_ref.shape[0] * (2 if paired else 1)
     pick = pick_ref[i]
-    a = recv_ref[jnp.minimum(pick, rows - 1)].astype(F32)
-    b = own_ref[jnp.maximum(pick - rows, 0)].astype(F32)
-    return jnp.where(pick < rows, a, b)
+    away = pick < slots
+    slot = jnp.minimum(pick, slots - 1)
+    b = own_ref[jnp.maximum(pick - slots, 0)].astype(F32)
+    if not paired:
+        return jnp.where(away, recv_ref[slot].astype(F32), b)
+    a = recv_ref[slot >> 1].astype(F32)
+    row = lax.broadcasted_iota(jnp.int32, (16, 128), 0)
+    a = jnp.where(row < 12, jnp.where((slot & 1) == 1, pltpu.roll(a, 12, 0), a)[0:16], 0.0)
+    return jnp.where(away, a, b)
 
 
 def edge_taps(w_ref, e, lo):
@@ -303,7 +322,7 @@
         compiler_params=params(),
         cost_estimate=pl.CostEstimate(flops=strips * lp * 2 * 384 * 256, bytes_accessed=strips * lp * 768, transcendentals=0),
         name="skip_step",
-    )(plan[1], plan[3], plan[5], rim, w.reshape(9, -1, c))
+    )(plan[2][0], plan[2][1], plan[2][3], rim, w.reshape(9, -1, c))
 
 
 def corners(end):
@@ -325,8 +344,7 @@
     edge_buf, ring_buf, sum_buf, out_buf = next(it), next(it), next(it), next(it)
     lhsn_ref, conn_ref, taps_ref, big_buf = [next(it) for _ in range(4)] if nxt == "halo" else [None] * 4
 
-    lp = recv_ref.shape[1]
-    strips = own_ref.shape[0]
+    strips, lp = own_ref.shape[0], own_ref.shape[1]
     tiles = strips // 4
     flip, keep = flip_matrices(lp, n)
 
@@ -415,14 +433,22 @@
         each_tile(tiles, put)
 
     def send(i):
-        send_ref[slot_ref[i]] = next_ref[i]
+        slot = slot_ref[i]
+        if next_ref.shape[1] == send_ref.shape[1]:
+            send_ref[slot] = next_ref[i]
+        else:
+            block, second = slot >> 1, (slot & 1) == 1
+            strip = jnp.concatenate([next_ref[i].astype(F32), jnp.zeros((8, 128), F32)], axis=0)
+            row = lax.broadcasted_iota(jnp.int32, (24, 128), 0)
+            held = send_ref[block].astype(F32)
+            both = jnp.where(second, jnp.where(row < 12, held, pltpu.roll(strip, 12, 0)), jnp.where(row < 12, strip, held))
+            send_ref[block] = both.astype(BF)
 
     each_listed(remote_ref, send)
 
 
-def rim_step(n, plan, recv, own, sums, w=None, ring=None, skip=None, wn=None):
-    rows, lp, c = recv.shape
-    strips = own.shape[0]
+def rim_step(n, devices, cap, plan, recv, own, sums, w=None, ring=None, skip=None, wn=None):
+    strips, lp, c = own.shape
     tiles = strips // 4
     side = group_of(tiles, 3)
     nxt = "shrink" if ring is not None else "halo"
@@ -435,7 +461,7 @@
     outs = [
         jax.ShapeDtypeStruct((strips, lp, c), BF),
         jax.ShapeDtypeStruct((strips, lo, c), BF),
-        jax.ShapeDtypeStruct((rows, lo, c), BF),
+        jax.ShapeDtypeStruct(send_shape(devices, cap, lo) + (c,), BF),
     ]
     scratch = [
         pltpu.VMEM((strips + 1, lp, 128), BF),
@@ -466,7 +492,7 @@
         compiler_params=params(),
         cost_estimate=pl.CostEstimate(flops=strips * lp * 2 * 384 * 512, bytes_accessed=strips * lp * 1500, transcendentals=0),
         name="rim_step",
-    )(*plan, *args)
+    )(plan[0][int(two_up(lp))], plan[2][0], plan[1][int(two_up(lo))], *plan[2][1:], *args)
 
 
 def spread_columns(strip, n, sublane, buf):
@@ -774,7 +800,7 @@
         input_output_aliases={4: 0},
         compiler_params=params(),
         name="last_step",
-    )(plan[0], recv, own, sums, x)
+    )(plan[0][0], recv, own, sums, x)
 
 
 def group_of(tiles, want):
@@ -918,11 +944,11 @@
     slot_row = send_slots(edge_table, position, tiles, cap)
 
     def trade(strips):
-        length = strips.shape[1]
-        out = lax.all_to_all(
-            strips.reshape(devices, cap * length, 128), "tile", split_axis=0, concat_axis=0, tiled=True
-        )
-        return out.reshape(rows, length, 128)
+        out = lax.all_to_all(strips.reshape(devices, -1, 128), "tile", split_axis=0, concat_axis=0, tiled=True)
+        return out.reshape(strips.shape)
+
+    def step(n, *args, **kw):
+        return rim_step(n, devices, cap, plan, *args, **kw)
 
     def after(value, token):
         return lax.optimization_barrier((value, token))[0]
@@ -932,17 +958,17 @@
     plan = receive_plan(after(edge_table, send), slot_row, position, tiles, cap, devices)
     recv = trade(send)
     enc0, sums, ring, x1 = enc_conv(features, None, w_enc0, 1)
-    enc0_rim, x1_rim, send = rim_step(n0, plan, recv, rim0, sums, w=w_enc0, ring=ring)
+    enc0_rim, x1_rim, send = step(n0, recv, rim0, sums, w=w_enc0, ring=ring)
 
     recv = trade(send)
     enc1, sums, ring, x2 = enc_conv(x1, x1_rim, w_enc1, 4)
-    enc1_rim, x2_rim, send = rim_step(n0 // 2, plan, recv, x1_rim, sums, w=w_enc1, ring=ring)
+    enc1_rim, x2_rim, send = step(n0 // 2, recv, x1_rim, sums, w=w_enc1, ring=ring)
 
     recv = trade(send)
     sums = inner_sums(patched(x2, x2_rim), w_enc2)
     enc2 = jax.nn.silu(sums).astype(BF)
-    enc2_rim, x3_rim, send = rim_step(
-        n0 // 4, plan, recv, x2_rim, strips_of(sums), w=w_enc2, ring=strips_of(enc2, 1)
+    enc2_rim, x3_rim, send = step(
+        n0 // 4, recv, x2_rim, strips_of(sums), w=w_enc2, ring=strips_of(enc2, 1)
     )
 
     recv = trade(send)
@@ -951,8 +977,8 @@
     skip2 = skip_step(n0 // 4, plan, enc2_rim, w_dec2)
     skip0 = skip_step(n0, plan, after(enc0_rim, x3_rim), w_dec0)
     sums, skip0 = lax.optimization_barrier((sums, skip0))
-    mid_rim, own, send = rim_step(
-        n0 // 8, plan, recv, x3_rim, strips_of(sums), w=w_mid,
+    mid_rim, own, send = step(
+        n0 // 8, recv, x3_rim, strips_of(sums), w=w_mid,
         skip=skip2, wn=w_dec2,
     )
 
@@ -961,14 +987,14 @@
     sums = inner_sums(joined, w_dec2)
     dec2 = jax.nn.silu(sums).astype(BF)
     skip1 = skip_step(n0 // 2, plan, after(enc1_rim, mid_rim), w_dec1)
-    dec2_rim, own, send = rim_step(
-        n0 // 4, plan, recv, own, strips_of(sums), skip=skip1, wn=w_dec1
+    dec2_rim, own, send = step(
+        n0 // 4, recv, own, strips_of(sums), skip=skip1, wn=w_dec1
     )
 
     recv = trade(send)
     dec1, sums = dec_conv(enc1, enc1_rim, patched(dec2, dec2_rim), None, w_dec1, 4)
-    dec1_rim, own, send = rim_step(
-        n0 // 2, plan, recv, own, sums, skip=skip0, wn=w_dec0
+    dec1_rim, own, send = step(
+        n0 // 2, recv, own, sums, skip=skip0, wn=w_dec0
     )
 
     recv = trade(send)

time: 309 us -> 300 us (0.971)
  waiting for transfers between devices: 41.7 us -> 33.8 us
  Pallas kernels: 178 us -> 172 us
  local copies, waits for them, and re-layouts: 33.3 us -> 36.5 us
    all_to_all x7, waiting for transfers between devices: 41.7 us -> 33.8 us  [trade(): lax.all_to_all(strips.reshape(devices, -1, 128), 'tile', split_axis=0, co...]
    pallas_call x6, Pallas kernels: 38.8 us -> 35.6 us  [rim_step(): pl.pallas_call(kernel, in_specs=[smem] * 6 + [vmem] * len(args), out_spec...]
    unnamed x106 -> x118, local copies, waits for them, and re-layouts: 26.6 us -> 27.2 us
  transfers between devices with their start and end apart: 7 -> 7, of which waited for: 6 -> 6; matrix products, arithmetic and copies ran while one was open for 8% -> 9% of each run, Pallas kernels for 40% -> 40%
where the time goes in v3:
time: 300 us; the launch traced here: 298 us
  Pallas kernels  172 us (57%)
  starting transfers between devices  38.8 us (13%)
  local copies, waits for them, and re-layouts  36.5 us (12%)
  waiting for transfers between devices  33.8 us (11%)
  matrix products  9.35 us (3%)
  other arithmetic  7 us (2%)
    pallas_call x2, Pallas kernels, dec_conv(): pl.pallas_call(kernel, grid=(tiles // g,), in_specs=specs, out_specs=[til...  60.5 us
    pallas_call x2, Pallas kernels, enc_conv(): pl.pallas_call(enc_kernel, grid=(tiles // g,), in_specs=specs, out_specs=...  49.6 us
    all_to_all x7, starting transfers between devices, trade(): lax.all_to_all(strips.reshape(devices, -1, 128), 'tile', split_axis=0, co...  38.8 us
    pallas_call x6, Pallas kernels, rim_step(): pl.pallas_call(kernel, in_specs=[smem] * 6 + [vmem] * len(args), out_spec...  35.6 us
    all_to_all x7, waiting for transfers between devices, trade(): lax.all_to_all(strips.reshape(devices, -1, 128), 'tile', split_axis=0, co...  33.8 us
    unnamed x118, local copies, waits for them, and re-layouts  27.2 us
    pallas_call x3, Pallas kernels, skip_step(): pl.pallas_call(lambda *refs: skip_kernel(n, *refs), in_specs=[smem, smem,...  10.7 us
    pallas_call x1, Pallas kernels, last_step(): pl.pallas_call(last_kernel, in_specs=[smem, vmem, vmem, vmem, anywhere],...  9.16 us
  transfers between devices with their start and end apart: 7, of which 6 were waited for; matrix products, arithmetic and copies ran while one was open for 9% of the time, Pallas kernels for 40%

profile of v3, /device:TPU:15, one launch (start us, length us, event | category | flops | bytes accessed | tf_op | source)
XLA Modules:
  0.0 298.3 jit_solution(6274667448198282735)
XLA Ops:
  0.0 0.8 constant_dynamic-slice_fusion.1
  1.2 6.2 %tile_rims.1 = (bf16[24,4,48,128]{3,2,1,0:T(8,128)(2,1)S(1)}, bf16[176,48,128]{2,1,0:T(8,128)(2,1)}) custom-call(s32[96]{0:T(128)S(1)} %compare_select_fusion.4.slot_ref.refs_2_, bf16[24,48,48,128]{3,2,1,0:T(8,128)(2,1)} %refs_0_.1, bf16[24,48,48,128]{3,2,1,0:T(8,128)(2,1)} %refs_0_.1, bf16[24,48,48,128]{3,2,1,0:T(8,128)(2,1)} %refs_0_.1, ...), custom_call_target="tpu_custom_call" | custom-call | tf_op jit(solution)/shard_map/tile_rims/pallas_call | solution.py:160
  7.4 1.0 copy-done.10
  8.5 6.7 %all-to-all-start = ((bf16[16,528,128]{2,1,0:T(8,128)(2,1)}), bf16[16,528,128]{2,1,0:T(8,128)(2,1)S(1)}, u32[]{:S(2)}, u32[]{:S(2)}) async-start(bf16[16,528,128]{2,1,0:T(8,128)(2,1)} %bitcast.11), calls=%async_computation | async-start | bytes 4325376 | tf_op jit(solution)/shard_map/all_to_all | solution.py:947
  17.7 1.3 compare_select_fusion.2
  19.0 1.3 fusion.46
  20.3 34.6 %enc_conv.2 = (bf16[24,24,2,48,128]{4,3,2,1,0:T(8,128)(2,1)}, f32[24,4,48,128]{3,2,1,0:T(8,128)S(1)}, bf16[24,4,48,128]{3,2,1,0:T(8,128)(2,1)S(1)}, bf16[24,24,24,128]{3,2,1,0:T(8,128)(2,1)}) custom-call(bf16[24,48,48,128]{3,2,1,0:T(8,128)(2,1)} %refs_0_.1, bf16[9,128,128]{2,1,0:T(8,128)(2,1)S(1)} %bitcast.185), custom_call_target="tpu_custom_call" | custom-call | flops 21743271936 | bytes 33177600 | tf_op jit(solution)/shard_map/enc_conv/pallas_call | solution.py:827
  54.9 1.4 copy-done.4
  56.3 1.0 copy-done.12
  57.3 6.7 %all-to-all-done = bf16[16,528,128]{2,1,0:T(8,128)(2,1)S(1)} async-done(((bf16[16,528,128]{2,1,0:T(8,128)(2,1)}), bf16[16,528,128]{2,1,0:T(8,128)(2,1)S(1)}, u32[]{:S(2)}, u32[]{:S(2)}) %all-to-all-start) | async-done | bytes 2162720 | tf_op jit(solution)/shard_map/all_to_all | solution.py:947
  64.0 1.4 copy-done.40
  65.3 8.4 %rim_step.6 = (bf16[96,48,128]{2,1,0:T(8,128)(2,1)S(1)}, bf16[96,24,128]{2,1,0:T(8,128)(2,1)S(1)}, bf16[176,24,128]{2,1,0:T(8,128)(2,1)}) custom-call(s32[96]{0:T(128)S(1)} %get-tuple-element.130.refs_0_.pick_ref, s32[97]{0:T(128)S(1)} %get-tuple-element.137.refs_1_.refs_0_, s32[96]{0:T(128)S(1)} %compare_select_fusion.4.slot_ref.refs_2_, ...), custom_call_target="tpu_custom_call" | custom-call | flops 1811939328 | bytes 6912000 | tf_op jit(solution)/shard_map/rim_step/pallas_call | solution.py:486
  73.7 1.1 copy-done.7
  74.8 5.0 %all-to-all-start.1 = ((bf16[16,264,128]{2,1,0:T(8,128)(2,1)}), bf16[16,264,128]{2,1,0:T(8,128)(2,1)S(1)}, u32[]{:S(2)}, u32[]{:S(2)}) async-start(bf16[16,264,128]{2,1,0:T(8,128)(2,1)} %bitcast.17), calls=%async_computation.1 | async-start | bytes 2162688 | tf_op jit(solution)/shard_map/all_to_all | solution.py:947
  79.9 15.0 %enc_conv.3 = (bf16[24,12,2,24,128]{4,3,2,1,0:T(8,128)(2,1)}, f32[24,4,24,128]{3,2,1,0:T(8,128)S(1)}, bf16[24,4,24,128]{3,2,1,0:T(8,128)(2,1)S(1)}, bf16[24,12,12,128]{3,2,1,0:T(8,128)(2,1)S(1)}) custom-call(bf16[24,24,24,128]{3,2,1,0:T(8,128)(2,1)} %get-tuple-element.49.refs_0_, bf16[9,128,128]{2,1,0:T(8,128)(2,1)S(1)} %bitcast.189, ...), custom_call_target="tpu_custom_call" | custom-call | flops 5435817984 | bytes 8294400 | tf_op jit(solution)/shard_map/enc_conv/pallas_call | solution.py:827
  94.9 1.0 copy-done.13
  95.9 1.4 slice.167
  97.3 8.2 %all-to-all-done.1 = bf16[16,264,128]{2,1,0:T(8,128)(2,1)S(1)} async-done(((bf16[16,264,128]{2,1,0:T(8,128)(2,1)}), bf16[16,264,128]{2,1,0:T(8,128)(2,1)S(1)}, u32[]{:S(2)}, u32[]{:S(2)}) %all-to-all-start.1) | async-done | bytes 1081376 | tf_op jit(solution)/shard_map/all_to_all | solution.py:947
  105.5 1.0 copy-done.41
  106.5 5.5 %rim_step.7 = (bf16[96,24,128]{2,1,0:T(8,128)(2,1)S(1)}, bf16[96,16,128]{2,1,0:T(8,128)(2,1)S(1)}, bf16[96,24,128]{2,1,0:T(8,128)(2,1)}) custom-call(s32[96]{0:T(128)S(1)} %get-tuple-element.130.refs_0_.pick_ref, s32[97]{0:T(128)S(1)} %get-tuple-element.137.refs_1_.refs_0_, s32[96]{0:T(128)S(1)} %get-tuple-element.79.refs_2_, ...), custom_call_target="tpu_custom_call" | custom-call | flops 905969664 | bytes 3456000 | tf_op jit(solution)/shard_map/rim_step/pallas_call | solution.py:486
  112.0 0.8 copy-done.17
  112.9 5.0 %all-to-all-start.2 = ((bf16[16,144,128]{2,1,0:T(8,128)(2,1)}), bf16[16,144,128]{2,1,0:T(8,128)(2,1)S(1)}, u32[]{:S(2)}, u32[]{:S(2)}) async-start(bf16[16,144,128]{2,1,0:T(8,128)(2,1)} %bitcast.23), calls=%async_computation.2 | async-start | bytes 1179648 | tf_op jit(solution)/shard_map/all_to_all | solution.py:947
  118.2 0.7 pad_maximum_fusion
  118.9 2.6 multiply_convert_fusion
  121.6 0.9 slice.232
  123.8 9.2 %all-to-all-done.2 = bf16[16,144,128]{2,1,0:T(8,128)(2,1)S(1)} async-done(((bf16[16,144,128]{2,1,0:T(8,128)(2,1)}), bf16[16,144,128]{2,1,0:T(8,128)(2,1)S(1)}, u32[]{:S(2)}, u32[]{:S(2)}) %all-to-all-start.2) | async-done | bytes 589856 | tf_op jit(solution)/shard_map/all_to_all | solution.py:947
  133.0 1.0 copy-done.27
  134.0 3.2 %rim_step.8 = (bf16[96,16,128]{2,1,0:T(8,128)(2,1)S(1)}, bf16[96,8,128]{2,1,0:T(8,128)(2,1)S(1)}, bf16[176,8,128]{2,1,0:T(8,128)(2,1)S(1)}) custom-call(s32[96]{0:T(128)S(1)} %get-tuple-element.82.refs_0_, s32[97]{0:T(128)S(1)} %get-tuple-element.137.refs_1_.refs_0_, s32[96]{0:T(128)S(1)} %compare_select_fusion.4.slot_ref.refs_2_, ...), custom_call_target="tpu_custom_call" | custom-call | flops 603979776 | bytes 2304000 | tf_op jit(solution)/shard_map/rim_step/pallas_call | solution.py:486
  137.2 0.7 copy-done.24
  138.0 0.7 copy-done.14
  139.4 4.9 %all-to-all-start.3 = ((bf16[16,88,128]{2,1,0:T(8,128)(2,1)}), bf16[16,88,128]{2,1,0:T(8,128)(2,1)S(1)}, u32[]{:S(2)}, u32[]{:S(2)}) async-start(bf16[16,88,128]{2,1,0:T(8,128)(2,1)} %bitcast.184), calls=%async_computation.3 | async-start | bytes 720896 | tf_op jit(solution)/shard_map/all_to_all | solution.py:947
  144.4 5.3 %skip_step.3.refs_9_ = f32[96,48,128]{2,1,0:T(8,128)} custom-call(s32[97]{0:T(128)S(1)} %get-tuple-element.137.refs_1_.refs_0_, s32[97]{0:T(128)S(1)} %get-tuple-element.136.refs_3_.refs_1_, s32[100]{0:T(128)S(1)} %get-tuple-element.127.refs_5_.refs_2_, bf16[96,48,128]{2,1,0:T(8,128)(2,1)S(1)} %copy-done.8, bf16[9,256,128]{2,1,0:T(8,128)(2,1)S(1)} %bitcast.153), custom_call_target="tpu_custom_call" | custom-call | flops 905969664 | bytes 3538944 | tf_op jit(solution)/shard_map/skip_step/pallas_call | solution.py:312
  149.7 0.7 fusion.19
  153.3 2.6 skip_step.4.refs_10_
  156.0 1.0 copy-done.29
  156.9 4.7 %rim_step.9 = (bf16[96,8,128]{2,1,0:T(8,128)(2,1)S(1)}, bf16[96,16,128]{2,1,0:T(8,128)(2,1)S(1)}, bf16[96,24,128]{2,1,0:T(8,128)(2,1)S(1)}) custom-call(s32[96]{0:T(128)S(1)} %get-tuple-element.130.refs_0_.pick_ref, s32[97]{0:T(128)S(1)} %get-tuple-element.137.refs_1_.refs_0_, s32[96]{0:T(128)S(1)} %get-tuple-element.79.refs_2_, ...), custom_call_target="tpu_custom_call" | custom-call | flops 301989888 | bytes 1152000 | tf_op jit(solution)/shard_map/rim_step/pallas_call | solution.py:486
  161.6 0.8 copy-done.16
  162.4 0.8 copy-done.20
  163.3 6.6 %all-to-all-start.4 = ((bf16[16,144,128]{2,1,0:T(8,128)(2,1)}), bf16[16,144,128]{2,1,0:T(8,128)(2,1)S(1)}, u32[]{:S(2)}, u32[]{:S(2)}) async-start(bf16[16,144,128]{2,1,0:T(8,128)(2,1)} %bitcast.178), calls=%async_computation.4 | async-start | bytes 1179648 | tf_op jit(solution)/shard_map/all_to_all | solution.py:947
  170.3 0.7 copy-done.43
  171.0 5.7 %fusion.4 = f32[24,12,12,128]{3,0,2,1:T(8,128)} fusion(bf16[3,3,256,128]{3,2,1,0:T(8,128)(2,1)S(1)} %copy-done.2, bf16[24,1,12,128]{3,0,2,1:T(8,128)(2,1)S(1)} %copy-done.47, bf16[24,10,1,128]{3,0,2,1:T(8,128)(2,1)S(1)} %bitcast.206, bf16[24,10,10,128]{3,0,2,1:T(8,128)(2,1)S(1)} %copy-done.43, bf16[24,10,1,128]{3,0,2,1:T(8,128)(2,1)S(1)} %bitcast.205, ...), kind=kOutput, calls=%fused_computation.6 | convolution fusion | flops 1828847616 | bytes 4128768 | tf_op jit(solution)/shard_map/conv_general_dilated | solution.py:918
  176.7 1.0 slice_bitcast_fusion.1
  177.7 1.0 fusion.61
  179.0 0.8 copy-done.3
  180.0 2.8 skip_step.5.refs_9_
  182.8 1.0 copy-done
  183.8 1.2 all-to-all-done.4
  186.2 5.8 %rim_step.10 = (bf16[96,16,128]{2,1,0:T(8,128)(2,1)S(1)}, bf16[96,24,128]{2,1,0:T(8,128)(2,1)S(1)}, bf16[176,24,128]{2,1,0:T(8,128)(2,1)}) custom-call(s32[96]{0:T(128)S(1)} %copy-done.37, s32[97]{0:T(128)S(1)} %get-tuple-element.137.refs_1_.refs_0_, s32[96]{0:T(128)S(1)} %copy-done.32, s32[97]{0:T(128)S(1)} %get-tuple-element.136.refs_3_.refs_1_, ...), custom_call_target="tpu_custom_call" | custom-call | flops 603979776 | bytes 2304000 | tf_op jit(solution)/shard_map/rim_step/pallas_call | solution.py:486
  191.9 0.7 copy-done.22
  192.7 5.2 %all-to-all-start.5 = ((bf16[16,264,128]{2,1,0:T(8,128)(2,1)}), bf16[16,264,128]{2,1,0:T(8,128)(2,1)S(1)}, u32[]{:S(2)}, u32[]{:S(2)}) async-start(bf16[16,264,128]{2,1,0:T(8,128)(2,1)} %bitcast.201), calls=%async_computation.5 | async-start | bytes 2162688 | tf_op jit(solution)/shard_map/all_to_all | solution.py:947
  197.9 1.4 slice.241
  200.2 0.7 pad_maximum_fusion.1.refs_2_
  201.0 17.9 %dec_conv.2 = (bf16[24,12,2,24,128]{4,3,2,1,0:T(8,128)(2,1)}, f32[24,4,24,128]{3,2,1,0:T(8,128)S(1)}) custom-call(bf16[24,24,24,128]{3,2,1,0:T(8,128)(2,1)} %bitcast.210, bf16[24,4,24,128]{3,2,1,0:T(8,128)(2,1)S(1)} %bitcast.179, bf16[24,12,12,128]{3,2,1,0:T(8,128)(2,1)S(1)} %pad_maximum_fusion.1.refs_2_, bf16[9,256,128]{2,1,0:T(8,128)(2,1)S(1)} %bitcast.161), custom_call_target="tpu_custom_call" | custom-call | flops 8139571200 | bytes 8294400 | tf_op jit(solution)/shard_map/dec_conv/pallas_call | solution.py:874
  218.9 1.0 copy-done.11
  219.9 3.6 %all-to-all-done.5 = bf16[16,264,128]{2,1,0:T(8,128)(2,1)S(1)} async-done(((bf16[16,264,128]{2,1,0:T(8,128)(2,1)}), bf16[16,264,128]{2,1,0:T(8,128)(2,1)S(1)}, u32[]{:S(2)}, u32[]{:S(2)}) %all-to-all-start.5) | async-done | bytes 1081376 | tf_op jit(solution)/shard_map/all_to_all | solution.py:947
  223.5 8.0 %rim_step.11 = (bf16[96,24,128]{2,1,0:T(8,128)(2,1)S(1)}, bf16[96,48,128]{2,1,0:T(8,128)(2,1)S(1)}, bf16[176,48,128]{2,1,0:T(8,128)(2,1)}) custom-call(s32[96]{0:T(128)S(1)} %copy-done.35, s32[97]{0:T(128)S(1)} %get-tuple-element.137.refs_1_.refs_0_, s32[96]{0:T(128)S(1)} %copy-done.33, s32[97]{0:T(128)S(1)} %get-tuple-element.136.refs_3_.refs_1_, ...), custom_call_target="tpu_custom_call" | custom-call | flops 905969664 | bytes 3456000 | tf_op jit(solution)/shard_map/rim_step/pallas_call | solution.py:486
  231.6 1.1 copy-done.5
  232.6 0.8 copy-done.38
  233.4 5.4 %all-to-all-start.6 = ((bf16[16,528,128]{2,1,0:T(8,128)(2,1)}), bf16[16,528,128]{2,1,0:T(8,128)(2,1)S(1)}, u32[]{:S(2)}, u32[]{:S(2)}) async-start(bf16[16,528,128]{2,1,0:T(8,128)(2,1)} %bitcast.199), calls=%async_computation.6 | async-start | bytes 4325376 | tf_op jit(solution)/shard_map/all_to_all | solution.py:947
  238.8 1.3 copy-done.9
  240.1 42.6 %dec_conv.3 = (bf16[24,24,2,48,128]{4,3,2,1,0:T(8,128)(2,1)}, f32[24,4,48,128]{3,2,1,0:T(8,128)}) custom-call(bf16[24,48,48,128]{3,2,1,0:T(8,128)(2,1)} %bitcast.209, bf16[24,4,48,128]{3,2,1,0:T(8,128)(2,1)S(1)} %bitcast.171, bf16[24,24,24,128]{3,2,1,0:T(8,128)(2,1)} %bitcast.211, bf16[24,4,24,128]{3,2,1,0:T(8,128)(2,1)S(1)} %bitcast.193, ...), custom_call_target="tpu_custom_call" | custom-call | flops 32558284800 | bytes 33177600 | tf_op jit(solution)/shard_map/dec_conv/pallas_call | solution.py:874
  282.7 5.0 %all-to-all-done.6 = bf16[16,528,128]{2,1,0:T(8,128)(2,1)S(1)} async-done(((bf16[16,528,128]{2,1,0:T(8,128)(2,1)}), bf16[16,528,128]{2,1,0:T(8,128)(2,1)S(1)}, u32[]{:S(2)}, u32[]{:S(2)}) %all-to-all-start.6) | async-done | bytes 2162720 | tf_op jit(solution)/shard_map/all_to_all | solution.py:947
  287.6 1.3 copy-done.6
  288.9 9.2 %last_step.1 = bf16[24,48,48,128]{3,2,1,0:T(8,128)(2,1)} custom-call(s32[96]{0:T(128)S(1)} %copy-done.35, bf16[176,48,128]{2,1,0:T(8,128)(2,1)S(1)} %bitcast.149, bf16[96,48,128]{2,1,0:T(8,128)(2,1)S(1)} %copy-done.6, f32[96,48,128]{2,1,0:T(8,128)} %bitcast.198, bf16[24,48,48,128]{3,2,1,0:T(8,128)(2,1)} %bitcast.194), custom_call_target="tpu_custom_call", output_to_operand_aliasing={{}: (4, {})} | custom-call | tf_op jit(solution)/shard_map/last_step/pallas_call | solution.py:786
  (159 shorter events, 10.9 us)
Async XLA Ops:
  1.2 131.8 %copy-start.31 = (s32[96]{0:T(128)}, s32[96]{0:T(128)S(1)}, u32[]{:S(2)}) copy-start(s32[96]{0:T(128)S(1)} %compare_select_fusion.4.slot_ref.refs_2_) | copy-start | bytes 1156
  7.4 1.0 copy-start.10
  8.5 6.7 %copy-start.50 = (s32[384,4,2]{0,2,1:T(2,128)S(1)}, s32[384,4,2]{0,2,1:T(2,128)}, u32[]{:S(2)}) copy-start(s32[384,4,2]{0,2,1:T(2,128)} %param.10) | copy-start | bytes 36868
  8.5 11.8 %copy-start.25 = (bf16[3,3,128,128]{3,2,1,0:T(8,128)(2,1)S(1)}, bf16[3,3,128,128]{3,2,1,0:T(8,128)(2,1)}, u32[]{:S(2)}) copy-start(bf16[3,3,128,128]{3,2,1,0:T(8,128)(2,1)} %param.11) | copy-start | bytes 884740
  8.5 55.5 %all-to-all-start = ((bf16[16,528,128]{2,1,0:T(8,128)(2,1)}), bf16[16,528,128]{2,1,0:T(8,128)(2,1)S(1)}, u32[]{:S(2)}, u32[]{:S(2)}) async-start(bf16[16,528,128]{2,1,0:T(8,128)(2,1)} %bitcast.11), calls=%async_computation | async-start | bytes 4325376 | tf_op jit(solution)/shard_map/all_to_all | solution.py:947
  16.5 116.5 %copy-start.36 = (s32[96]{0:T(128)}, s32[96]{0:T(128)S(1)}, u32[]{:S(2)}) copy-start(s32[96]{0:T(128)S(1)} %get-tuple-element.82.refs_0_) | copy-start | bytes 1156
  17.1 138.8 %copy-start.34 = (s32[96]{0:T(128)}, s32[96]{0:T(128)S(1)}, u32[]{:S(2)}) copy-start(s32[96]{0:T(128)S(1)} %get-tuple-element.130.refs_0_.pick_ref) | copy-start | bytes 1156
  54.9 1.4 copy-start.4
  56.3 1.0 copy-start.12
  64.0 1.4 copy-start.40
  73.7 1.1 copy-start.7
  74.8 5.0 %copy-start.30 = (bf16[3,3,128,128]{3,2,1,0:T(8,128)(2,1)S(1)}, bf16[3,3,128,128]{3,2,1,0:T(8,128)(2,1)}, u32[]{:S(2)}) copy-start(bf16[3,3,128,128]{3,2,1,0:T(8,128)(2,1)} %param.12) | copy-start | bytes 884740
  74.8 30.7 %all-to-all-start.1 = ((bf16[16,264,128]{2,1,0:T(8,128)(2,1)}), bf16[16,264,128]{2,1,0:T(8,128)(2,1)S(1)}, u32[]{:S(2)}, u32[]{:S(2)}) async-start(bf16[16,264,128]{2,1,0:T(8,128)(2,1)} %bitcast.17), calls=%async_computation.1 | async-start | bytes 2162688 | tf_op jit(solution)/shard_map/all_to_all | solution.py:947
  94.9 1.0 copy-start.13
  105.5 1.0 copy-start.41
  112.0 0.8 copy-start.17
  112.8 5.3 %copy-start.42 = (bf16[24,10,10,128]{3,2,1,0:T(8,128)(2,1)S(1)}, bf16[24,10,10,128]{3,2,1,0:T(8,128)(2,1)}, u32[]{:S(2)}) copy-start(bf16[24,10,10,128]{3,2,1,0:T(8,128)(2,1)} %slice.167) | copy-start | bytes 1843204
  112.9 20.1 %all-to-all-start.2 = ((bf16[16,144,128]{2,1,0:T(8,128)(2,1)}), bf16[16,144,128]{2,1,0:T(8,128)(2,1)S(1)}, u32[]{:S(2)}, u32[]{:S(2)}) async-start(bf16[16,144,128]{2,1,0:T(8,128)(2,1)} %bitcast.23), calls=%async_computation.2 | async-start | bytes 1179648 | tf_op jit(solution)/shard_map/all_to_all | solution.py:947
  118.0 1.0 copy-start.26
  133.0 1.0 copy-start.27
  134.0 10.4 %copy-start.1 = (bf16[3,3,256,128]{3,2,1,0:T(8,128)(2,1)S(1)}, bf16[3,3,256,128]{3,2,1,0:T(8,128)(2,1)}, u32[]{:S(2)}) copy-start(bf16[3,3,256,128]{3,2,1,0:T(8,128)(2,1)} %param.17) | copy-start | bytes 1769476
  137.2 0.7 copy-start.24
  138.0 6.4 %copy-start.8 = (bf16[96,48,128]{2,1,0:T(8,128)(2,1)S(1)}, bf16[96,48,128]{2,1,0:T(8,128)(2,1)}, u32[]{:S(2)}) copy-start(bf16[96,48,128]{2,1,0:T(8,128)(2,1)} %copy-done.7) | copy-start | bytes 3538948
  138.0 0.7 copy-start.14
  139.4 16.5 %all-to-all-start.3 = ((bf16[16,88,128]{2,1,0:T(8,128)(2,1)}), bf16[16,88,128]{2,1,0:T(8,128)(2,1)S(1)}, u32[]{:S(2)}, u32[]{:S(2)}) async-start(bf16[16,88,128]{2,1,0:T(8,128)(2,1)} %bitcast.184), calls=%async_computation.3 | async-start | bytes 720896 | tf_op jit(solution)/shard_map/all_to_all | solution.py:947
  144.4 5.3 %copy-start.28 = (bf16[3,3,128,128]{3,2,1,0:T(8,128)(2,1)S(1)}, bf16[3,3,128,128]{3,2,1,0:T(8,128)(2,1)}, u32[]{:S(2)}) copy-start(bf16[3,3,128,128]{3,2,1,0:T(8,128)(2,1)} %param.14) | copy-start | bytes 884740
  144.4 5.3 %copy-start.45 = (bf16[24,4,4,128]{3,0,2,1:T(8,128)(2,1)S(1)}, bf16[24,4,4,128]{3,0,2,1:T(8,128)(2,1)}, u32[]{:S(2)}) copy-start(bf16[24,4,4,128]{3,0,2,1:T(8,128)(2,1)} %fusion.29) | copy-start | bytes 294916
  144.4 6.1 %copy-start.44 = (bf16[24,1,12,128]{3,2,1,0:T(8,128)(2,1)S(1)}, bf16[24,1,12,128]{3,2,1,0:T(8,128)(2,1)}, u32[]{:S(2)}) copy-start(bf16[24,1,12,128]{3,2,1,0:T(8,128)(2,1)} %get-tuple-element.109) | copy-start | bytes 221188
  150.5 2.8 copy-start.2
  153.1 2.8 copy-start.15
  156.0 1.0 copy-start.29
  161.6 0.8 copy-start.16
  162.4 0.8 copy-start.20
  163.3 7.0 %copy-start.46 = (bf16[24,1,12,128]{3,0,2,1:T(8,128)(2,1)S(1)}, bf16[24,1,12,128]{3,0,2,1:T(8,128)(2,1)}, u32[]{:S(2)}) copy-start(bf16[24,1,12,128]{3,0,2,1:T(8,128)(2,1)} %copy.155) | copy-start | bytes 221188
  163.3 7.0 %copy-start.47 = (bf16[24,1,12,128]{3,0,2,1:T(8,128)(2,1)S(1)}, bf16[24,1,12,128]{3,0,2,1:T(8,128)(2,1)}, u32[]{:S(2)}) copy-start(bf16[24,1,12,128]{3,0,2,1:T(8,128)(2,1)} %copy.158) | copy-start | bytes 221188
  163.3 7.0 %copy-start.48 = (bf16[24,1,10,128]{3,0,2,1:T(8,128)(2,1)S(1)}, bf16[24,1,10,128]{3,0,2,1:T(8,128)(2,1)}, u32[]{:S(2)}) copy-start(bf16[24,1,10,128]{3,0,2,1:T(8,128)(2,1)} %copy.190) | copy-start | bytes 184324
  163.3 21.7 %all-to-all-start.4 = ((bf16[16,144,128]{2,1,0:T(8,128)(2,1)}), bf16[16,144,128]{2,1,0:T(8,128)(2,1)S(1)}, u32[]{:S(2)}, u32[]{:S(2)}) async-start(bf16[16,144,128]{2,1,0:T(8,128)(2,1)} %bitcast.178), calls=%async_computation.4 | async-start | bytes 1179648 | tf_op jit(solution)/shard_map/all_to_all | solution.py:947
  169.9 1.1 copy-start.43
  169.9 1.1 copy-start.49
  178.7 1.1 copy-start.3
  178.8 1.2 copy-start.18
  178.9 6.1 %copy-start.21 = (bf16[96,16,128]{2,1,0:T(8,128)(2,1)S(1)}, bf16[96,16,128]{2,1,0:T(8,128)(2,1)}, u32[]{:S(2)}) copy-start(bf16[96,16,128]{2,1,0:T(8,128)(2,1)} %copy-done.20) | copy-start | bytes 1179652
  182.8 1.0 copy-start
  185.0 0.6 copy-start.32
  185.5 0.6 copy-start.37
  191.9 0.7 copy-start.22
  192.7 30.9 %all-to-all-start.5 = ((bf16[16,264,128]{2,1,0:T(8,128)(2,1)}), bf16[16,264,128]{2,1,0:T(8,128)(2,1)S(1)}, u32[]{:S(2)}, u32[]{:S(2)}) async-start(bf16[16,264,128]{2,1,0:T(8,128)(2,1)} %bitcast.201), calls=%async_computation.5 | async-start | bytes 2162688 | tf_op jit(solution)/shard_map/all_to_all | solution.py:947
  197.9 2.0 copy-start.23
  199.9 1.1 copy-start.19
  201.0 22.5 %copy-start.33 = (s32[96]{0:T(128)S(1)}, s32[96]{0:T(128)}, u32[]{:S(2)}) copy-start(s32[96]{0:T(128)} %copy-done.31) | copy-start | bytes 1156
  201.0 22.5 %copy-start.35 = (s32[96]{0:T(128)S(1)}, s32[96]{0:T(128)}, u32[]{:S(2)}) copy-start(s32[96]{0:T(128)} %copy-done.34) | copy-start | bytes 1156
  218.9 1.0 copy-start.11
  231.6 1.1 copy-start.5
  232.6 0.8 copy-start.38
  233.4 5.4 %copy-start.39 = (bf16[96,24,128]{2,1,0:T(8,128)(2,1)S(1)}, bf16[96,24,128]{2,1,0:T(8,128)(2,1)}, u32[]{:S(2)}) copy-start(bf16[96,24,128]{2,1,0:T(8,128)(2,1)} %copy-done.38) | copy-start | bytes 1769476
  233.4 54.2 %all-to-all-start.6 = ((bf16[16,528,128]{2,1,0:T(8,128)(2,1)}), bf16[16,528,128]{2,1,0:T(8,128)(2,1)S(1)}, u32[]{:S(2)}, u32[]{:S(2)}) async-start(bf16[16,528,128]{2,1,0:T(8,128)(2,1)} %bitcast.199), calls=%async_computation.6 | async-start | bytes 4325376 | tf_op jit(solution)/shard_map/all_to_all | solution.py:947
  238.8 1.3 copy-start.9
  287.6 1.3 copy-start.6

commit v4 on v3

--- a/solution.py
+++ b/solution.py
@@ -8,6 +8,7 @@
 
 FACE_TILES = 8
 RIM_TILES = 12
+SIDE = 4
 VMEM_LIMIT = 50 * 2**20
 BF = jnp.bfloat16
 F32 = jnp.float32
@@ -205,7 +206,7 @@
 
 
 def each_tile(tiles, body):
-    side = group_of(tiles, 3)
+    side = group_of(tiles, SIDE)
 
     def step(i, carry):
         for k in range(side):
@@ -340,7 +341,7 @@
     ring_ref = next(it) if nxt == "shrink" else None
     skip_ref, wn_ref = (next(it), next(it)) if nxt == "halo" else (None, None)
     rim_ref, next_ref, send_ref = next(it), next(it), next(it)
-    halo_ref, lhs_ref, con_ref = next(it), next(it), next(it)
+    lhs_ref, con_ref = next(it), next(it)
     edge_buf, ring_buf, sum_buf, out_buf = next(it), next(it), next(it), next(it)
     lhsn_ref, conn_ref, taps_ref, big_buf = [next(it) for _ in range(4)] if nxt == "halo" else [None] * 4
 
@@ -350,36 +351,23 @@
 
     if strips_in:
 
-        def fetch(t, k):
-            for e in range(4):
-                i = t * 4 + e
-                halo_ref[i] = incoming(pick_ref, recv_ref, own_ref, i).astype(BF)
-
-        each_tile(tiles, fetch)
-
-        def turn(four):
-            halos = [turned(rev_ref, i, halo_ref[i], flip, keep).astype(BF) for i in four]
-            for i, h in zip(four, halos):
-                halo_ref[i] = h
-
-        each_four(odd_ref, turn)
-
         def fill(t, k):
             for e in range(4):
-                put_shifts(lhs_ref, (e, t), 0, halo_ref[t * 4 + e].astype(F32), n)
+                put_shifts(lhs_ref, (e, t), 0, incoming(pick_ref, recv_ref, own_ref, t * 4 + e), n)
 
         each_tile(tiles, fill)
+
+        def turn(four):
+            halos = [lhs_ref[i % 4, i // 4, :, 128:256] for i in four]
+            halos = [turned(rev_ref, i, h, flip, keep) for i, h in zip(four, halos)]
+            for i, h in zip(four, halos):
+                put_shifts(lhs_ref, (i % 4, i // 4), 0, h, n)
+
+        each_four(odd_ref, turn)
         for e in range(4):
-            lhs = lhs_ref[e].reshape(tiles * lp, 384).astype(BF)
+            lhs = lhs_ref[e, 0:tiles].reshape(tiles * lp, 384).astype(BF)
             out = jnp.dot(lhs, edge_taps(w_ref, e, 0), preferred_element_type=F32)
             con_ref[e] = out.reshape(tiles, lp, 128)
-    else:
-
-        def fill(t, k):
-            for e in range(4):
-                con_ref[e, t] = incoming(pick_ref, recv_ref, own_ref, t * 4 + e)
-
-        each_tile(tiles, fill)
 
     end = n - 1
     joints = (
@@ -390,11 +378,15 @@
         out_buf[...] = jnp.zeros_like(out_buf)
 
     def finish(t, k):
+        if strips_in:
+            con = [con_ref[e, t] for e in range(4)]
+        else:
+            con = [incoming(pick_ref, recv_ref, own_ref, t * 4 + e) for e in range(4)]
         for e in range(4):
-            edge_buf[k, e] = sum_ref[t * 4 + e] + con_ref[e, t]
+            edge_buf[k, e] = sum_ref[t * 4 + e] + con[e]
         for e, cell, other, at in corners(end):
             cells = slice(cell, cell + 1)
-            edge_buf[k, e, cells] = edge_buf[k, e, cells] + con_ref[other, t, at : at + 1]
+            edge_buf[k, e, cells] = edge_buf[k, e, cells] + con[other][at : at + 1]
         for e in range(4):
             y = silu(edge_buf[k, e]).astype(BF)
             rim_ref[t * 4 + e] = y
@@ -450,7 +442,7 @@
 def rim_step(n, devices, cap, plan, recv, own, sums, w=None, ring=None, skip=None, wn=None):
     strips, lp, c = own.shape
     tiles = strips // 4
-    side = group_of(tiles, 3)
+    side = group_of(tiles, SIDE)
     nxt = "shrink" if ring is not None else "halo"
     smem = pl.BlockSpec(memory_space=pltpu.SMEM)
     vmem = pl.BlockSpec(memory_space=pltpu.VMEM)
@@ -464,8 +456,7 @@
         jax.ShapeDtypeStruct(send_shape(devices, cap, lo) + (c,), BF),
     ]
     scratch = [
-        pltpu.VMEM((strips + 1, lp, 128), BF),
-        pltpu.VMEM((4, tiles, lp, 384), wide(lp)),
+        pltpu.VMEM((4, tiles + 1, lp, 384), wide(lp)),
         pltpu.VMEM((4, tiles, lp, 128), F32),
         pltpu.VMEM((side, 4, lp, 128), F32),
         pltpu.VMEM((side, 4, lp, 128), F32),
@@ -790,7 +781,7 @@
         out_shape=jax.ShapeDtypeStruct(x.shape, BF),
         scratch_shapes=[
             pltpu.VMEM((tiles, 4, n, c), BF),
-            pltpu.VMEM((group_of(tiles, 3), 4, n, c), F32),
+            pltpu.VMEM((group_of(tiles, SIDE), 4, n, c), F32),
             pltpu.VMEM((2, tiles, n, 16, c), BF),
             pltpu.VMEM((n * 8, c), F32),
             pltpu.SemaphoreType.DMA((2, parts)),

time: 300 us -> 303 us (1.010)
  starting transfers between devices: 38.8 us -> 43.6 us
    all_to_all x7, starting transfers between devices: 38.8 us -> 43.6 us  [trade(): lax.all_to_all(strips.reshape(devices, -1, 128), 'tile', split_axis=0, co...]
where the time goes in v4:
time: 303 us; the launch traced here: 302 us
  Pallas kernels  170 us (56%)
  starting transfers between devices  43.6 us (14%)
  local copies, waits for them, and re-layouts  36.5 us (12%)
  waiting for transfers between devices  33.8 us (11%)
  matrix products  9.34 us (3%)
  other arithmetic  7 us (2%)
    pallas_call x2, Pallas kernels, dec_conv(): pl.pallas_call(kernel, grid=(tiles // g,), in_specs=specs, out_specs=[til...  60.5 us
    pallas_call x2, Pallas kernels, enc_conv(): pl.pallas_call(enc_kernel, grid=(tiles // g,), in_specs=specs, out_specs=...  49.6 us
    all_to_all x7, starting transfers between devices, trade(): lax.all_to_all(strips.reshape(devices, -1, 128), 'tile', split_axis=0, co...  43.6 us
    pallas_call x6, Pallas kernels, rim_step(): pl.pallas_call(kernel, in_specs=[smem] * 6 + [vmem] * len(args), out_spec...  34.3 us
    all_to_all x7, waiting for transfers between devices, trade(): lax.all_to_all(strips.reshape(devices, -1, 128), 'tile', split_axis=0, co...  33.8 us
    unnamed x118, local copies, waits for them, and re-layouts  27.2 us
    pallas_call x3, Pallas kernels, skip_step(): pl.pallas_call(lambda *refs: skip_kernel(n, *refs), in_specs=[smem, smem,...  10.6 us
    pallas_call x1, Pallas kernels, last_step(): pl.pallas_call(last_kernel, in_specs=[smem, vmem, vmem, vmem, anywhere],...  9.16 us
  transfers between devices with their start and end apart: 7, of which 6 were waited for; matrix products, arithmetic and copies ran while one was open for 9% of the time, Pallas kernels for 40%

profile of v4, /device:TPU:15, one launch (start us, length us, event | category | flops | bytes accessed | tf_op | source)
XLA Modules:
  0.0 301.7 jit_solution(17552892557633866740)
XLA Ops:
  0.0 0.8 constant_dynamic-slice_fusion.1
  1.2 6.2 %tile_rims.1 = (bf16[24,4,48,128]{3,2,1,0:T(8,128)(2,1)S(1)}, bf16[176,48,128]{2,1,0:T(8,128)(2,1)}) custom-call(s32[96]{0:T(128)S(1)} %compare_select_fusion.4.slot_ref.refs_2_, bf16[24,48,48,128]{3,2,1,0:T(8,128)(2,1)} %refs_0_.1, bf16[24,48,48,128]{3,2,1,0:T(8,128)(2,1)} %refs_0_.1, bf16[24,48,48,128]{3,2,1,0:T(8,128)(2,1)} %refs_0_.1, ...), custom_call_target="tpu_custom_call" | custom-call | tf_op jit(solution)/shard_map/tile_rims/pallas_call | solution.py:161
  7.4 1.0 copy-done.10
  8.5 6.7 %all-to-all-start = ((bf16[16,528,128]{2,1,0:T(8,128)(2,1)}), bf16[16,528,128]{2,1,0:T(8,128)(2,1)S(1)}, u32[]{:S(2)}, u32[]{:S(2)}) async-start(bf16[16,528,128]{2,1,0:T(8,128)(2,1)} %bitcast.11), calls=%async_computation | async-start | bytes 4325376 | tf_op jit(solution)/shard_map/all_to_all | solution.py:938
  17.7 1.3 compare_select_fusion.2
  19.0 1.3 fusion.46
  20.3 34.6 %enc_conv.2 = (bf16[24,24,2,48,128]{4,3,2,1,0:T(8,128)(2,1)}, f32[24,4,48,128]{3,2,1,0:T(8,128)S(1)}, bf16[24,4,48,128]{3,2,1,0:T(8,128)(2,1)S(1)}, bf16[24,24,24,128]{3,2,1,0:T(8,128)(2,1)}) custom-call(bf16[24,48,48,128]{3,2,1,0:T(8,128)(2,1)} %refs_0_.1, bf16[9,128,128]{2,1,0:T(8,128)(2,1)S(1)} %bitcast.185), custom_call_target="tpu_custom_call" | custom-call | flops 21743271936 | bytes 33177600 | tf_op jit(solution)/shard_map/enc_conv/pallas_call | solution.py:818
  54.9 1.4 copy-done.4
  56.2 1.0 copy-done.12
  57.3 6.7 %all-to-all-done = bf16[16,528,128]{2,1,0:T(8,128)(2,1)S(1)} async-done(((bf16[16,528,128]{2,1,0:T(8,128)(2,1)}), bf16[16,528,128]{2,1,0:T(8,128)(2,1)S(1)}, u32[]{:S(2)}, u32[]{:S(2)}) %all-to-all-start) | async-done | bytes 2162720 | tf_op jit(solution)/shard_map/all_to_all | solution.py:938
  64.0 1.4 copy-done.40
  65.3 8.1 %rim_step.6 = (bf16[96,48,128]{2,1,0:T(8,128)(2,1)S(1)}, bf16[96,24,128]{2,1,0:T(8,128)(2,1)S(1)}, bf16[176,24,128]{2,1,0:T(8,128)(2,1)}) custom-call(s32[96]{0:T(128)S(1)} %get-tuple-element.130.refs_0_.pick_ref, s32[97]{0:T(128)S(1)} %get-tuple-element.137.refs_1_.refs_0_, s32[96]{0:T(128)S(1)} %compare_select_fusion.4.slot_ref.refs_2_, ...), custom_call_target="tpu_custom_call" | custom-call | flops 1811939328 | bytes 6912000 | tf_op jit(solution)/shard_map/rim_step/pallas_call | solution.py:477
  73.4 1.1 copy-done.7
  74.6 5.5 %all-to-all-start.1 = ((bf16[16,264,128]{2,1,0:T(8,128)(2,1)}), bf16[16,264,128]{2,1,0:T(8,128)(2,1)S(1)}, u32[]{:S(2)}, u32[]{:S(2)}) async-start(bf16[16,264,128]{2,1,0:T(8,128)(2,1)} %bitcast.17), calls=%async_computation.1 | async-start | bytes 2162688 | tf_op jit(solution)/shard_map/all_to_all | solution.py:938
  80.1 15.0 %enc_conv.3 = (bf16[24,12,2,24,128]{4,3,2,1,0:T(8,128)(2,1)}, f32[24,4,24,128]{3,2,1,0:T(8,128)S(1)}, bf16[24,4,24,128]{3,2,1,0:T(8,128)(2,1)S(1)}, bf16[24,12,12,128]{3,2,1,0:T(8,128)(2,1)S(1)}) custom-call(bf16[24,24,24,128]{3,2,1,0:T(8,128)(2,1)} %get-tuple-element.49.refs_0_, bf16[9,128,128]{2,1,0:T(8,128)(2,1)S(1)} %bitcast.189, ...), custom_call_target="tpu_custom_call" | custom-call | flops 5435817984 | bytes 8294400 | tf_op jit(solution)/shard_map/enc_conv/pallas_call | solution.py:818
  95.1 1.0 copy-done.13
  96.2 1.4 slice.167
  97.6 8.2 %all-to-all-done.1 = bf16[16,264,128]{2,1,0:T(8,128)(2,1)S(1)} async-done(((bf16[16,264,128]{2,1,0:T(8,128)(2,1)}), bf16[16,264,128]{2,1,0:T(8,128)(2,1)S(1)}, u32[]{:S(2)}, u32[]{:S(2)}) %all-to-all-start.1) | async-done | bytes 1081376 | tf_op jit(solution)/shard_map/all_to_all | solution.py:938
  105.8 1.0 copy-done.41
  106.8 5.3 %rim_step.7 = (bf16[96,24,128]{2,1,0:T(8,128)(2,1)S(1)}, bf16[96,16,128]{2,1,0:T(8,128)(2,1)S(1)}, bf16[96,24,128]{2,1,0:T(8,128)(2,1)}) custom-call(s32[96]{0:T(128)S(1)} %get-tuple-element.130.refs_0_.pick_ref, s32[97]{0:T(128)S(1)} %get-tuple-element.137.refs_1_.refs_0_, s32[96]{0:T(128)S(1)} %get-tuple-element.79.refs_2_, ...), custom_call_target="tpu_custom_call" | custom-call | flops 905969664 | bytes 3456000 | tf_op jit(solution)/shard_map/rim_step/pallas_call | solution.py:477
  112.1 0.8 copy-done.17
  113.0 5.5 %all-to-all-start.2 = ((bf16[16,144,128]{2,1,0:T(8,128)(2,1)}), bf16[16,144,128]{2,1,0:T(8,128)(2,1)S(1)}, u32[]{:S(2)}, u32[]{:S(2)}) async-start(bf16[16,144,128]{2,1,0:T(8,128)(2,1)} %bitcast.23), calls=%async_computation.2 | async-start | bytes 1179648 | tf_op jit(solution)/shard_map/all_to_all | solution.py:938
  118.7 0.7 pad_maximum_fusion
  119.5 2.6 multiply_convert_fusion
  122.1 0.9 slice.232
  124.3 9.2 %all-to-all-done.2 = bf16[16,144,128]{2,1,0:T(8,128)(2,1)S(1)} async-done(((bf16[16,144,128]{2,1,0:T(8,128)(2,1)}), bf16[16,144,128]{2,1,0:T(8,128)(2,1)S(1)}, u32[]{:S(2)}, u32[]{:S(2)}) %all-to-all-start.2) | async-done | bytes 589856 | tf_op jit(solution)/shard_map/all_to_all | solution.py:938
  133.6 1.0 copy-done.27
  134.5 3.0 %rim_step.8 = (bf16[96,16,128]{2,1,0:T(8,128)(2,1)S(1)}, bf16[96,8,128]{2,1,0:T(8,128)(2,1)S(1)}, bf16[176,8,128]{2,1,0:T(8,128)(2,1)S(1)}) custom-call(s32[96]{0:T(128)S(1)} %get-tuple-element.82.refs_0_, s32[97]{0:T(128)S(1)} %get-tuple-element.137.refs_1_.refs_0_, s32[96]{0:T(128)S(1)} %compare_select_fusion.4.slot_ref.refs_2_, ...), custom_call_target="tpu_custom_call" | custom-call | flops 603979776 | bytes 2304000 | tf_op jit(solution)/shard_map/rim_step/pallas_call | solution.py:477
  137.6 0.7 copy-done.24
  138.4 0.7 copy-done.14
  139.8 5.4 %all-to-all-start.3 = ((bf16[16,88,128]{2,1,0:T(8,128)(2,1)}), bf16[16,88,128]{2,1,0:T(8,128)(2,1)S(1)}, u32[]{:S(2)}, u32[]{:S(2)}) async-start(bf16[16,88,128]{2,1,0:T(8,128)(2,1)} %bitcast.184), calls=%async_computation.3 | async-start | bytes 720896 | tf_op jit(solution)/shard_map/all_to_all | solution.py:938
  145.3 5.3 %skip_step.3.refs_9_ = f32[96,48,128]{2,1,0:T(8,128)} custom-call(s32[97]{0:T(128)S(1)} %get-tuple-element.137.refs_1_.refs_0_, s32[97]{0:T(128)S(1)} %get-tuple-element.136.refs_3_.refs_1_, s32[100]{0:T(128)S(1)} %get-tuple-element.127.refs_5_.refs_2_, bf16[96,48,128]{2,1,0:T(8,128)(2,1)S(1)} %copy-done.8, bf16[9,256,128]{2,1,0:T(8,128)(2,1)S(1)} %bitcast.153), custom_call_target="tpu_custom_call" | custom-call | flops 905969664 | bytes 3538944 | tf_op jit(solution)/shard_map/skip_step/pallas_call | solution.py:313
  150.6 0.7 fusion.19
  154.1 2.6 skip_step.4.refs_10_
  156.8 1.0 copy-done.29
  157.8 4.5 %rim_step.9 = (bf16[96,8,128]{2,1,0:T(8,128)(2,1)S(1)}, bf16[96,16,128]{2,1,0:T(8,128)(2,1)S(1)}, bf16[96,24,128]{2,1,0:T(8,128)(2,1)S(1)}) custom-call(s32[96]{0:T(128)S(1)} %get-tuple-element.130.refs_0_.pick_ref, s32[97]{0:T(128)S(1)} %get-tuple-element.137.refs_1_.refs_0_, s32[96]{0:T(128)S(1)} %get-tuple-element.79.refs_2_, ...), custom_call_target="tpu_custom_call" | custom-call | flops 301989888 | bytes 1152000 | tf_op jit(solution)/shard_map/rim_step/pallas_call | solution.py:477
  162.2 0.8 copy-done.16
  163.1 0.8 copy-done.20
  163.9 8.5 %all-to-all-start.4 = ((bf16[16,144,128]{2,1,0:T(8,128)(2,1)}), bf16[16,144,128]{2,1,0:T(8,128)(2,1)S(1)}, u32[]{:S(2)}, u32[]{:S(2)}) async-start(bf16[16,144,128]{2,1,0:T(8,128)(2,1)} %bitcast.178), calls=%async_computation.4 | async-start | bytes 1179648 | tf_op jit(solution)/shard_map/all_to_all | solution.py:938
  172.8 0.7 copy-done.43
  173.5 5.7 %fusion.4 = f32[24,12,12,128]{3,0,2,1:T(8,128)} fusion(bf16[3,3,256,128]{3,2,1,0:T(8,128)(2,1)S(1)} %copy-done.2, bf16[24,1,12,128]{3,0,2,1:T(8,128)(2,1)S(1)} %copy-done.47, bf16[24,10,1,128]{3,0,2,1:T(8,128)(2,1)S(1)} %bitcast.206, bf16[24,10,10,128]{3,0,2,1:T(8,128)(2,1)S(1)} %copy-done.43, bf16[24,10,1,128]{3,0,2,1:T(8,128)(2,1)S(1)} %bitcast.205, ...), kind=kOutput, calls=%fused_computation.6 | convolution fusion | flops 1828847616 | bytes 4128768 | tf_op jit(solution)/shard_map/conv_general_dilated | solution.py:909
  179.2 1.0 slice_bitcast_fusion.1
  180.2 1.0 fusion.61
  181.4 0.8 copy-done.3
  182.5 2.8 skip_step.5.refs_9_
  185.2 1.0 copy-done
  186.3 1.2 all-to-all-done.4
  188.7 5.6 %rim_step.10 = (bf16[96,16,128]{2,1,0:T(8,128)(2,1)S(1)}, bf16[96,24,128]{2,1,0:T(8,128)(2,1)S(1)}, bf16[176,24,128]{2,1,0:T(8,128)(2,1)}) custom-call(s32[96]{0:T(128)S(1)} %copy-done.37, s32[97]{0:T(128)S(1)} %get-tuple-element.137.refs_1_.refs_0_, s32[96]{0:T(128)S(1)} %copy-done.32, s32[97]{0:T(128)S(1)} %get-tuple-element.136.refs_3_.refs_1_, ...), custom_call_target="tpu_custom_call" | custom-call | flops 603979776 | bytes 2304000 | tf_op jit(solution)/shard_map/rim_step/pallas_call | solution.py:477
  194.2 0.7 copy-done.22
  195.0 6.2 %all-to-all-start.5 = ((bf16[16,264,128]{2,1,0:T(8,128)(2,1)}), bf16[16,264,128]{2,1,0:T(8,128)(2,1)S(1)}, u32[]{:S(2)}, u32[]{:S(2)}) async-start(bf16[16,264,128]{2,1,0:T(8,128)(2,1)} %bitcast.201), calls=%async_computation.5 | async-start | bytes 2162688 | tf_op jit(solution)/shard_map/all_to_all | solution.py:938
  201.2 1.4 slice.241
  203.4 0.7 pad_maximum_fusion.1.refs_2_
  204.3 17.9 %dec_conv.2 = (bf16[24,12,2,24,128]{4,3,2,1,0:T(8,128)(2,1)}, f32[24,4,24,128]{3,2,1,0:T(8,128)S(1)}) custom-call(bf16[24,24,24,128]{3,2,1,0:T(8,128)(2,1)} %bitcast.210, bf16[24,4,24,128]{3,2,1,0:T(8,128)(2,1)S(1)} %bitcast.179, bf16[24,12,12,128]{3,2,1,0:T(8,128)(2,1)S(1)} %pad_maximum_fusion.1.refs_2_, bf16[9,256,128]{2,1,0:T(8,128)(2,1)S(1)} %bitcast.161), custom_call_target="tpu_custom_call" | custom-call | flops 8139571200 | bytes 8294400 | tf_op jit(solution)/shard_map/dec_conv/pallas_call | solution.py:865
  222.1 1.0 copy-done.11
  223.2 3.6 %all-to-all-done.5 = bf16[16,264,128]{2,1,0:T(8,128)(2,1)S(1)} async-done(((bf16[16,264,128]{2,1,0:T(8,128)(2,1)}), bf16[16,264,128]{2,1,0:T(8,128)(2,1)S(1)}, u32[]{:S(2)}, u32[]{:S(2)}) %all-to-all-start.5) | async-done | bytes 1081376 | tf_op jit(solution)/shard_map/all_to_all | solution.py:938
  226.8 7.8 %rim_step.11 = (bf16[96,24,128]{2,1,0:T(8,128)(2,1)S(1)}, bf16[96,48,128]{2,1,0:T(8,128)(2,1)S(1)}, bf16[176,48,128]{2,1,0:T(8,128)(2,1)}) custom-call(s32[96]{0:T(128)S(1)} %copy-done.35, s32[97]{0:T(128)S(1)} %get-tuple-element.137.refs_1_.refs_0_, s32[96]{0:T(128)S(1)} %copy-done.33, s32[97]{0:T(128)S(1)} %get-tuple-element.136.refs_3_.refs_1_, ...), custom_call_target="tpu_custom_call" | custom-call | flops 905969664 | bytes 3456000 | tf_op jit(solution)/shard_map/rim_step/pallas_call | solution.py:477
  234.6 1.1 copy-done.5
  235.6 0.8 copy-done.38
  236.4 5.8 %all-to-all-start.6 = ((bf16[16,528,128]{2,1,0:T(8,128)(2,1)}), bf16[16,528,128]{2,1,0:T(8,128)(2,1)S(1)}, u32[]{:S(2)}, u32[]{:S(2)}) async-start(bf16[16,528,128]{2,1,0:T(8,128)(2,1)} %bitcast.199), calls=%async_computation.6 | async-start | bytes 4325376 | tf_op jit(solution)/shard_map/all_to_all | solution.py:938
  242.3 1.3 copy-done.9
  243.5 42.6 %dec_conv.3 = (bf16[24,24,2,48,128]{4,3,2,1,0:T(8,128)(2,1)}, f32[24,4,48,128]{3,2,1,0:T(8,128)}) custom-call(bf16[24,48,48,128]{3,2,1,0:T(8,128)(2,1)} %bitcast.209, bf16[24,4,48,128]{3,2,1,0:T(8,128)(2,1)S(1)} %bitcast.171, bf16[24,24,24,128]{3,2,1,0:T(8,128)(2,1)} %bitcast.211, bf16[24,4,24,128]{3,2,1,0:T(8,128)(2,1)S(1)} %bitcast.193, ...), custom_call_target="tpu_custom_call" | custom-call | flops 32558284800 | bytes 33177600 | tf_op jit(solution)/shard_map/dec_conv/pallas_call | solution.py:865
  286.1 5.0 %all-to-all-done.6 = bf16[16,528,128]{2,1,0:T(8,128)(2,1)S(1)} async-done(((bf16[16,528,128]{2,1,0:T(8,128)(2,1)}), bf16[16,528,128]{2,1,0:T(8,128)(2,1)S(1)}, u32[]{:S(2)}, u32[]{:S(2)}) %all-to-all-start.6) | async-done | bytes 2162720 | tf_op jit(solution)/shard_map/all_to_all | solution.py:938
  291.1 1.3 copy-done.6
  292.4 9.2 %last_step.1 = bf16[24,48,48,128]{3,2,1,0:T(8,128)(2,1)} custom-call(s32[96]{0:T(128)S(1)} %copy-done.35, bf16[176,48,128]{2,1,0:T(8,128)(2,1)S(1)} %bitcast.149, bf16[96,48,128]{2,1,0:T(8,128)(2,1)S(1)} %copy-done.6, f32[96,48,128]{2,1,0:T(8,128)} %bitcast.198, bf16[24,48,48,128]{3,2,1,0:T(8,128)(2,1)} %bitcast.194), custom_call_target="tpu_custom_call", output_to_operand_aliasing={{}: (4, {})} | custom-call | tf_op jit(solution)/shard_map/last_step/pallas_call | solution.py:777
  (159 shorter events, 10.9 us)
Async XLA Ops:
  1.2 132.4 %copy-start.31 = (s32[96]{0:T(128)}, s32[96]{0:T(128)S(1)}, u32[]{:S(2)}) copy-start(s32[96]{0:T(128)S(1)} %compare_select_fusion.4.slot_ref.refs_2_) | copy-start | bytes 1156
  7.4 1.0 copy-start.10
  8.5 6.7 %copy-start.50 = (s32[384,4,2]{0,2,1:T(2,128)S(1)}, s32[384,4,2]{0,2,1:T(2,128)}, u32[]{:S(2)}) copy-start(s32[384,4,2]{0,2,1:T(2,128)} %param.10) | copy-start | bytes 36868
  8.5 11.8 %copy-start.25 = (bf16[3,3,128,128]{3,2,1,0:T(8,128)(2,1)S(1)}, bf16[3,3,128,128]{3,2,1,0:T(8,128)(2,1)}, u32[]{:S(2)}) copy-start(bf16[3,3,128,128]{3,2,1,0:T(8,128)(2,1)} %param.11) | copy-start | bytes 884740
  8.5 55.5 %all-to-all-start = ((bf16[16,528,128]{2,1,0:T(8,128)(2,1)}), bf16[16,528,128]{2,1,0:T(8,128)(2,1)S(1)}, u32[]{:S(2)}, u32[]{:S(2)}) async-start(bf16[16,528,128]{2,1,0:T(8,128)(2,1)} %bitcast.11), calls=%async_computation | async-start | bytes 4325376 | tf_op jit(solution)/shard_map/all_to_all | solution.py:938
  16.5 117.1 %copy-start.36 = (s32[96]{0:T(128)}, s32[96]{0:T(128)S(1)}, u32[]{:S(2)}) copy-start(s32[96]{0:T(128)S(1)} %get-tuple-element.82.refs_0_) | copy-start | bytes 1156
  17.1 139.7 %copy-start.34 = (s32[96]{0:T(128)}, s32[96]{0:T(128)S(1)}, u32[]{:S(2)}) copy-start(s32[96]{0:T(128)S(1)} %get-tuple-element.130.refs_0_.pick_ref) | copy-start | bytes 1156
  54.9 1.4 copy-start.4
  56.2 1.0 copy-start.12
  64.0 1.4 copy-start.40
  73.4 1.1 copy-start.7
  74.6 5.5 %copy-start.30 = (bf16[3,3,128,128]{3,2,1,0:T(8,128)(2,1)S(1)}, bf16[3,3,128,128]{3,2,1,0:T(8,128)(2,1)}, u32[]{:S(2)}) copy-start(bf16[3,3,128,128]{3,2,1,0:T(8,128)(2,1)} %param.12) | copy-start | bytes 884740
  74.6 31.2 %all-to-all-start.1 = ((bf16[16,264,128]{2,1,0:T(8,128)(2,1)}), bf16[16,264,128]{2,1,0:T(8,128)(2,1)S(1)}, u32[]{:S(2)}, u32[]{:S(2)}) async-start(bf16[16,264,128]{2,1,0:T(8,128)(2,1)} %bitcast.17), calls=%async_computation.1 | async-start | bytes 2162688 | tf_op jit(solution)/shard_map/all_to_all | solution.py:938
  95.1 1.0 copy-start.13
  105.8 1.0 copy-start.41
  112.1 0.8 copy-start.17
  112.9 5.8 %copy-start.42 = (bf16[24,10,10,128]{3,2,1,0:T(8,128)(2,1)S(1)}, bf16[24,10,10,128]{3,2,1,0:T(8,128)(2,1)}, u32[]{:S(2)}) copy-start(bf16[24,10,10,128]{3,2,1,0:T(8,128)(2,1)} %slice.167) | copy-start | bytes 1843204
  113.0 20.5 %all-to-all-start.2 = ((bf16[16,144,128]{2,1,0:T(8,128)(2,1)}), bf16[16,144,128]{2,1,0:T(8,128)(2,1)S(1)}, u32[]{:S(2)}, u32[]{:S(2)}) async-start(bf16[16,144,128]{2,1,0:T(8,128)(2,1)} %bitcast.23), calls=%async_computation.2 | async-start | bytes 1179648 | tf_op jit(solution)/shard_map/all_to_all | solution.py:938
  118.5 1.0 copy-start.26
  133.6 1.0 copy-start.27
  134.5 10.7 %copy-start.1 = (bf16[3,3,256,128]{3,2,1,0:T(8,128)(2,1)S(1)}, bf16[3,3,256,128]{3,2,1,0:T(8,128)(2,1)}, u32[]{:S(2)}) copy-start(bf16[3,3,256,128]{3,2,1,0:T(8,128)(2,1)} %param.17) | copy-start | bytes 1769476
  137.6 0.7 copy-start.24
  138.3 6.9 %copy-start.8 = (bf16[96,48,128]{2,1,0:T(8,128)(2,1)S(1)}, bf16[96,48,128]{2,1,0:T(8,128)(2,1)}, u32[]{:S(2)}) copy-start(bf16[96,48,128]{2,1,0:T(8,128)(2,1)} %copy-done.7) | copy-start | bytes 3538948
  138.4 0.7 copy-start.14
  139.8 17.0 %all-to-all-start.3 = ((bf16[16,88,128]{2,1,0:T(8,128)(2,1)}), bf16[16,88,128]{2,1,0:T(8,128)(2,1)S(1)}, u32[]{:S(2)}, u32[]{:S(2)}) async-start(bf16[16,88,128]{2,1,0:T(8,128)(2,1)} %bitcast.184), calls=%async_computation.3 | async-start | bytes 720896 | tf_op jit(solution)/shard_map/all_to_all | solution.py:938
  145.2 5.3 %copy-start.28 = (bf16[3,3,128,128]{3,2,1,0:T(8,128)(2,1)S(1)}, bf16[3,3,128,128]{3,2,1,0:T(8,128)(2,1)}, u32[]{:S(2)}) copy-start(bf16[3,3,128,128]{3,2,1,0:T(8,128)(2,1)} %param.14) | copy-start | bytes 884740
  145.2 5.3 %copy-start.45 = (bf16[24,4,4,128]{3,0,2,1:T(8,128)(2,1)S(1)}, bf16[24,4,4,128]{3,0,2,1:T(8,128)(2,1)}, u32[]{:S(2)}) copy-start(bf16[24,4,4,128]{3,0,2,1:T(8,128)(2,1)} %fusion.29) | copy-start | bytes 294916
  145.3 6.1 %copy-start.44 = (bf16[24,1,12,128]{3,2,1,0:T(8,128)(2,1)S(1)}, bf16[24,1,12,128]{3,2,1,0:T(8,128)(2,1)}, u32[]{:S(2)}) copy-start(bf16[24,1,12,128]{3,2,1,0:T(8,128)(2,1)} %get-tuple-element.109) | copy-start | bytes 221188
  151.3 2.8 copy-start.2
  154.0 2.8 copy-start.15
  156.8 1.0 copy-start.29
  162.2 0.8 copy-start.16
  163.1 0.8 copy-start.20
  163.9 8.8 %copy-start.46 = (bf16[24,1,12,128]{3,0,2,1:T(8,128)(2,1)S(1)}, bf16[24,1,12,128]{3,0,2,1:T(8,128)(2,1)}, u32[]{:S(2)}) copy-start(bf16[24,1,12,128]{3,0,2,1:T(8,128)(2,1)} %copy.155) | copy-start | bytes 221188
  163.9 8.8 %copy-start.47 = (bf16[24,1,12,128]{3,0,2,1:T(8,128)(2,1)S(1)}, bf16[24,1,12,128]{3,0,2,1:T(8,128)(2,1)}, u32[]{:S(2)}) copy-start(bf16[24,1,12,128]{3,0,2,1:T(8,128)(2,1)} %copy.158) | copy-start | bytes 221188
  163.9 8.8 %copy-start.48 = (bf16[24,1,10,128]{3,0,2,1:T(8,128)(2,1)S(1)}, bf16[24,1,10,128]{3,0,2,1:T(8,128)(2,1)}, u32[]{:S(2)}) copy-start(bf16[24,1,10,128]{3,0,2,1:T(8,128)(2,1)} %copy.190) | copy-start | bytes 184324
  163.9 23.5 %all-to-all-start.4 = ((bf16[16,144,128]{2,1,0:T(8,128)(2,1)}), bf16[16,144,128]{2,1,0:T(8,128)(2,1)S(1)}, u32[]{:S(2)}, u32[]{:S(2)}) async-start(bf16[16,144,128]{2,1,0:T(8,128)(2,1)} %bitcast.178), calls=%async_computation.4 | async-start | bytes 1179648 | tf_op jit(solution)/shard_map/all_to_all | solution.py:938
  172.4 1.1 copy-start.43
  172.4 1.1 copy-start.49
  181.2 1.1 copy-start.3
  181.2 1.2 copy-start.18
  181.4 6.1 %copy-start.21 = (bf16[96,16,128]{2,1,0:T(8,128)(2,1)S(1)}, bf16[96,16,128]{2,1,0:T(8,128)(2,1)}, u32[]{:S(2)}) copy-start(bf16[96,16,128]{2,1,0:T(8,128)(2,1)} %copy-done.20) | copy-start | bytes 1179652
  185.2 1.0 copy-start
  187.4 0.6 copy-start.32
  188.0 0.6 copy-start.37
  194.2 0.7 copy-start.22
  195.0 31.8 %all-to-all-start.5 = ((bf16[16,264,128]{2,1,0:T(8,128)(2,1)}), bf16[16,264,128]{2,1,0:T(8,128)(2,1)S(1)}, u32[]{:S(2)}, u32[]{:S(2)}) async-start(bf16[16,264,128]{2,1,0:T(8,128)(2,1)} %bitcast.201), calls=%async_computation.5 | async-start | bytes 2162688 | tf_op jit(solution)/shard_map/all_to_all | solution.py:938
  201.2 2.0 copy-start.23
  203.2 1.1 copy-start.19
  204.3 22.5 %copy-start.33 = (s32[96]{0:T(128)S(1)}, s32[96]{0:T(128)}, u32[]{:S(2)}) copy-start(s32[96]{0:T(128)} %copy-done.31) | copy-start | bytes 1156
  204.3 22.5 %copy-start.35 = (s32[96]{0:T(128)S(1)}, s32[96]{0:T(128)}, u32[]{:S(2)}) copy-start(s32[96]{0:T(128)} %copy-done.34) | copy-start | bytes 1156
  222.1 1.0 copy-start.11
  234.6 1.1 copy-start.5
  235.6 0.8 copy-start.38
  236.4 5.8 %copy-start.39 = (bf16[96,24,128]{2,1,0:T(8,128)(2,1)S(1)}, bf16[96,24,128]{2,1,0:T(8,128)(2,1)}, u32[]{:S(2)}) copy-start(bf16[96,24,128]{2,1,0:T(8,128)(2,1)} %copy-done.38) | copy-start | bytes 1769476
  236.4 54.6 %all-to-all-start.6 = ((bf16[16,528,128]{2,1,0:T(8,128)(2,1)}), bf16[16,528,128]{2,1,0:T(8,128)(2,1)S(1)}, u32[]{:S(2)}, u32[]{:S(2)}) async-start(bf16[16,528,128]{2,1,0:T(8,128)(2,1)} %bitcast.199), calls=%async_computation.6 | async-start | bytes 4325376 | tf_op jit(solution)/shard_map/all_to_all | solution.py:938
  242.3 1.3 copy-start.9
  291.1 1.3 copy-start.6

commit v5 on v4

--- a/solution.py
+++ b/solution.py
@@ -8,7 +8,7 @@
 
 FACE_TILES = 8
 RIM_TILES = 12
-SIDE = 4
+SIDE = 6
 VMEM_LIMIT = 50 * 2**20
 BF = jnp.bfloat16
 F32 = jnp.float32

time: 303 us -> 302 us (level)
  Pallas kernels: 170 us -> 165 us
  starting transfers between devices: 43.6 us -> 46.9 us
    pallas_call x6, Pallas kernels: 34.3 us -> 30.9 us  [rim_step(): pl.pallas_call(kernel, in_specs=[smem] * 6 + [vmem] * len(args), out_spec...]
    all_to_all x7, starting transfers between devices: 43.6 us -> 46.9 us  [trade(): lax.all_to_all(strips.reshape(devices, -1, 128), 'tile', split_axis=0, co...]
where the time goes in v5:
time: 302 us; the launch traced here: 300 us
  Pallas kernels  165 us (55%)
  starting transfers between devices  46.9 us (16%)
  local copies, waits for them, and re-layouts  36.5 us (12%)
  waiting for transfers between devices  34.4 us (11%)
  matrix products  9.35 us (3%)
  other arithmetic  7 us (2%)
    pallas_call x2, Pallas kernels, dec_conv(): pl.pallas_call(kernel, grid=(tiles // g,), in_specs=specs, out_specs=[til...  60.5 us
    pallas_call x2, Pallas kernels, enc_conv(): pl.pallas_call(enc_kernel, grid=(tiles // g,), in_specs=specs, out_specs=...  49.6 us
    all_to_all x7, starting transfers between devices, trade(): lax.all_to_all(strips.reshape(devices, -1, 128), 'tile', split_axis=0, co...  46.9 us
    all_to_all x7, waiting for transfers between devices, trade(): lax.all_to_all(strips.reshape(devices, -1, 128), 'tile', split_axis=0, co...  34.4 us
    pallas_call x6, Pallas kernels, rim_step(): pl.pallas_call(kernel, in_specs=[smem] * 6 + [vmem] * len(args), out_spec...  30.9 us
    unnamed x118, local copies, waits for them, and re-layouts  27.2 us
    pallas_call x1, Pallas kernels, last_step(): pl.pallas_call(last_kernel, in_specs=[smem, vmem, vmem, vmem, anywhere],...  9.16 us
    conv_general_dilated x3, matrix products, inner_sums(): lax.conv_general_dilated(field, weight, (1, 1), ((1, 1), (1, 1)), dimensi...  9 us
  transfers between devices with their start and end apart: 7, of which 6 were waited for; matrix products, arithmetic and copies ran while one was open for 9% of the time, Pallas kernels for 40%

profile of v5, /device:TPU:15, one launch (start us, length us, event | category | flops | bytes accessed | tf_op | source)
XLA Modules:
  0.0 300.3 jit_solution(3147299526837186907)
XLA Ops:
  0.0 0.8 constant_dynamic-slice_fusion.1
  1.2 6.2 %tile_rims.1 = (bf16[24,4,48,128]{3,2,1,0:T(8,128)(2,1)S(1)}, bf16[176,48,128]{2,1,0:T(8,128)(2,1)}) custom-call(s32[96]{0:T(128)S(1)} %compare_select_fusion.4.slot_ref.refs_2_, bf16[24,48,48,128]{3,2,1,0:T(8,128)(2,1)} %refs_0_.1, bf16[24,48,48,128]{3,2,1,0:T(8,128)(2,1)} %refs_0_.1, bf16[24,48,48,128]{3,2,1,0:T(8,128)(2,1)} %refs_0_.1, ...), custom_call_target="tpu_custom_call" | custom-call | tf_op jit(solution)/shard_map/tile_rims/pallas_call | solution.py:161
  7.4 1.0 copy-done.10
  8.5 6.7 %all-to-all-start = ((bf16[16,528,128]{2,1,0:T(8,128)(2,1)}), bf16[16,528,128]{2,1,0:T(8,128)(2,1)S(1)}, u32[]{:S(2)}, u32[]{:S(2)}) async-start(bf16[16,528,128]{2,1,0:T(8,128)(2,1)} %bitcast.11), calls=%async_computation | async-start | bytes 4325376 | tf_op jit(solution)/shard_map/all_to_all | solution.py:938
  17.7 1.3 compare_select_fusion.2
  19.0 1.3 fusion.46
  20.3 34.6 %enc_conv.2 = (bf16[24,24,2,48,128]{4,3,2,1,0:T(8,128)(2,1)}, f32[24,4,48,128]{3,2,1,0:T(8,128)S(1)}, bf16[24,4,48,128]{3,2,1,0:T(8,128)(2,1)S(1)}, bf16[24,24,24,128]{3,2,1,0:T(8,128)(2,1)}) custom-call(bf16[24,48,48,128]{3,2,1,0:T(8,128)(2,1)} %refs_0_.1, bf16[9,128,128]{2,1,0:T(8,128)(2,1)S(1)} %bitcast.185), custom_call_target="tpu_custom_call" | custom-call | flops 21743271936 | bytes 33177600 | tf_op jit(solution)/shard_map/enc_conv/pallas_call | solution.py:818
  54.9 1.4 copy-done.4
  56.3 1.0 copy-done.12
  57.3 6.7 %all-to-all-done = bf16[16,528,128]{2,1,0:T(8,128)(2,1)S(1)} async-done(((bf16[16,528,128]{2,1,0:T(8,128)(2,1)}), bf16[16,528,128]{2,1,0:T(8,128)(2,1)S(1)}, u32[]{:S(2)}, u32[]{:S(2)}) %all-to-all-start) | async-done | bytes 2162720 | tf_op jit(solution)/shard_map/all_to_all | solution.py:938
  64.0 1.4 copy-done.40
  65.3 7.7 %rim_step.6 = (bf16[96,48,128]{2,1,0:T(8,128)(2,1)S(1)}, bf16[96,24,128]{2,1,0:T(8,128)(2,1)S(1)}, bf16[176,24,128]{2,1,0:T(8,128)(2,1)}) custom-call(s32[96]{0:T(128)S(1)} %get-tuple-element.130.refs_0_.pick_ref, s32[97]{0:T(128)S(1)} %get-tuple-element.137.refs_1_.refs_0_, s32[96]{0:T(128)S(1)} %compare_select_fusion.4.slot_ref.refs_2_, ...), custom_call_target="tpu_custom_call" | custom-call | flops 1811939328 | bytes 6912000 | tf_op jit(solution)/shard_map/rim_step/pallas_call | solution.py:477
  73.1 1.1 copy-done.7
  74.2 5.8 %all-to-all-start.1 = ((bf16[16,264,128]{2,1,0:T(8,128)(2,1)}), bf16[16,264,128]{2,1,0:T(8,128)(2,1)S(1)}, u32[]{:S(2)}, u32[]{:S(2)}) async-start(bf16[16,264,128]{2,1,0:T(8,128)(2,1)} %bitcast.17), calls=%async_computation.1 | async-start | bytes 2162688 | tf_op jit(solution)/shard_map/all_to_all | solution.py:938
  80.0 15.0 %enc_conv.3 = (bf16[24,12,2,24,128]{4,3,2,1,0:T(8,128)(2,1)}, f32[24,4,24,128]{3,2,1,0:T(8,128)S(1)}, bf16[24,4,24,128]{3,2,1,0:T(8,128)(2,1)S(1)}, bf16[24,12,12,128]{3,2,1,0:T(8,128)(2,1)S(1)}) custom-call(bf16[24,24,24,128]{3,2,1,0:T(8,128)(2,1)} %get-tuple-element.49.refs_0_, bf16[9,128,128]{2,1,0:T(8,128)(2,1)S(1)} %bitcast.189, ...), custom_call_target="tpu_custom_call" | custom-call | flops 5435817984 | bytes 8294400 | tf_op jit(solution)/shard_map/enc_conv/pallas_call | solution.py:818
  95.0 1.0 copy-done.13
  96.0 1.4 slice.167
  97.4 8.2 %all-to-all-done.1 = bf16[16,264,128]{2,1,0:T(8,128)(2,1)S(1)} async-done(((bf16[16,264,128]{2,1,0:T(8,128)(2,1)}), bf16[16,264,128]{2,1,0:T(8,128)(2,1)S(1)}, u32[]{:S(2)}, u32[]{:S(2)}) %all-to-all-start.1) | async-done | bytes 1081376 | tf_op jit(solution)/shard_map/all_to_all | solution.py:938
  105.6 1.0 copy-done.41
  106.6 5.0 %rim_step.7 = (bf16[96,24,128]{2,1,0:T(8,128)(2,1)S(1)}, bf16[96,16,128]{2,1,0:T(8,128)(2,1)S(1)}, bf16[96,24,128]{2,1,0:T(8,128)(2,1)}) custom-call(s32[96]{0:T(128)S(1)} %get-tuple-element.130.refs_0_.pick_ref, s32[97]{0:T(128)S(1)} %get-tuple-element.137.refs_1_.refs_0_, s32[96]{0:T(128)S(1)} %get-tuple-element.79.refs_2_, ...), custom_call_target="tpu_custom_call" | custom-call | flops 905969664 | bytes 3456000 | tf_op jit(solution)/shard_map/rim_step/pallas_call | solution.py:477
  111.6 0.8 copy-done.17
  112.5 5.7 %all-to-all-start.2 = ((bf16[16,144,128]{2,1,0:T(8,128)(2,1)}), bf16[16,144,128]{2,1,0:T(8,128)(2,1)S(1)}, u32[]{:S(2)}, u32[]{:S(2)}) async-start(bf16[16,144,128]{2,1,0:T(8,128)(2,1)} %bitcast.23), calls=%async_computation.2 | async-start | bytes 1179648 | tf_op jit(solution)/shard_map/all_to_all | solution.py:938
  118.4 0.7 pad_maximum_fusion
  119.1 2.6 multiply_convert_fusion
  121.8 0.9 slice.232
  124.0 9.2 %all-to-all-done.2 = bf16[16,144,128]{2,1,0:T(8,128)(2,1)S(1)} async-done(((bf16[16,144,128]{2,1,0:T(8,128)(2,1)}), bf16[16,144,128]{2,1,0:T(8,128)(2,1)S(1)}, u32[]{:S(2)}, u32[]{:S(2)}) %all-to-all-start.2) | async-done | bytes 589856 | tf_op jit(solution)/shard_map/all_to_all | solution.py:938
  133.2 1.0 copy-done.27
  134.2 2.7 rim_step.8
  136.9 0.7 copy-done.24
  137.7 0.7 copy-done.14
  139.0 5.6 %all-to-all-start.3 = ((bf16[16,88,128]{2,1,0:T(8,128)(2,1)}), bf16[16,88,128]{2,1,0:T(8,128)(2,1)S(1)}, u32[]{:S(2)}, u32[]{:S(2)}) async-start(bf16[16,88,128]{2,1,0:T(8,128)(2,1)} %bitcast.184), calls=%async_computation.3 | async-start | bytes 720896 | tf_op jit(solution)/shard_map/all_to_all | solution.py:938
  144.7 4.6 %skip_step.3.refs_9_ = f32[96,48,128]{2,1,0:T(8,128)} custom-call(s32[97]{0:T(128)S(1)} %get-tuple-element.137.refs_1_.refs_0_, s32[97]{0:T(128)S(1)} %get-tuple-element.136.refs_3_.refs_1_, s32[100]{0:T(128)S(1)} %get-tuple-element.127.refs_5_.refs_2_, bf16[96,48,128]{2,1,0:T(8,128)(2,1)S(1)} %copy-done.8, bf16[9,256,128]{2,1,0:T(8,128)(2,1)S(1)} %bitcast.153), custom_call_target="tpu_custom_call" | custom-call | flops 905969664 | bytes 3538944 | tf_op jit(solution)/shard_map/skip_step/pallas_call | solution.py:313
  149.3 0.7 fusion.19
  152.9 2.0 skip_step.4.refs_10_
  155.0 1.0 copy-done.29
  155.9 3.6 %rim_step.9 = (bf16[96,8,128]{2,1,0:T(8,128)(2,1)S(1)}, bf16[96,16,128]{2,1,0:T(8,128)(2,1)S(1)}, bf16[96,24,128]{2,1,0:T(8,128)(2,1)S(1)}) custom-call(s32[96]{0:T(128)S(1)} %get-tuple-element.130.refs_0_.pick_ref, s32[97]{0:T(128)S(1)} %get-tuple-element.137.refs_1_.refs_0_, s32[96]{0:T(128)S(1)} %get-tuple-element.79.refs_2_, ...), custom_call_target="tpu_custom_call" | custom-call | flops 301989888 | bytes 1152000 | tf_op jit(solution)/shard_map/rim_step/pallas_call | solution.py:477
  159.6 0.8 copy-done.16
  160.4 0.8 copy-done.20
  161.2 10.3 %all-to-all-start.4 = ((bf16[16,144,128]{2,1,0:T(8,128)(2,1)}), bf16[16,144,128]{2,1,0:T(8,128)(2,1)S(1)}, u32[]{:S(2)}, u32[]{:S(2)}) async-start(bf16[16,144,128]{2,1,0:T(8,128)(2,1)} %bitcast.178), calls=%async_computation.4 | async-start | bytes 1179648 | tf_op jit(solution)/shard_map/all_to_all | solution.py:938
  171.9 0.7 copy-done.43
  172.6 5.7 %fusion.4 = f32[24,12,12,128]{3,0,2,1:T(8,128)} fusion(bf16[3,3,256,128]{3,2,1,0:T(8,128)(2,1)S(1)} %copy-done.2, bf16[24,1,12,128]{3,0,2,1:T(8,128)(2,1)S(1)} %copy-done.47, bf16[24,10,1,128]{3,0,2,1:T(8,128)(2,1)S(1)} %bitcast.206, bf16[24,10,10,128]{3,0,2,1:T(8,128)(2,1)S(1)} %copy-done.43, bf16[24,10,1,128]{3,0,2,1:T(8,128)(2,1)S(1)} %bitcast.205, ...), kind=kOutput, calls=%fused_computation.6 | convolution fusion | flops 1828847616 | bytes 4128768 | tf_op jit(solution)/shard_map/conv_general_dilated | solution.py:909
  178.3 1.0 slice_bitcast_fusion.1
  179.3 1.0 fusion.61
  180.6 0.8 copy-done.3
  181.6 2.2 skip_step.5.refs_9_
  183.8 1.0 copy-done
  184.8 1.8 all-to-all-done.4
  187.8 5.0 %rim_step.10 = (bf16[96,16,128]{2,1,0:T(8,128)(2,1)S(1)}, bf16[96,24,128]{2,1,0:T(8,128)(2,1)S(1)}, bf16[176,24,128]{2,1,0:T(8,128)(2,1)}) custom-call(s32[96]{0:T(128)S(1)} %copy-done.37, s32[97]{0:T(128)S(1)} %get-tuple-element.137.refs_1_.refs_0_, s32[96]{0:T(128)S(1)} %copy-done.32, s32[97]{0:T(128)S(1)} %get-tuple-element.136.refs_3_.refs_1_, ...), custom_call_target="tpu_custom_call" | custom-call | flops 603979776 | bytes 2304000 | tf_op jit(solution)/shard_map/rim_step/pallas_call | solution.py:477
  192.8 0.7 copy-done.22
  193.5 6.5 %all-to-all-start.5 = ((bf16[16,264,128]{2,1,0:T(8,128)(2,1)}), bf16[16,264,128]{2,1,0:T(8,128)(2,1)S(1)}, u32[]{:S(2)}, u32[]{:S(2)}) async-start(bf16[16,264,128]{2,1,0:T(8,128)(2,1)} %bitcast.201), calls=%async_computation.5 | async-start | bytes 2162688 | tf_op jit(solution)/shard_map/all_to_all | solution.py:938
  200.0 1.4 slice.241
  202.3 0.7 pad_maximum_fusion.1.refs_2_
  203.1 17.9 %dec_conv.2 = (bf16[24,12,2,24,128]{4,3,2,1,0:T(8,128)(2,1)}, f32[24,4,24,128]{3,2,1,0:T(8,128)S(1)}) custom-call(bf16[24,24,24,128]{3,2,1,0:T(8,128)(2,1)} %bitcast.210, bf16[24,4,24,128]{3,2,1,0:T(8,128)(2,1)S(1)} %bitcast.179, bf16[24,12,12,128]{3,2,1,0:T(8,128)(2,1)S(1)} %pad_maximum_fusion.1.refs_2_, bf16[9,256,128]{2,1,0:T(8,128)(2,1)S(1)} %bitcast.161), custom_call_target="tpu_custom_call" | custom-call | flops 8139571200 | bytes 8294400 | tf_op jit(solution)/shard_map/dec_conv/pallas_call | solution.py:865
  221.0 1.0 copy-done.11
  222.0 3.6 %all-to-all-done.5 = bf16[16,264,128]{2,1,0:T(8,128)(2,1)S(1)} async-done(((bf16[16,264,128]{2,1,0:T(8,128)(2,1)}), bf16[16,264,128]{2,1,0:T(8,128)(2,1)S(1)}, u32[]{:S(2)}, u32[]{:S(2)}) %all-to-all-start.5) | async-done | bytes 1081376 | tf_op jit(solution)/shard_map/all_to_all | solution.py:938
  225.6 7.0 %rim_step.11 = (bf16[96,24,128]{2,1,0:T(8,128)(2,1)S(1)}, bf16[96,48,128]{2,1,0:T(8,128)(2,1)S(1)}, bf16[176,48,128]{2,1,0:T(8,128)(2,1)}) custom-call(s32[96]{0:T(128)S(1)} %copy-done.35, s32[97]{0:T(128)S(1)} %get-tuple-element.137.refs_1_.refs_0_, s32[96]{0:T(128)S(1)} %copy-done.33, s32[97]{0:T(128)S(1)} %get-tuple-element.136.refs_3_.refs_1_, ...), custom_call_target="tpu_custom_call" | custom-call | flops 905969664 | bytes 3456000 | tf_op jit(solution)/shard_map/rim_step/pallas_call | solution.py:477
  232.6 1.1 copy-done.5
  233.7 0.8 copy-done.38
  234.5 6.4 %all-to-all-start.6 = ((bf16[16,528,128]{2,1,0:T(8,128)(2,1)}), bf16[16,528,128]{2,1,0:T(8,128)(2,1)S(1)}, u32[]{:S(2)}, u32[]{:S(2)}) async-start(bf16[16,528,128]{2,1,0:T(8,128)(2,1)} %bitcast.199), calls=%async_computation.6 | async-start | bytes 4325376 | tf_op jit(solution)/shard_map/all_to_all | solution.py:938
  240.9 1.3 copy-done.9
  242.2 42.6 %dec_conv.3 = (bf16[24,24,2,48,128]{4,3,2,1,0:T(8,128)(2,1)}, f32[24,4,48,128]{3,2,1,0:T(8,128)}) custom-call(bf16[24,48,48,128]{3,2,1,0:T(8,128)(2,1)} %bitcast.209, bf16[24,4,48,128]{3,2,1,0:T(8,128)(2,1)S(1)} %bitcast.171, bf16[24,24,24,128]{3,2,1,0:T(8,128)(2,1)} %bitcast.211, bf16[24,4,24,128]{3,2,1,0:T(8,128)(2,1)S(1)} %bitcast.193, ...), custom_call_target="tpu_custom_call" | custom-call | flops 32558284800 | bytes 33177600 | tf_op jit(solution)/shard_map/dec_conv/pallas_call | solution.py:865
  284.7 5.0 %all-to-all-done.6 = bf16[16,528,128]{2,1,0:T(8,128)(2,1)S(1)} async-done(((bf16[16,528,128]{2,1,0:T(8,128)(2,1)}), bf16[16,528,128]{2,1,0:T(8,128)(2,1)S(1)}, u32[]{:S(2)}, u32[]{:S(2)}) %all-to-all-start.6) | async-done | bytes 2162720 | tf_op jit(solution)/shard_map/all_to_all | solution.py:938
  289.7 1.3 copy-done.6
  291.0 9.2 %last_step.1 = bf16[24,48,48,128]{3,2,1,0:T(8,128)(2,1)} custom-call(s32[96]{0:T(128)S(1)} %copy-done.35, bf16[176,48,128]{2,1,0:T(8,128)(2,1)S(1)} %bitcast.149, bf16[96,48,128]{2,1,0:T(8,128)(2,1)S(1)} %copy-done.6, f32[96,48,128]{2,1,0:T(8,128)} %bitcast.198, bf16[24,48,48,128]{3,2,1,0:T(8,128)(2,1)} %bitcast.194), custom_call_target="tpu_custom_call", output_to_operand_aliasing={{}: (4, {})} | custom-call | tf_op jit(solution)/shard_map/last_step/pallas_call | solution.py:777
  (159 shorter events, 10.9 us)
Async XLA Ops:
  1.2 132.0 %copy-start.31 = (s32[96]{0:T(128)}, s32[96]{0:T(128)S(1)}, u32[]{:S(2)}) copy-start(s32[96]{0:T(128)S(1)} %compare_select_fusion.4.slot_ref.refs_2_) | copy-start | bytes 1156
  7.4 1.0 copy-start.10
  8.5 6.7 %copy-start.50 = (s32[384,4,2]{0,2,1:T(2,128)S(1)}, s32[384,4,2]{0,2,1:T(2,128)}, u32[]{:S(2)}) copy-start(s32[384,4,2]{0,2,1:T(2,128)} %param.10) | copy-start | bytes 36868
  8.5 11.8 %copy-start.25 = (bf16[3,3,128,128]{3,2,1,0:T(8,128)(2,1)S(1)}, bf16[3,3,128,128]{3,2,1,0:T(8,128)(2,1)}, u32[]{:S(2)}) copy-start(bf16[3,3,128,128]{3,2,1,0:T(8,128)(2,1)} %param.11) | copy-start | bytes 884740
  8.5 55.5 %all-to-all-start = ((bf16[16,528,128]{2,1,0:T(8,128)(2,1)}), bf16[16,528,128]{2,1,0:T(8,128)(2,1)S(1)}, u32[]{:S(2)}, u32[]{:S(2)}) async-start(bf16[16,528,128]{2,1,0:T(8,128)(2,1)} %bitcast.11), calls=%async_computation | async-start | bytes 4325376 | tf_op jit(solution)/shard_map/all_to_all | solution.py:938
  16.5 116.7 %copy-start.36 = (s32[96]{0:T(128)}, s32[96]{0:T(128)S(1)}, u32[]{:S(2)}) copy-start(s32[96]{0:T(128)S(1)} %get-tuple-element.82.refs_0_) | copy-start | bytes 1156
  17.1 137.8 %copy-start.34 = (s32[96]{0:T(128)}, s32[96]{0:T(128)S(1)}, u32[]{:S(2)}) copy-start(s32[96]{0:T(128)S(1)} %get-tuple-element.130.refs_0_.pick_ref) | copy-start | bytes 1156
  54.9 1.4 copy-start.4
  56.3 1.0 copy-start.12
  64.0 1.4 copy-start.40
  73.1 1.1 copy-start.7
  74.2 5.8 %copy-start.30 = (bf16[3,3,128,128]{3,2,1,0:T(8,128)(2,1)S(1)}, bf16[3,3,128,128]{3,2,1,0:T(8,128)(2,1)}, u32[]{:S(2)}) copy-start(bf16[3,3,128,128]{3,2,1,0:T(8,128)(2,1)} %param.12) | copy-start | bytes 884740
  74.2 31.4 %all-to-all-start.1 = ((bf16[16,264,128]{2,1,0:T(8,128)(2,1)}), bf16[16,264,128]{2,1,0:T(8,128)(2,1)S(1)}, u32[]{:S(2)}, u32[]{:S(2)}) async-start(bf16[16,264,128]{2,1,0:T(8,128)(2,1)} %bitcast.17), calls=%async_computation.1 | async-start | bytes 2162688 | tf_op jit(solution)/shard_map/all_to_all | solution.py:938
  95.0 1.0 copy-start.13
  105.6 1.0 copy-start.41
  111.6 0.8 copy-start.17
  112.4 6.0 %copy-start.42 = (bf16[24,10,10,128]{3,2,1,0:T(8,128)(2,1)S(1)}, bf16[24,10,10,128]{3,2,1,0:T(8,128)(2,1)}, u32[]{:S(2)}) copy-start(bf16[24,10,10,128]{3,2,1,0:T(8,128)(2,1)} %slice.167) | copy-start | bytes 1843204
  112.5 20.7 %all-to-all-start.2 = ((bf16[16,144,128]{2,1,0:T(8,128)(2,1)}), bf16[16,144,128]{2,1,0:T(8,128)(2,1)S(1)}, u32[]{:S(2)}, u32[]{:S(2)}) async-start(bf16[16,144,128]{2,1,0:T(8,128)(2,1)} %bitcast.23), calls=%async_computation.2 | async-start | bytes 1179648 | tf_op jit(solution)/shard_map/all_to_all | solution.py:938
  118.2 1.0 copy-start.26
  133.2 1.0 copy-start.27
  134.2 10.5 %copy-start.1 = (bf16[3,3,256,128]{3,2,1,0:T(8,128)(2,1)S(1)}, bf16[3,3,256,128]{3,2,1,0:T(8,128)(2,1)}, u32[]{:S(2)}) copy-start(bf16[3,3,256,128]{3,2,1,0:T(8,128)(2,1)} %param.17) | copy-start | bytes 1769476
  136.8 0.7 copy-start.24
  137.6 7.1 %copy-start.8 = (bf16[96,48,128]{2,1,0:T(8,128)(2,1)S(1)}, bf16[96,48,128]{2,1,0:T(8,128)(2,1)}, u32[]{:S(2)}) copy-start(bf16[96,48,128]{2,1,0:T(8,128)(2,1)} %copy-done.7) | copy-start | bytes 3538948
  137.6 0.7 copy-start.14
  139.0 15.9 %all-to-all-start.3 = ((bf16[16,88,128]{2,1,0:T(8,128)(2,1)}), bf16[16,88,128]{2,1,0:T(8,128)(2,1)S(1)}, u32[]{:S(2)}, u32[]{:S(2)}) async-start(bf16[16,88,128]{2,1,0:T(8,128)(2,1)} %bitcast.184), calls=%async_computation.3 | async-start | bytes 720896 | tf_op jit(solution)/shard_map/all_to_all | solution.py:938
  144.7 4.6 %copy-start.28 = (bf16[3,3,128,128]{3,2,1,0:T(8,128)(2,1)S(1)}, bf16[3,3,128,128]{3,2,1,0:T(8,128)(2,1)}, u32[]{:S(2)}) copy-start(bf16[3,3,128,128]{3,2,1,0:T(8,128)(2,1)} %param.14) | copy-start | bytes 884740
  144.7 4.6 %copy-start.45 = (bf16[24,4,4,128]{3,0,2,1:T(8,128)(2,1)S(1)}, bf16[24,4,4,128]{3,0,2,1:T(8,128)(2,1)}, u32[]{:S(2)}) copy-start(bf16[24,4,4,128]{3,0,2,1:T(8,128)(2,1)} %fusion.29) | copy-start | bytes 294916
  144.7 5.4 %copy-start.44 = (bf16[24,1,12,128]{3,2,1,0:T(8,128)(2,1)S(1)}, bf16[24,1,12,128]{3,2,1,0:T(8,128)(2,1)}, u32[]{:S(2)}) copy-start(bf16[24,1,12,128]{3,2,1,0:T(8,128)(2,1)} %get-tuple-element.109) | copy-start | bytes 221188
  150.1 2.8 copy-start.2
  152.7 2.2 copy-start.15
  155.0 1.0 copy-start.29
  159.5 0.8 copy-start.16
  160.4 0.8 copy-start.20
  161.2 10.7 %copy-start.46 = (bf16[24,1,12,128]{3,0,2,1:T(8,128)(2,1)S(1)}, bf16[24,1,12,128]{3,0,2,1:T(8,128)(2,1)}, u32[]{:S(2)}) copy-start(bf16[24,1,12,128]{3,0,2,1:T(8,128)(2,1)} %copy.155) | copy-start | bytes 221188
  161.2 10.7 %copy-start.47 = (bf16[24,1,12,128]{3,0,2,1:T(8,128)(2,1)S(1)}, bf16[24,1,12,128]{3,0,2,1:T(8,128)(2,1)}, u32[]{:S(2)}) copy-start(bf16[24,1,12,128]{3,0,2,1:T(8,128)(2,1)} %copy.158) | copy-start | bytes 221188
  161.2 10.7 %copy-start.48 = (bf16[24,1,10,128]{3,0,2,1:T(8,128)(2,1)S(1)}, bf16[24,1,10,128]{3,0,2,1:T(8,128)(2,1)}, u32[]{:S(2)}) copy-start(bf16[24,1,10,128]{3,0,2,1:T(8,128)(2,1)} %copy.190) | copy-start | bytes 184324
  161.2 25.3 %all-to-all-start.4 = ((bf16[16,144,128]{2,1,0:T(8,128)(2,1)}), bf16[16,144,128]{2,1,0:T(8,128)(2,1)S(1)}, u32[]{:S(2)}, u32[]{:S(2)}) async-start(bf16[16,144,128]{2,1,0:T(8,128)(2,1)} %bitcast.178), calls=%async_computation.4 | async-start | bytes 1179648 | tf_op jit(solution)/shard_map/all_to_all | solution.py:938
  171.5 1.1 copy-start.43
  171.5 1.1 copy-start.49
  180.4 1.1 copy-start.3
  180.4 1.2 copy-start.18
  180.5 6.1 %copy-start.21 = (bf16[96,16,128]{2,1,0:T(8,128)(2,1)S(1)}, bf16[96,16,128]{2,1,0:T(8,128)(2,1)}, u32[]{:S(2)}) copy-start(bf16[96,16,128]{2,1,0:T(8,128)(2,1)} %copy-done.20) | copy-start | bytes 1179652
  183.8 1.0 copy-start
  186.6 0.6 copy-start.32
  187.1 0.6 copy-start.37
  192.8 0.7 copy-start.22
  193.5 32.1 %all-to-all-start.5 = ((bf16[16,264,128]{2,1,0:T(8,128)(2,1)}), bf16[16,264,128]{2,1,0:T(8,128)(2,1)S(1)}, u32[]{:S(2)}, u32[]{:S(2)}) async-start(bf16[16,264,128]{2,1,0:T(8,128)(2,1)} %bitcast.201), calls=%async_computation.5 | async-start | bytes 2162688 | tf_op jit(solution)/shard_map/all_to_all | solution.py:938
  200.0 2.0 copy-start.23
  202.0 1.1 copy-start.19
  203.1 22.5 %copy-start.33 = (s32[96]{0:T(128)S(1)}, s32[96]{0:T(128)}, u32[]{:S(2)}) copy-start(s32[96]{0:T(128)} %copy-done.31) | copy-start | bytes 1156
  203.1 22.5 %copy-start.35 = (s32[96]{0:T(128)S(1)}, s32[96]{0:T(128)}, u32[]{:S(2)}) copy-start(s32[96]{0:T(128)} %copy-done.34) | copy-start | bytes 1156
  221.0 1.0 copy-start.11
  232.6 1.1 copy-start.5
  233.7 0.8 copy-start.38
  234.5 6.4 %copy-start.39 = (bf16[96,24,128]{2,1,0:T(8,128)(2,1)S(1)}, bf16[96,24,128]{2,1,0:T(8,128)(2,1)}, u32[]{:S(2)}) copy-start(bf16[96,24,128]{2,1,0:T(8,128)(2,1)} %copy-done.38) | copy-start | bytes 1769476
  234.5 55.2 %all-to-all-start.6 = ((bf16[16,528,128]{2,1,0:T(8,128)(2,1)}), bf16[16,528,128]{2,1,0:T(8,128)(2,1)S(1)}, u32[]{:S(2)}, u32[]{:S(2)}) async-start(bf16[16,528,128]{2,1,0:T(8,128)(2,1)} %bitcast.199), calls=%async_computation.6 | async-start | bytes 4325376 | tf_op jit(solution)/shard_map/all_to_all | solution.py:938
  240.9 1.3 copy-start.9
  289.7 1.3 copy-start.6
